TPU v7x, 128 devices: a whole 4x4x4 slice. The times are simulated.
128 devices in a mesh: group: 8 (over x, z_hi), fsdp: 16 (over z_lo, y, core).
Axes of the slice: x: 4, y: 4, z: 4 (z_hi: 2, z_lo: 2; z = z_hi * 2 + z_lo), core: 2. Of those that a mesh axis runs over, the one named last changes fastest.
Arguments:
- tokens: bfloat16 [1024, 4608], P('fsdp'), may hold values from -6 to 6
- pre_gain: float32 [4608], replicated, may hold values from 0.1 to 1.9
- post_gain: float32 [4608], replicated, may hold values from 0.1 to 1.9
- qkv_weight: bfloat16 [4608, 16, 4, 128], P(None, 'fsdp')
- out_weight: bfloat16 [16, 2, 128, 4608], P('fsdp'), may hold values from -0.09375 to 0.09375
- doc_ids: int32 [1024], replicated, may hold values from 0 to 3, never falling along the last dimension, each value on 1 to 512 neighbouring positions
- cotangent: bfloat16 [1024, 4608], P('fsdp'), may hold values from -6 to 6
- outer_delta: bfloat16 [8, 2048, 4608], P('group', 'fsdp'), may hold values from -6 to 6
- momentum: float32 [2048, 4608], P('fsdp'), may hold values from -6 to 6
- fragment: float32 [2048, 4608], P('fsdp'), may hold values from -6 to 6
Outputs:
- output: bfloat16 [1024, 4608], P('fsdp')
- grad_qkv: bfloat16 [4608, 16, 4, 128], P(None, 'fsdp')
- grad_out: bfloat16 [16, 2, 128, 4608], P('fsdp')
- new_momentum: float32 [2048, 4608], P('fsdp')
- new_fragment: float32 [2048, 4608], P('fsdp')
Inputs may be any that keep to these rules, and one draw needn't show every extreme that they name: doc_ids never falls along the sequence; each document holds 1 to 512 tokens and one holds exactly 512.
All inputs are finite; a program needn't handle non-finite values.
Results may differ from a plain program's by a relative error of at most 0.015.
The roundings to bfloat16 on the way count: a program that leaves them out, or rounds other values in their place, can miss the bound.
Values may be sent and summed in bfloat16 or wider, within the bound.
A program may use at most 192 MiB of HBM per device.

v0:
```python
import jax
import jax.numpy as jnp
from jax import lax
from jax.sharding import PartitionSpec as P

softcap = 50.0
query_scale = 1.0 / 12.0


def rms_norm(values, gain):
    scale = lax.rsqrt(jnp.mean(values * values, axis=-1, keepdims=True) + 1e-06)
    return values * scale * gain


def rms_backward(values, gain, grads):
    scale = lax.rsqrt(jnp.mean(values * values, axis=-1, keepdims=True) + 1e-06)
    normal = values * scale
    dnorm = grads * gain
    return scale * (dnorm - normal * jnp.mean(dnorm * normal, axis=-1, keepdims=True))


def tables(length, width):
    half = width // 2
    positions = jnp.arange(length, dtype=jnp.float32)[:, None]
    freqs = jnp.power(jnp.float32(10000.0), -(2.0 * jnp.arange(half, dtype=jnp.float32) / width))
    angle = positions * freqs[None, :]
    return (jnp.cos(angle), jnp.sin(angle))


def rotate(values, cosine, sine):
    half = values.shape[-1] // 2
    first, second = (values[..., :half], values[..., half:])
    return jnp.concatenate(
        [first * cosine - second * sine, second * cosine + first * sine], axis=-1
    )


def unrotate(grads, cosine, sine):
    half = grads.shape[-1] // 2
    first, second = (grads[..., :half], grads[..., half:])
    return jnp.concatenate(
        [first * cosine + second * sine, second * cosine - first * sine], axis=-1
    )


def attend(query, keyed, valued, allowed):
    scores = jnp.dot(query, keyed.T, preferred_element_type=jnp.float32) * query_scale
    capped = softcap * jnp.tanh(scores / softcap)
    weights = jnp.where(allowed, jnp.exp(capped), jnp.float32(0.0))
    probs = weights / jnp.sum(weights, axis=-1, keepdims=True)
    rounded = probs.astype(jnp.bfloat16)
    result = jnp.dot(rounded, valued, preferred_element_type=jnp.float32)
    return (result, probs, rounded, capped)


def attend_back(query, keyed, valued, probs, rounded, capped, grad_head):
    dprob = jnp.dot(grad_head, valued.T, preferred_element_type=jnp.float32)
    dvalue = jnp.dot(rounded.T, grad_head, preferred_element_type=jnp.float32)
    dcap = probs * (dprob - jnp.sum(dprob * probs, axis=-1, keepdims=True))
    dscore = (dcap * (1.0 - (capped / softcap) ** 2) * query_scale).astype(jnp.bfloat16)
    dquery = jnp.dot(dscore, keyed, preferred_element_type=jnp.float32)
    dkey = jnp.dot(dscore.T, query, preferred_element_type=jnp.float32)
    return (dquery, dkey, dvalue)


def nesterov(mean_delta, moment_part, params_part):
    moment_next = 0.9 * moment_part + mean_delta
    return (moment_next, params_part - 0.7 * (mean_delta + 0.9 * moment_next))


def local(
    tokens,
    pre_gain,
    post_gain,
    qkv_weight,
    out_weight,
    doc_ids,
    cotangent,
    outer_delta,
    momentum,
    fragment,
):
    every_cotangent = lax.all_gather(cotangent, "fsdp", axis=0, tiled=True)
    inputs = tokens.astype(jnp.float32)
    normed = rms_norm(inputs, pre_gain).astype(jnp.bfloat16)
    gathered = lax.all_gather(normed, "fsdp", axis=0, tiled=True)
    length, width = gathered.shape
    key_heads, parts, head_dim = (qkv_weight.shape[1], qkv_weight.shape[2], qkv_weight.shape[3])
    query_count = parts - 2
    proj = jnp.dot(
        gathered,
        qkv_weight.reshape(width, key_heads * parts * head_dim),
        preferred_element_type=jnp.float32,
    )
    proj = proj.reshape(length, key_heads, parts, head_dim)
    cosine, sine = tables(length, head_dim)
    cosine_four, sine_four = (cosine[:, None, None, :], sine[:, None, None, :])
    cosine_three, sine_three = (cosine[:, None, :], sine[:, None, :])
    queries = rotate(proj[:, :, :query_count], cosine_four, sine_four).astype(jnp.bfloat16)
    keys = rotate(proj[:, :, query_count], cosine_three, sine_three).astype(jnp.bfloat16)
    values = proj[:, :, query_count + 1].astype(jnp.bfloat16)
    position = jnp.arange(length, dtype=jnp.int32)
    allowed = (position[None, :] <= position[:, None]) & (doc_ids[None, :] == doc_ids[:, None])
    qhead = jnp.transpose(queries, (1, 2, 0, 3))
    khead = jnp.transpose(keys, (1, 0, 2))
    vhead = jnp.transpose(values, (1, 0, 2))

    def forward_group(query_set, keyed, valued):
        return jax.vmap(attend, in_axes=(0, None, None, None))(query_set, keyed, valued, allowed)

    result, probs, rounded, capped = jax.vmap(forward_group)(qhead, khead, vhead)
    heads = jnp.transpose(result.astype(jnp.bfloat16), (2, 0, 1, 3))
    head_flat = heads.reshape(length, key_heads * query_count * head_dim)
    out_flat = out_weight.reshape(key_heads * query_count * head_dim, width)
    attn = lax.psum_scatter(
        jnp.dot(head_flat, out_flat, preferred_element_type=jnp.float32),
        "fsdp",
        scatter_dimension=0,
        tiled=True,
    )
    attn_all = lax.all_gather(attn, "fsdp", axis=0, tiled=True)
    grad_rows = rms_backward(attn_all, post_gain, every_cotangent.astype(jnp.float32)).astype(
        jnp.bfloat16
    )
    output = (inputs + rms_norm(attn, post_gain)).astype(jnp.bfloat16)
    grad_out = lax.dot_general(
        head_flat, grad_rows, (((0,), (0,)), ((), ())), preferred_element_type=jnp.float32
    )
    grad_out = grad_out.astype(jnp.bfloat16).reshape(out_weight.shape)
    grad_heads = lax.dot_general(
        grad_rows, out_flat, (((1,), (1,)), ((), ())), preferred_element_type=jnp.float32
    )
    grad_heads = grad_heads.astype(jnp.bfloat16).reshape(length, key_heads, query_count, head_dim)
    grad_heads = jnp.transpose(grad_heads, (1, 2, 0, 3))

    def backward_group(query_set, keyed, valued, prob_set, round_set, cap_set, grad_set):
        dquery, dkey, dvalue = jax.vmap(attend_back, in_axes=(0, None, None, 0, 0, 0, 0))(
            query_set, keyed, valued, prob_set, round_set, cap_set, grad_set
        )
        return (dquery, jnp.sum(dkey, axis=0), jnp.sum(dvalue, axis=0))

    dquery, dkey, dvalue = jax.vmap(backward_group)(
        qhead, khead, vhead, probs, rounded, capped, grad_heads
    )
    dquery = unrotate(jnp.transpose(dquery, (2, 0, 1, 3)), cosine_four, sine_four)
    dkey = unrotate(jnp.transpose(dkey, (1, 0, 2)), cosine_three, sine_three)
    dvalue = jnp.transpose(dvalue, (1, 0, 2))
    grad_proj = jnp.concatenate([dquery, dkey[:, :, None], dvalue[:, :, None]], axis=2).astype(
        jnp.bfloat16
    )
    grad_qkv = lax.dot_general(
        gathered,
        grad_proj.reshape(length, key_heads * parts * head_dim),
        (((0,), (0,)), ((), ())),
        preferred_element_type=jnp.float32,
    )
    grad_qkv = grad_qkv.astype(jnp.bfloat16).reshape(qkv_weight.shape)
    own_delta = outer_delta[0].astype(jnp.float32)
    total = lax.psum(own_delta.astype(jnp.bfloat16), "group").astype(jnp.float32)
    new_momentum, new_fragment = nesterov(total / lax.axis_size("group"), momentum, fragment)
    return (output, grad_qkv, grad_out, new_momentum, new_fragment)


def solution(mesh):
    placed = (
        P("fsdp", None),
        P(),
        P(),
        P(None, "fsdp", None, None),
        P("fsdp", None, None, None),
        P(),
        P("fsdp", None),
        P("group", "fsdp", None),
        P("fsdp", None),
        P("fsdp", None),
    )
    return jax.shard_map(
        local,
        mesh=mesh,
        in_specs=placed,
        out_specs=(
            P("fsdp", None),
            P(None, "fsdp", None, None),
            P("fsdp", None, None, None),
            P("fsdp", None),
            P("fsdp", None),
        ),
        check_vma=False,
    )
```

profile of v0, /device:TPU:1, one launch (start us, length us, event | category | flops | bytes accessed | tf_op | source)
XLA Modules:
  0.0 502.1 jit_solution(87739846189134601)
XLA Ops:
  8.0 0.0 copy-start
  8.0 0.0 all-gather.4.cloned.1.call-start
  8.1 1.4 fusion.39
  9.5 2.1 fusion.41
  11.6 0.0 all-gather.4.cloned.1.call-update
  11.6 0.0 reduce-scatter.2.cloned.1.call-start
  11.7 0.0 copy-start.25
  11.7 5.3 %copy.39 = bf16[576,8,4,128]{3,1,2,0:T(8,128)(2,1)} copy(bf16[576,8,4,128]{3,2,1,0:T(4,128)(2,1)} %bitcast.106) | data formatting | bytes 9437184
  17.0 6.7 %copy.15 = bf16[512,4608]{1,0:T(8,128)(2,1)} copy(bf16[512,4608]{0,1:T(8,128)(2,1)} %bitcast.105) | data formatting | bytes 9437184 | tf_op jit(solution)/shard_map/dot_general | solution.py:90
  23.7 1.0 fusion.58
  24.7 0.0 copy-done.25
  24.7 0.0 copy-start.6
  24.7 0.0 copy-start.8
  24.7 1.6 fusion.8
  26.3 46.2 %all-gather.4.cloned.1.call-done = bf16[1024,4608]{1,0:T(8,128)(2,1)} async-done(((bf16[64,4608]{1,0:T(8,128)(2,1)}), bf16[1024,4608]{1,0:T(8,128)(2,1)}) %all-gather.4.cloned.1.call-update) | async-done | bytes 9437200 | tf_op jit(solution)/shard_map/all_gather | solution.py:86
  72.5 9.1 %fusion.21 = f32[1024,1,4,128]{0,3,2,1:T(8,128)S(1)} fusion(bf16[4,128,4608]{2,1,0:T(8,128)(2,1)} %bitcast.107, bf16[1024,4608]{1,0:T(8,128)(2,1)} %all-gather.4.cloned.1.call-done), kind=kOutput, calls=%fused_computation.33 | convolution fusion | flops 4831838208 | bytes 16252928 | tf_op jit(solution)/shard_map/dot_general | solution.py:90
  81.6 0.0 copy-start.10
  81.7 1.2 subtract_convert_fusion.3
  82.9 0.0 copy-start.21
  82.9 0.0 copy-start.23
  82.9 0.0 copy-done.6
  82.9 0.0 copy-done.8
  82.9 0.2 subtract_convert_fusion.1
  83.1 0.0 copy-start.15
  83.1 0.0 copy-start.17
  83.1 2.6 fusion.5
  85.7 3.3 fusion.27
  89.1 0.0 copy-done.26
  89.1 0.0 copy-start.13
  89.1 0.8 copy-done.13
  89.9 7.9 %convolution_bitcast_fusion = f32[1024,4608]{1,0:T(8,128)} fusion(bf16[1,2,128,4608]{3,2,1,0:T(8,128)(2,1)S(1)} %copy-done, bf16[2,1024,128]{1,2,0:T(8,128)(2,1)S(1)} %fusion.27), kind=kOutput, calls=%fused_computation.5 | convolution fusion | flops 2415919104 | bytes 21757952 | tf_op jit(solution)/shard_map/dot_general | solution.py:116
  97.8 0.0 reduce-scatter.2.cloned.1.call-update
  97.9 0.0 all-reduce.2.cloned.1.call-start
  97.9 0.5 all-reduce.2.cloned.1.call-update
  98.5 0.0 all-gather.6.cloned.1.call-start
  98.5 107.3 %reduce-scatter.2.cloned.1.call-done = f32[64,4608]{1,0:T(8,128)} async-done(((f32[1024,4608]{1,0:T(8,128)}), f32[64,4608]{1,0:T(8,128)}) %reduce-scatter.2.cloned.1.call-update) | async-done | bytes 1179664 | tf_op jit(solution)/shard_map/reduce_scatter | solution.py:115
  205.8 0.0 all-gather.6.cloned.1.call-update
  205.9 0.2 all-gather.8.cloned.1.call-start
  206.1 0.3 all-gather.8.cloned.1.call-update
  206.4 154.4 %all-reduce.2.cloned.1.call-done = bf16[128,4608]{1,0:T(8,128)(2,1)} async-done(((bf16[128,4608]{1,0:T(8,128)(2,1)}), bf16[128,4608]{1,0:T(8,128)(2,1)}) %all-reduce.2.cloned.1.call-update) | async-done | bytes 1179664 | tf_op jit(solution)/shard_map/psum | solution.py:159
  360.8 5.7 %multiply_subtract_fusion = (f32[128,4608]{1,0:T(8,128)}, f32[128,4608]{1,0:T(8,128)}) fusion(f32[128,4608]{1,0:T(8,128)} %param.19, bf16[128,4608]{1,0:T(8,128)(2,1)} %all-reduce.2.cloned.1.call-done, f32[128,4608]{1,0:T(8,128)} %param.18), kind=kLoop, calls=%fused_computation.21 | loop fusion | flops 4718592 | bytes 10616832 | tf_op jit(solution)/shard_map/sub | solution.py:68
  366.6 0.2 multiply_reduce_fusion.3
  366.8 0.0 copy-done.19
  366.8 1.1 fusion.42
  367.9 8.0 %multiply_reduce_fusion.1 = f32[1024]{0:T(1024)S(1)} fusion(f32[1024,4608]{1,0:T(8,128)} %all-gather.6.cloned.1.call-done), kind=kLoop, calls=%fused_computation.4 | loop fusion | flops 9436160 | bytes 18878464 | tf_op jit(solution)/shard_map/reduce_sum | solution.py:16
  375.9 17.4 %all-gather.8.cloned.1.call-done = bf16[1024,4608]{1,0:T(8,128)(2,1)} async-done(((bf16[64,4608]{1,0:T(8,128)(2,1)}), bf16[1024,4608]{1,0:T(8,128)(2,1)}) %all-gather.8.cloned.1.call-update) | async-done | bytes 9437200 | tf_op jit(solution)/shard_map/all_gather | solution.py:83
  393.3 0.0 copy-done.20
  393.3 12.5 %multiply_reduce_fusion = f32[1024]{0:T(1024)S(1)} fusion(bf16[1024,4608]{1,0:T(8,128)(2,1)} %all-gather.8.cloned.1.call-done, f32[1024,4608]{1,0:T(8,128)} %all-gather.6.cloned.1.call-done, f32[4608]{0:T(1024)S(1)} %copy-done.20, f32[1024]{0:T(1024)S(1)} %add_rsqrt_fusion), kind=kLoop, calls=%fused_computation.2 | loop fusion | flops 23591936 | bytes 28338176 | tf_op jit(solution)/shard_map/reduce_sum | solution.py:19
  405.7 2.0 copy-done.2
  407.8 2.7 copy-done.3
  410.5 7.5 %multiply_convert_fusion = bf16[1024,4608]{1,0:T(8,128)(2,1)} fusion(bf16[1024,4608]{1,0:T(8,128)(2,1)S(1)} %copy-done.3, f32[1024,4608]{1,0:T(8,128)S(1)} %copy-done.2, f32[1024]{0:T(1024)S(1)} %broadcast_multiply_fusion, f32[4608]{0:T(1024)S(1)} %copy-done.20, f32[1024]{0:T(1024)S(1)} %add_rsqrt_fusion), kind=kLoop, calls=%fused_computation.1 | loop fusion | flops 33030144 | bytes 37775360 | tf_op jit(solution)/shard_map/convert_element_type | solution.py:122
  417.9 6.4 %convolution_convert_fusion.2 = bf16[1024,256]{0,1:T(8,128)(2,1)S(1)} fusion(bf16[1024,4608]{1,0:T(8,128)(2,1)} %multiply_convert_fusion, bf16[256,4608]{1,0:T(8,128)(2,1)S(1)} %bitcast.104), kind=kOutput, calls=%fused_computation.36 | convolution fusion | flops 2416181248 | bytes 12320768 | tf_op jit(solution)/shard_map/dot_general | solution.py:130
  424.4 6.2 %fusion.43 = bf16[1024,1,1,128]{0,3,2,1:T(8,128)(2,1)} fusion(bf16[2,1024,128]{1,2,0:T(8,128)(2,1)S(1)} %bitcast.109, f32[2,1024,1024]{1,2,0:T(8,128)} %copy-done.26, f32[2,1024]{1,0:T(2,128)S(1)} %get-tuple-element.22, pred[1024,1024]{0,1:T(8,128)(4,1)S(1)} %copy-done.12), kind=kOutput, calls=%fused_computation.45 | convolution fusion | flops 547487744 | bytes 10231808 | tf_op jit(solution)/shard_map/vmap(vmap())/dot_general | solution.py:58
  430.6 5.7 %fusion.52 = f32[2,1024,1024]{1,2,0:T(8,128)} fusion(bf16[2,1024,128]{1,2,0:T(8,128)(2,1)S(1)} %bitcast.110, f32[1024,1,4,128]{0,3,2,1:T(8,128)} %copy-done.10), kind=kOutput, calls=%fused_computation.63 | convolution fusion | flops 536870912 | bytes 9175040 | tf_op jit(solution)/shard_map/vmap(vmap())/dot_general | solution.py:57
  436.3 0.0 copy-done.16
  436.3 14.1 %fusion.33 = f32[1024,1,128]{0,2,1:T(8,128)S(1)} fusion(f32[2,1024,1024]{1,2,0:T(8,128)} %fusion.52, f32[2,1024,1024]{1,2,0:T(8,128)} %copy-done.26, bf16[1024,1,2,64]{0,3,2,1:T(8,128)(2,1)S(1)} %copy-done.18, bf16[1024,1,2,64]{0,3,2,1:T(8,128)(2,1)S(1)} %copy-done.16, f32[2,1024]{1,0:T(2,128)S(1)} %get-tuple-element.22, pred[1024,1024]{0,1:T(8,128)(4,1)S(1)} %copy-done.12), kind=kOutput, calls=%fused_computation.38 | convolution fusion | flops 571476992 | bytes 18882560 | tf_op jit(solution)/shard_map/vmap(vmap())/dot_general | solution.py:62
  450.4 1.2 add_convert_fusion.2
  451.6 15.6 %fusion.24 = f32[1024,1,2,128]{0,3,2,1:T(8,128)S(1)} fusion(f32[2,1024,1024]{1,2,0:T(8,128)} %fusion.52, f32[2,1024,1024]{1,2,0:T(8,128)} %copy-done.26, bf16[1024,64]{0,1:T(8,128)(2,1)S(1)} %bitcast.115, bf16[1024,64]{0,1:T(8,128)(2,1)S(1)} %bitcast.114, f32[2,1024]{1,0:T(2,128)S(1)} %get-tuple-element.22, pred[1024,1024]{0,1:T(8,128)(4,1)S(1)} %copy-done.12), kind=kOutput, calls=%fused_computation.34 | convolution fusion | flops 570952704 | bytes 19144704 | tf_op jit(solution)/shard_map/vmap(vmap())/dot_general | solution.py:61
  467.2 0.2 add_convert_fusion
  467.4 1.0 pad_maximum_fusion
  468.5 10.4 %convolution_convert_fusion = bf16[4608,512]{0,1:T(8,128)(2,1)} fusion(bf16[1024,512]{0,1:T(8,128)(2,1)S(1)} %bitcast.112, bf16[1024,4608]{1,0:T(8,128)(2,1)} %all-gather.4.cloned.1.call-done), kind=kOutput, calls=%fused_computation.13 | convolution fusion | flops 4834197504 | bytes 15204352 | tf_op jit(solution)/shard_map/dot_general | solution.py:151
  478.9 8.4 %copy.25 = bf16[4608,1,4,128]{3,2,1,0:T(4,128)(2,1)} copy(bf16[4608,1,4,128]{0,3,2,1:T(8,128)(2,1)} %bitcast.108) | data formatting | bytes 9437184
  487.3 0.0 copy-done.14
  487.3 7.7 %convolution_convert_fusion.1 = bf16[256,4608]{1,0:T(8,128)(2,1)} fusion(bf16[1024,256]{0,1:T(8,128)(2,1)S(1)} %bitcast.113, bf16[1024,4608]{1,0:T(8,128)(2,1)} %multiply_convert_fusion), kind=kOutput, calls=%fused_computation.14 | convolution fusion | flops 2417098752 | bytes 12320768 | tf_op jit(solution)/shard_map/dot_general | solution.py:126
  (41 shorter events, 0.2 us)
Async XLA Ops:
  8.0 81.9 %copy-start = (bf16[1,2,128,4608]{3,2,1,0:T(8,128)(2,1)S(1)}, bf16[1,2,128,4608]{3,2,1,0:T(8,128)(2,1)}, u32[]{:S(2)}) copy-start(bf16[1,2,128,4608]{3,2,1,0:T(8,128)(2,1)} %param.14) | copy-start | bytes 7077892
  8.0 64.5 %all-gather.4.cloned.1.call-start = ((), (), s32[]{:S(2)}) async-start(), calls=%async_computation.1 | async-start | bytes 10027008 | tf_op jit(solution)/shard_map/all_gather | solution.py:86
  11.6 194.2 %reduce-scatter.2.cloned.1.call-start = ((), (), s32[]{:S(2)}) async-start(), calls=%async_computation.2 | async-start | bytes 20054016 | tf_op jit(solution)/shard_map/reduce_scatter | solution.py:115
  11.7 13.0 %copy-start.25 = (s32[1024]{0:T(1024)S(1)}, s32[1024]{0:T(1024)}, u32[]{:S(2)}) copy-start(s32[1024]{0:T(1024)} %param.15) | copy-start | bytes 12292
  24.7 58.2 %copy-start.6 = (f32[1024,64]{0,1:T(8,128)}, f32[1024,64]{0,1:T(8,128)S(1)}, u32[]{:S(2)}) copy-start(f32[1024,64]{0,1:T(8,128)S(1)} %get-tuple-element.20) | copy-start | bytes 786436
  24.7 58.2 %copy-start.8 = (f32[1024,64]{0,1:T(8,128)}, f32[1024,64]{0,1:T(8,128)S(1)}, u32[]{:S(2)}) copy-start(f32[1024,64]{0,1:T(8,128)S(1)} %get-tuple-element.21) | copy-start | bytes 786436
  72.5 10.6 %copy-start.11 = (pred[1024,1024]{0,1:T(8,128)(4,1)S(1)}, pred[1024,1024]{0,1:T(8,128)(4,1)}, u32[]{:S(2)}) copy-start(pred[1024,1024]{0,1:T(8,128)(4,1)} %fusion.8) | copy-start | bytes 3145732
  81.6 4.1 copy-start.10
  82.9 2.8 copy-start.21
  82.9 2.8 copy-start.23
  83.1 2.6 copy-start.15
  83.1 2.6 copy-start.17
  85.7 3.4 copy-start.26
  89.1 0.8 copy-start.13
  97.9 263.0 %all-reduce.2.cloned.1.call-start = ((), (), s32[]{:S(2)}) async-start(), calls=%async_computation.5 | async-start | bytes 2359296 | tf_op jit(solution)/shard_map/psum | solution.py:159
  98.5 269.4 %all-gather.6.cloned.1.call-start = ((), (), s32[]{:S(2)}) async-start(), calls=%async_computation.3 | async-start | bytes 20054016 | tf_op jit(solution)/shard_map/all_gather | solution.py:121
  205.8 160.7 %copy-start.4 = (f32[64,4608]{1,0:T(8,128)S(1)}, f32[64,4608]{1,0:T(8,128)}, u32[]{:S(2)}) copy-start(f32[64,4608]{1,0:T(8,128)} %reduce-scatter.2.cloned.1.call-done) | copy-start | bytes 3538948
  205.9 187.4 %all-gather.8.cloned.1.call-start = ((), (), s32[]{:S(2)}) async-start(), calls=%async_computation.4 | async-start | bytes 10027008 | tf_op jit(solution)/shard_map/all_gather | solution.py:83
  360.8 5.9 %copy-start.5 = (bf16[64,4608]{1,0:T(8,128)(2,1)S(1)}, bf16[64,4608]{1,0:T(8,128)(2,1)}, u32[]{:S(2)}) copy-start(bf16[64,4608]{1,0:T(8,128)(2,1)} %param.10) | copy-start | bytes 1769476
  360.8 5.9 %copy-start.19 = (f32[4608]{0:T(1024)S(1)}, f32[4608]{0:T(1024)}, u32[]{:S(2)}) copy-start(f32[4608]{0:T(1024)} %param.12) | copy-start | bytes 55300
  367.9 25.4 %copy-start.20 = (f32[4608]{0:T(1024)S(1)}, f32[4608]{0:T(1024)}, u32[]{:S(2)}) copy-start(f32[4608]{0:T(1024)} %param.12) | copy-start | bytes 55300
  393.3 14.5 %copy-start.2 = (f32[1024,4608]{1,0:T(8,128)S(1)}, f32[1024,4608]{1,0:T(8,128)}, u32[]{:S(2)}) copy-start(f32[1024,4608]{1,0:T(8,128)} %all-gather.6.cloned.1.call-done) | copy-start | bytes 56623108
  393.3 17.2 %copy-start.3 = (bf16[1024,4608]{1,0:T(8,128)(2,1)S(1)}, bf16[1024,4608]{1,0:T(8,128)(2,1)}, u32[]{:S(2)}) copy-start(bf16[1024,4608]{1,0:T(8,128)(2,1)} %all-gather.8.cloned.1.call-done) | copy-start | bytes 28311556
  417.9 6.4 %copy-start.12 = (pred[1024,1024]{0,1:T(8,128)(4,1)S(1)}, pred[1024,1024]{0,1:T(8,128)(4,1)}, u32[]{:S(2)}) copy-start(pred[1024,1024]{0,1:T(8,128)(4,1)} %fusion.8) | copy-start | bytes 3145732
  430.6 5.7 %copy-start.16 = (bf16[1024,1,2,64]{0,3,2,1:T(8,128)(2,1)S(1)}, bf16[1024,1,2,64]{0,3,2,1:T(8,128)(2,1)}, u32[]{:S(2)}) copy-start(bf16[1024,1,2,64]{0,3,2,1:T(8,128)(2,1)} %copy-done.15) | copy-start | bytes 786436
  430.6 5.7 %copy-start.18 = (bf16[1024,1,2,64]{0,3,2,1:T(8,128)(2,1)S(1)}, bf16[1024,1,2,64]{0,3,2,1:T(8,128)(2,1)}, u32[]{:S(2)}) copy-start(bf16[1024,1,2,64]{0,3,2,1:T(8,128)(2,1)} %copy-done.17) | copy-start | bytes 786436
  436.3 15.3 %copy-start.22 = (bf16[1024,1,64]{0,2,1:T(8,128)(2,1)S(1)}, bf16[1024,1,64]{0,2,1:T(8,128)(2,1)}, u32[]{:S(2)}) copy-start(bf16[1024,1,64]{0,2,1:T(8,128)(2,1)} %copy-done.21) | copy-start | bytes 393220
  436.3 15.3 %copy-start.24 = (bf16[1024,1,64]{0,2,1:T(8,128)(2,1)S(1)}, bf16[1024,1,64]{0,2,1:T(8,128)(2,1)}, u32[]{:S(2)}) copy-start(bf16[1024,1,64]{0,2,1:T(8,128)(2,1)} %copy-done.23) | copy-start | bytes 393220
  451.6 15.6 %copy-start.7 = (f32[1024,64]{0,1:T(8,128)S(1)}, f32[1024,64]{0,1:T(8,128)}, u32[]{:S(2)}) copy-start(f32[1024,64]{0,1:T(8,128)} %copy-done.6) | copy-start | bytes 786436
  451.6 15.6 %copy-start.9 = (f32[1024,64]{0,1:T(8,128)S(1)}, f32[1024,64]{0,1:T(8,128)}, u32[]{:S(2)}) copy-start(f32[1024,64]{0,1:T(8,128)} %copy-done.8) | copy-start | bytes 786436
  478.9 8.4 %copy-start.14 = (bf16[2,1024,128]{1,2,0:T(8,128)(2,1)S(1)}, bf16[2,1024,128]{1,2,0:T(8,128)(2,1)}, u32[]{:S(2)}) copy-start(bf16[2,1024,128]{1,2,0:T(8,128)(2,1)} %copy-done.13) | copy-start | bytes 1572868
  487.3 7.7 %copy-start.1 = (bf16[1,2,128,4608]{3,2,1,0:T(8,128)(2,1)S(1)}, bf16[1,2,128,4608]{3,2,1,0:T(8,128)(2,1)}, u32[]{:S(2)}) copy-start(bf16[1,2,128,4608]{3,2,1,0:T(8,128)(2,1)} %param.14) | copy-start | bytes 7077892
Sparse Core Ops, SparseCore 0:
  11.7 60.7 all-gather.3
  98.0 107.8 reduce-scatter.1
  207.6 120.1 all-gather.5
  329.3 63.9 all-gather.7
Sparse Core Ops, SparseCore 1:
  100.8 259.9 all-reduce.1
where the time goes:
time: 503 us; the launch traced here: 502 us
  waiting for transfers between devices  326 us (65%)
  matrix products  89 us (18%)
  other arithmetic  44.8 us (9%)
  local copies, waits for them, and re-layouts  26.1 us (5%)
  between operations  15.6 us (3%)
    psum x1, waiting for transfers between devices, local(): lax.psum(own_delta.astype(jnp.bfloat16), 'group').astype(jnp.float32)  154 us
    reduce_scatter x1, waiting for transfers between devices, local(): lax.psum_scatter(jnp.dot(head_flat, out_flat, preferred_element_type=jnp....  107 us
    all_gather x1, waiting for transfers between devices, local(): gathered = lax.all_gather(normed, 'fsdp', axis=0, tiled=True)  46.2 us
    unnamed x56, local copies, waits for them, and re-layouts  19.4 us
    all_gather x1, waiting for transfers between devices, local(): every_cotangent = lax.all_gather(cotangent, 'fsdp', axis=0, tiled=True)  17.4 us
    dot_general x1, matrix products, attend_back(): dquery = jnp.dot(dscore, keyed, preferred_element_type=jnp.float32)  15.6 us
    dot_general x1, matrix products, attend_back(): dkey = jnp.dot(dscore.T, query, preferred_element_type=jnp.float32)  14.1 us
    reduce_sum x1, other arithmetic, rms_backward(): jnp.mean(dnorm * normal, axis=-1, keepdims=True)  12.5 us
  transfers between devices with their start and end apart: 5, of which 4 were waited for; matrix products, arithmetic and copies ran while one was open for 6% of the time, Pallas kernels for 0%

commit v1 on v0

--- a/solution.py
+++ b/solution.py
@@ -1,22 +1,291 @@
+import functools
+
 import jax
 import jax.numpy as jnp
 from jax import lax
+from jax.experimental import pallas as pl
+from jax.experimental.pallas import tpu as pltpu
 from jax.sharding import PartitionSpec as P
 
 softcap = 50.0
 query_scale = 1.0 / 12.0
-
-
-def rms_norm(values, gain):
+MESH = pl.DeviceIdType.MESH
+WIDTH = 4608
+HALF = WIDTH // 2
+ROWS = 64
+N1, N2, NQ = 4 * 128, 12 * 128, 5 * 128
+NP = N1 + N2
+
+
+def place():
+    group, fsdp = lax.axis_index("group"), lax.axis_index("fsdp")
+    return group // 2, group % 2, fsdp // 8, (fsdp // 2) % 4, fsdp % 2
+
+
+def device(x, zh, zl, y, c):
+    return (x * 2 + zh, (zl * 4 + y) * 2 + c)
+
+
+class Sender:
+    def __init__(self, sems):
+        self.sems, self.copies = sems, []
+
+    def __call__(self, src, dst, recv, to):
+        copy = pltpu.make_async_remote_copy(
+            src_ref=src,
+            dst_ref=dst,
+            send_sem=self.sems.at[len(self.copies)],
+            recv_sem=recv,
+            device_id=to,
+            device_id_type=MESH,
+        )
+        copy.start()
+        self.copies.append(copy)
+
+    def arrived(self, ref, recv, to):
+        pltpu.make_async_remote_copy(
+            src_ref=ref,
+            dst_ref=ref,
+            send_sem=self.sems.at[0],
+            recv_sem=recv,
+            device_id=to,
+            device_id_type=MESH,
+        ).wait_recv()
+
+    def finish(self):
+        for copy in self.copies:
+            copy.wait_send()
+
+
+SPREAD_SENDS = 57
+
+
+def spread(own, full, send, piece_sems, pair_sems, local_sem):
+    x, zh, zl, y, c = place()
+    k, kz = zl * 4 + y, (1 - zl) * 4 + y
+    ys = [(y + 1) % 4, (y + 3) % 4, (y + 2) % 4]
+    to_sib = device(x, zh, zl, y, 1 - c)
+    to_z = device(x, zh, 1 - zl, y, c)
+    to_y = [device(x, zh, zl, yy, c) for yy in ys]
+    to_x = [device(xx, zh, zl, y, c) for xx in [(x + 1) % 4, (x + 3) % 4, (x + 2) % 4]]
+    quarter = lambda w: pl.ds(pl.multiple_of(NP + w * NQ, 128), NQ)
+    cols = {"a": pl.ds(0, N1), "b": pl.ds(N1, N2), "q": quarter(x)}
+    index = {"a": 0, "b": 1, "q": 2 + x}
+
+    def block(kk, t):
+        return full.at[2 * kk + c, :, cols[t]]
+
+    def push(kk, t, to):
+        src = own.at[:, cols[t]] if kk is k else block(kk, t)
+        send(src, block(kk, t), piece_sems.at[index[t], kk], to)
+
+    def await_piece(kk, t):
+        send.arrived(block(kk, t), piece_sems.at[index[t], kk], to_sib)
+
+    def pair(kk, lo, size, slot):
+        ref = full.at[2 * kk + c, :, pl.ds(lo, size)]
+        send(ref, ref, pair_sems.at[kk, slot], to_sib)
+
+    keep = pltpu.make_async_copy(own, full.at[2 * k + c], local_sem)
+    keep.start()
+    for t in ("q", "a"):
+        push(k, t, to_z)
+    for t in ("b", "q", "a"):
+        for to in to_y:
+            push(k, t, to)
+    push(k, "b", to_z)
+    send(own, full.at[2 * k + c], pair_sems.at[k, 0], to_sib)
+
+    for t in ("q", "a"):
+        await_piece(kz, t)
+        for to in to_y:
+            push(kz, t, to)
+    for to in to_x:
+        push(kz, "q", to)
+    for yy in ys:
+        kk = zl * 4 + yy
+        await_piece(kk, "b")
+        push(kk, "b", to_z)
+        await_piece(kk, "q")
+        for to in to_x:
+            push(kk, "q", to)
+        await_piece(kk, "a")
+        pair(kk, 0, NP, 0)
+    await_piece(kz, "b")
+    pair(kz, 0, NP, 0)
+    for yy in ys:
+        kk = (1 - zl) * 4 + yy
+        await_piece(kk, "q")
+        for to in to_x:
+            push(kk, "q", to)
+        await_piece(kk, "a")
+        await_piece(kk, "b")
+        pair(kk, 0, NP, 0)
+    others = [kz] + [zl * 4 + yy for yy in ys] + [(1 - zl) * 4 + yy for yy in ys]
+    for kk in others:
+        for step in (1, 3, 2):
+            w = (x + step) % 4
+            send.arrived(full.at[2 * kk + c, :, quarter(w)], piece_sems.at[2 + w, kk], to_sib)
+        pair(kk, NP, 4 * NQ, 1)
+    send.arrived(full.at[2 * k + 1 - c], pair_sems.at[k, 0], to_sib)
+    for kk in others:
+        send.arrived(full.at[2 * kk + 1 - c, :, pl.ds(0, NP)], pair_sems.at[kk, 0], to_sib)
+        send.arrived(full.at[2 * kk + 1 - c, :, pl.ds(NP, 4 * NQ)], pair_sems.at[kk, 1], to_sib)
+    keep.wait()
+
+
+def near():
+    x, zh, zl, y, c = place()
+    out = [device(x, zh, zl, y, 1 - c), device(x, zh, 1 - zl, y, c)]
+    out += [device(x, zh, zl, (y + s) % 4, c) for s in (1, 2, 3)]
+    return out + [device((x + s) % 4, zh, zl, y, c) for s in (1, 2, 3)]
+
+
+def greet(devices):
+    barrier = pltpu.get_barrier_semaphore()
+    for to in devices:
+        pl.semaphore_signal(barrier, inc=1, device_id=to, device_id_type=MESH)
+
+
+def met(devices):
+    pl.semaphore_wait(pltpu.get_barrier_semaphore(), len(devices))
+
+
+def normed_kernel(tokens, gain, full, own, send_sems, piece_sems, pair_sems, local_sem):
+    greet(near())
+    values = tokens[...].astype(jnp.float32)
     scale = lax.rsqrt(jnp.mean(values * values, axis=-1, keepdims=True) + 1e-06)
-    return values * scale * gain
-
-
-def rms_backward(values, gain, grads):
-    scale = lax.rsqrt(jnp.mean(values * values, axis=-1, keepdims=True) + 1e-06)
-    normal = values * scale
-    dnorm = grads * gain
-    return scale * (dnorm - normal * jnp.mean(dnorm * normal, axis=-1, keepdims=True))
+    own[...] = (values * scale * gain[...]).astype(jnp.bfloat16)
+    met(near())
+    send = Sender(send_sems)
+    spread(own, full, send, piece_sems, pair_sems, local_sem)
+    send.finish()
+
+
+def gather_normed(tokens, gain):
+    vmem = pl.BlockSpec(memory_space=pltpu.VMEM)
+    return pl.pallas_call(
+        normed_kernel,
+        out_shape=jax.ShapeDtypeStruct((16, ROWS, WIDTH), jnp.bfloat16),
+        in_specs=[vmem, vmem],
+        out_specs=pl.BlockSpec(memory_space=pl.ANY),
+        scratch_shapes=[
+            pltpu.VMEM((ROWS, WIDTH), jnp.bfloat16),
+            pltpu.SemaphoreType.DMA((SPREAD_SENDS,)),
+            pltpu.SemaphoreType.DMA((6, 8)),
+            pltpu.SemaphoreType.DMA((8, 2)),
+            pltpu.SemaphoreType.DMA,
+        ],
+        compiler_params=pltpu.CompilerParams(
+            collective_id=0, has_side_effects=True, vmem_limit_bytes=24 * 2**20
+        ),
+        name="gather_normed",
+    )(tokens, gain)
+
+
+def stacked(rows):
+    return jnp.concatenate([rows[:, :HALF], rows[:, HALF:]], axis=0)
+
+
+def unstacked(rows):
+    return jnp.concatenate([rows[:8], rows[8:]], axis=1)
+
+
+def middle_kernel(
+    heads, weight, tokens, cotangent, gain, output, full,
+    partial, received, mate, total, mine, group_in, own,
+    send_sems, mate_sem, part_sems, group_sems, piece_sems, pair_sems, local_sem,
+):
+    x, zh, zl, y, c = place()
+    k, g = zl * 4 + y, x * 2 + zh
+    sib = device(x, zh, zl, y, 1 - c)
+    chips = [(a, b) for a in range(2) for b in range(4)][1:]
+    fellows = [((zl + a) % 2, (y + b) % 4) for a, b in chips]
+    to_fellows = [device(x, zh, a, b, c) for a, b in fellows]
+    kin = [((x + b) % 4, (zh + a) % 2) for a, b in chips]
+    to_kin = [device(a, b, zl, y, c) for a, b in kin]
+    greet([sib] + to_fellows + to_kin)
+    for core in range(2):
+        left = jnp.dot(heads[pl.ds(core * 64, 64)], weight[:, pl.ds(0, HALF)], preferred_element_type=jnp.float32)
+        right = jnp.dot(heads[pl.ds(core * 64, 64)], weight[:, pl.ds(HALF, HALF)], preferred_element_type=jnp.float32)
+        for kk in range(8):
+            both = jnp.concatenate([left[kk * 8 : kk * 8 + 8], right[kk * 8 : kk * 8 + 8]], axis=0)
+            partial[core, kk] = both.astype(jnp.bfloat16)
+    met([sib] + to_fellows + to_kin)
+    send = Sender(send_sems)
+    send(partial.at[1 - c], mate, mate_sem, sib)
+    send.arrived(mate, mate_sem, sib)
+    for kk in range(8):
+        total[kk] = (partial[c, kk].astype(jnp.float32) + mate[kk].astype(jnp.float32)).astype(jnp.bfloat16)
+    for (a, b), to in zip(fellows, to_fellows):
+        send(total.at[a * 4 + b], received.at[k], part_sems.at[k], to)
+    both = partial[c, k].astype(jnp.float32) + mate[k].astype(jnp.float32)
+    for a, b in fellows:
+        kk = a * 4 + b
+        send.arrived(received.at[kk], part_sems.at[kk], sib)
+        both = both + received[kk].astype(jnp.float32)
+    attn = unstacked(both)
+    scale = lax.rsqrt(jnp.mean(attn * attn, axis=-1, keepdims=True) + 1e-06)
+    normal = attn * scale
+    out = tokens[...] + normal * gain[...]
+    dnorm = cotangent[...] * gain[...]
+    grad = scale * (dnorm - normal * jnp.mean(dnorm * normal, axis=-1, keepdims=True))
+    mine[0] = stacked(grad).astype(jnp.bfloat16)
+    mine[1] = stacked(out).astype(jnp.bfloat16)
+    for i in range(2):
+        for to in to_kin:
+            send(mine.at[i], group_in.at[i, g], group_sems.at[i, g], to)
+    group_in[0, g] = mine[0]
+    group_in[1, g] = mine[1]
+    for a, b in kin:
+        gg = a * 2 + b
+        send.arrived(group_in.at[0, gg], group_sems.at[0, gg], sib)
+    for gg in range(0, 8, 2):
+        first = unstacked(group_in[0, gg].astype(jnp.float32))
+        second = unstacked(group_in[0, gg + 1].astype(jnp.float32))
+        own[pl.ds(gg * 8, 16), :] = jnp.concatenate([first, second], axis=0).astype(jnp.bfloat16)
+    spread(own, full, send, piece_sems, pair_sems, local_sem)
+    for a, b in kin:
+        gg = a * 2 + b
+        send.arrived(group_in.at[1, gg], group_sems.at[1, gg], sib)
+    for gg in range(0, 8, 2):
+        first = unstacked(group_in[1, gg].astype(jnp.float32))
+        second = unstacked(group_in[1, gg + 1].astype(jnp.float32))
+        output[pl.ds(gg * 8, 16), :] = jnp.concatenate([first, second], axis=0).astype(jnp.bfloat16)
+    send.finish()
+
+
+def middle(heads, weight, tokens, cotangent, gain):
+    vmem = pl.BlockSpec(memory_space=pltpu.VMEM)
+    return pl.pallas_call(
+        middle_kernel,
+        out_shape=(
+            jax.ShapeDtypeStruct((ROWS, WIDTH), jnp.bfloat16),
+            jax.ShapeDtypeStruct((16, ROWS, WIDTH), jnp.bfloat16),
+        ),
+        in_specs=[vmem] * 5,
+        out_specs=(vmem, pl.BlockSpec(memory_space=pl.ANY)),
+        scratch_shapes=[
+            pltpu.VMEM((2, 8, 16, HALF), jnp.bfloat16),
+            pltpu.VMEM((8, 16, HALF), jnp.bfloat16),
+            pltpu.VMEM((8, 16, HALF), jnp.bfloat16),
+            pltpu.VMEM((8, 16, HALF), jnp.bfloat16),
+            pltpu.VMEM((2, 16, HALF), jnp.bfloat16),
+            pltpu.VMEM((2, 8, 16, HALF), jnp.bfloat16),
+            pltpu.VMEM((ROWS, WIDTH), jnp.bfloat16),
+            pltpu.SemaphoreType.DMA((1 + 7 + 14 + SPREAD_SENDS,)),
+            pltpu.SemaphoreType.DMA,
+            pltpu.SemaphoreType.DMA((8,)),
+            pltpu.SemaphoreType.DMA((2, 8)),
+            pltpu.SemaphoreType.DMA((6, 8)),
+            pltpu.SemaphoreType.DMA((8, 2)),
+            pltpu.SemaphoreType.DMA,
+        ],
+        compiler_params=pltpu.CompilerParams(
+            collective_id=1, has_side_effects=True, vmem_limit_bytes=32 * 2**20
+        ),
+        name="middle",
+    )(heads, weight, tokens, cotangent, gain)
 
 
 def tables(length, width):
@@ -80,10 +349,8 @@
     momentum,
     fragment,
 ):
-    every_cotangent = lax.all_gather(cotangent, "fsdp", axis=0, tiled=True)
-    inputs = tokens.astype(jnp.float32)
-    normed = rms_norm(inputs, pre_gain).astype(jnp.bfloat16)
-    gathered = lax.all_gather(normed, "fsdp", axis=0, tiled=True)
+    group = lax.axis_index("group")
+    gathered = gather_normed(tokens, pre_gain[None, :]).reshape(16 * ROWS, WIDTH)
     length, width = gathered.shape
     key_heads, parts, head_dim = (qkv_weight.shape[1], qkv_weight.shape[2], qkv_weight.shape[3])
     query_count = parts - 2
@@ -112,17 +379,12 @@
     heads = jnp.transpose(result.astype(jnp.bfloat16), (2, 0, 1, 3))
     head_flat = heads.reshape(length, key_heads * query_count * head_dim)
     out_flat = out_weight.reshape(key_heads * query_count * head_dim, width)
-    attn = lax.psum_scatter(
-        jnp.dot(head_flat, out_flat, preferred_element_type=jnp.float32),
-        "fsdp",
-        scatter_dimension=0,
-        tiled=True,
-    )
-    attn_all = lax.all_gather(attn, "fsdp", axis=0, tiled=True)
-    grad_rows = rms_backward(attn_all, post_gain, every_cotangent.astype(jnp.float32)).astype(
-        jnp.bfloat16
-    )
-    output = (inputs + rms_norm(attn, post_gain)).astype(jnp.bfloat16)
+    share = lax.dynamic_slice_in_dim(head_flat.reshape(8, 2, 8, 8, 256), group, 1, axis=2)
+    share = jnp.transpose(share[:, :, 0], (1, 0, 2, 3)).reshape(128, 256)
+    own_tokens = lax.dynamic_slice_in_dim(tokens, group * 8, 8, axis=0).astype(jnp.float32)
+    own_cotangent = lax.dynamic_slice_in_dim(cotangent, group * 8, 8, axis=0).astype(jnp.float32)
+    output, grad_rows = middle(share, out_flat, own_tokens, own_cotangent, post_gain[None, :])
+    grad_rows = grad_rows.reshape(length, width)
     grad_out = lax.dot_general(
         head_flat, grad_rows, (((0,), (0,)), ((), ())), preferred_element_type=jnp.float32
     )
@@ -155,8 +417,7 @@
         preferred_element_type=jnp.float32,
     )
     grad_qkv = grad_qkv.astype(jnp.bfloat16).reshape(qkv_weight.shape)
-    own_delta = outer_delta[0].astype(jnp.float32)
-    total = lax.psum(own_delta.astype(jnp.bfloat16), "group").astype(jnp.float32)
+    total = lax.psum(outer_delta[0], "group").astype(jnp.float32)
     new_momentum, new_fragment = nesterov(total / lax.axis_size("group"), momentum, fragment)
     return (output, grad_qkv, grad_out, new_momentum, new_fragment)
 

time: 503 us -> 250 us (0.50)
  waiting for transfers between devices: 326 us -> 0.68 us
  Pallas kernels: 0 us -> 120 us
  other arithmetic: 44.8 us -> 12.1 us
  matrix products: 89 us -> 71.8 us
    psum x1, waiting for transfers between devices: 154 us -> 0.01 us  [local(): total = lax.psum(outer_delta[0], 'group').astype(jnp.float32)]
    pallas_call x0 -> x2, Pallas kernels: none -> 120 us  [the longest x1 68.2 us: middle(): pl.pallas_call(middle_kernel, out_shape=(jax.ShapeDtypeStruct((ROWS, WIDT...]
    reduce_scatter x1 -> x0, waiting for transfers between devices: 107 us -> none  [local(): lax.psum_scatter(jnp.dot(head_flat, out_flat, preferred_element_type=jnp....]
    all_gather x3 -> x0, waiting for transfers between devices: 63.6 us -> none  [the longest x1 46.2 us: local(): gathered = lax.all_gather(normed, 'fsdp', axis=0, tiled=True)]
    reduce_sum x4 -> x0, other arithmetic: 22.1 us -> none  [the longest x1 12.5 us: rms_backward(): jnp.mean(dnorm * normal, axis=-1, keepdims=True)]
    convert_element_type x3 -> x1, other arithmetic: 10.6 us -> 0.91 us  [local(): lax.dynamic_slice_in_dim(cotangent, group * 8, 8, axis=0)]
    dot_general x1 -> x0, matrix products: 7.91 us -> none  [local(): jnp.dot(head_flat, out_flat, preferred_element_type=jnp.float32)]
    unnamed x56 -> x49, local copies, waits for them, and re-layouts: 19.4 us -> 16.8 us
  transfers between devices with their start and end apart: 5 -> 1, of which waited for: 4 -> 0; matrix products, arithmetic and copies ran while one was open for 6% -> 42% of each run, Pallas kernels for 0% -> 48%
where the time goes in v1:
time: 250 us; the launch traced here: 248 us
  Pallas kernels  120 us (48%)
  matrix products  71.8 us (29%)
  local copies, waits for them, and re-layouts  29.3 us (12%)
  between operations  14.4 us (6%)
  other arithmetic  12.1 us (5%)
    pallas_call x1, Pallas kernels, middle(): pl.pallas_call(middle_kernel, out_shape=(jax.ShapeDtypeStruct((ROWS, WIDT...  68.2 us
    pallas_call x1, Pallas kernels, gather_normed(): pl.pallas_call(normed_kernel, out_shape=jax.ShapeDtypeStruct((16, ROWS, W...  51.7 us
    unnamed x49, local copies, waits for them, and re-layouts  16.8 us
    dot_general x1, matrix products, attend_back(): dquery = jnp.dot(dscore, keyed, preferred_element_type=jnp.float32)  15.1 us
    dot_general x1, matrix products, attend_back(): dkey = jnp.dot(dscore.T, query, preferred_element_type=jnp.float32)  14.8 us
    dot_general x1, matrix products, local(): lax.dot_general(gathered, grad_proj.reshape(length, key_heads * parts * h...  10.4 us
    dot_general x1, matrix products, local(): lax.dot_general(head_flat, grad_rows, (((0,), (0,)), ((), ())), preferred...  7.68 us
    dot_general x1, local copies, waits for them, and re-layouts, local(): jnp.dot(gathered, qkv_weight.reshape(width, key_heads * parts * head_dim)...  6.73 us
  transfers between devices with their start and end apart: 1, of which 0 were waited for; matrix products, arithmetic and copies ran while one was open for 42% of the time, Pallas kernels for 48%

profile of v1, /device:TPU:1, one launch (start us, length us, event | category | flops | bytes accessed | tf_op | source)
XLA Modules:
  0.0 248.3 jit_solution(12231996703040313618)
XLA Ops:
  7.2 0.0 all-reduce.2.cloned.1.call-start
  7.2 0.7 all-reduce.2.cloned.1.call-update
  7.9 0.7 broadcast_in_dim.11.gain
  8.7 0.0 copy-start.2
  8.7 5.4 %copy.61 = bf16[576,8,4,128]{3,1,2,0:T(8,128)(2,1)} copy(bf16[576,8,4,128]{3,2,1,0:T(4,128)(2,1)} %bitcast.110) | data formatting | bytes 9437184
  14.1 6.7 %copy.37 = bf16[512,4608]{1,0:T(8,128)(2,1)} copy(bf16[512,4608]{0,1:T(8,128)(2,1)} %bitcast.109) | data formatting | bytes 9437184 | tf_op jit(solution)/shard_map/dot_general | solution.py:357
  20.8 1.0 fusion.47
  21.8 0.0 copy-done.2
  21.8 0.0 copy-start.5
  21.8 0.0 slice-start.1
  21.8 51.7 %gather_normed.1 = bf16[16,64,4608]{2,1,0:T(8,128)(2,1)S(1)} custom-call(bf16[64,4608]{1,0:T(8,128)(2,1)S(1)} %copy-done.2, f32[1,4608]{1,0:T(1,128)S(1)} %broadcast_in_dim.11.gain), custom_call_target="tpu_custom_call" | custom-call | tf_op jit(solution)/shard_map/gather_normed/pallas_call | solution.py:167
  73.6 0.0 copy-start
  73.6 0.0 slice-done
  73.6 0.0 slice-done.1
  73.6 0.0 copy-start.17
  73.6 5.0 %convolution_bitcast_fusion = f32[1024,1,4,128]{0,3,2,1:T(8,128)S(1)} fusion(bf16[1024,4608,1]{1,0,2:T(8,128)(2,1)S(1)} %bitcast.102, bf16[4,128,4608]{2,1,0:T(8,128)(2,1)S(1)} %bitcast.113), kind=kOutput, calls=%fused_computation.22 | convolution fusion | flops 4831838208 | bytes 16252928 | tf_op jit(solution)/shard_map/dot_general | solution.py:357
  78.7 0.0 copy-done
  78.7 0.0 copy-start.7
  78.8 1.2 subtract_convert_fusion.3
  79.9 0.0 copy-done.17
  80.0 0.0 copy-start.15
  80.0 0.6 fusion.6
  80.6 0.0 copy-start.8
  80.6 0.0 copy-done.5
  80.6 0.2 subtract_convert_fusion.1
  80.8 0.0 copy-start.11
  80.8 0.0 copy-start.13
  80.8 2.6 %fusion.3 = (f32[2,1024]{1,0:T(2,128)S(1)}, f32[2,1024,1024]{1,2,0:T(8,128)S(1)}) fusion(pred[1024,1024]{0,1:T(8,128)(4,1)S(1)} %fusion.6, bf16[1024,1,64]{0,2,1:T(8,128)(2,1)S(1)} %get-tuple-element.33, bf16[1024,1,64]{0,2,1:T(8,128)(2,1)S(1)} %get-tuple-element.32, bf16[1024,1,2,64]{0,3,2,1:T(8,128)(2,1)S(1)} %get-tuple-element.27, ...), kind=kOutput, calls=%fused_computation.9 | convolution fusion | flops 546830336 | bytes 10231808 | tf_op jit(solution)/shard_map/vmap(vmap())/dot_general | solution.py:316
  83.3 0.0 copy-done.15
  83.4 0.0 copy-done.11
  83.4 0.0 copy-done.13
  83.4 0.0 copy-start.18
  83.4 0.0 copy-done.7
  83.4 0.0 copy-done.8
  83.4 0.0 copy-start.16
  83.4 0.0 copy-start.1
  83.4 4.0 %fusion.21 = bf16[2,1024,128]{1,2,0:T(8,128)(2,1)} fusion(f32[1024,1,4,128]{0,3,2,1:T(8,128)S(1)} %convolution_bitcast_fusion, f32[2,1024,1024]{1,2,0:T(8,128)S(1)} %get-tuple-element.37, f32[2,1024]{1,0:T(2,128)S(1)} %get-tuple-element.36, pred[1024,1024]{0,1:T(8,128)(4,1)S(1)} %fusion.6), kind=kOutput, calls=%fused_computation.24 | convolution fusion | flops 547618816 | bytes 10231808 | tf_op jit(solution)/shard_map/vmap(vmap())/dot_general | solution.py:321
  87.4 0.0 copy-done.18
  87.5 2.0 copy.41
  89.5 2.2 reshape_reshape.3
  91.6 0.8 dynamic-slice_bitcast_fusion
  92.5 0.0 copy-done.16
  92.5 0.9 dynamic-slice_convert_fusion
  93.4 0.0 copy-done.1
  93.4 0.0 slice-start.2
  93.5 68.2 %middle.1 = (bf16[64,4608]{1,0:T(8,128)(2,1)S(1)}, bf16[16,64,4608]{2,1,0:T(8,128)(2,1)S(1)}) custom-call(bf16[128,256]{1,0:T(8,128)(2,1)S(1)} %bitcast.106, bf16[256,4608]{1,0:T(8,128)(2,1)S(1)} %bitcast.104, f32[8,4608]{1,0:T(8,128)S(1)} %get-tuple-element.39.tokens, f32[8,4608]{1,0:T(8,128)S(1)} %get-tuple-element.38.cotangent, ...), custom_call_target="tpu_custom_call" | custom-call | tf_op jit(solution)/shard_map/middle/pallas_call | solution.py:260
  161.6 0.0 copy-start.3
  161.7 0.0 slice-start.3
  161.7 2.6 %convolution_convert_fusion.2 = bf16[1024,256]{0,1:T(8,128)(2,1)S(1)} fusion(bf16[1024,4608]{1,0:T(8,128)(2,1)S(1)} %bitcast.107, bf16[256,4608]{1,0:T(8,128)(2,1)S(1)} %bitcast.105), kind=kOutput, calls=%fused_computation.25 | convolution fusion | flops 2416181248 | bytes 12320768 | tf_op jit(solution)/shard_map/dot_general | solution.py:392
  164.3 2.0 copy-done.3
  166.3 5.7 %fusion.41 = f32[2,1024,1024]{1,2,0:T(8,128)} fusion(bf16[2,1024,128]{1,2,0:T(8,128)(2,1)S(1)} %bitcast.115, f32[1024,1,4,128]{0,3,2,1:T(8,128)} %copy-done.7), kind=kOutput, calls=%fused_computation.46 | convolution fusion | flops 536870912 | bytes 9175040 | tf_op jit(solution)/shard_map/vmap(vmap())/dot_general | solution.py:326
  172.0 0.0 slice-done.2
  172.0 3.9 %fusion.33 = bf16[1024,1,1,128]{0,3,2,1:T(8,128)(2,1)} fusion(bf16[2,1024,128]{1,2,0:T(8,128)(2,1)S(1)} %bitcast.116, f32[2,1024,1024]{1,2,0:T(8,128)S(1)} %bitcast.125, f32[2,1024]{1,0:T(2,128)S(1)} %get-tuple-element.36, pred[1024,1024]{0,1:T(8,128)(4,1)S(1)} %copy-done.9), kind=kOutput, calls=%fused_computation.29 | convolution fusion | flops 547487744 | bytes 10231808 | tf_op jit(solution)/shard_map/vmap(vmap())/dot_general | solution.py:327
  175.9 0.0 copy-done.12
  175.9 14.8 %fusion.27 = f32[1024,1,128]{0,2,1:T(8,128)} fusion(f32[2,1024,1024]{1,2,0:T(8,128)} %fusion.41, f32[2,1024,1024]{1,2,0:T(8,128)} %copy-done.18, bf16[1024,1,2,64]{0,3,2,1:T(8,128)(2,1)S(1)} %copy-done.14, bf16[1024,1,2,64]{0,3,2,1:T(8,128)(2,1)S(1)} %copy-done.12, f32[2,1024]{1,0:T(2,128)S(1)} %get-tuple-element.36, pred[1024,1024]{0,1:T(8,128)(4,1)S(1)} %copy-done.9), kind=kOutput, calls=%fused_computation.27 | convolution fusion | flops 571476992 | bytes 18882560 | tf_op jit(solution)/shard_map/vmap(vmap())/dot_general | solution.py:331
  190.7 15.1 %fusion.18 = f32[1024,1,2,128]{0,3,2,1:T(8,128)S(1)} fusion(f32[2,1024,1024]{1,2,0:T(8,128)} %fusion.41, f32[2,1024,1024]{1,2,0:T(8,128)} %copy-done.18, bf16[1024,64]{0,1:T(8,128)(2,1)} %bitcast.122, bf16[1024,64]{0,1:T(8,128)(2,1)S(1)} %bitcast.121, f32[2,1024]{1,0:T(2,128)S(1)} %get-tuple-element.36, pred[1024,1024]{0,1:T(8,128)(4,1)S(1)} %copy-done.9), kind=kOutput, calls=%fused_computation.23 | convolution fusion | flops 570952704 | bytes 19144704 | tf_op jit(solution)/shard_map/vmap(vmap())/dot_general | solution.py:330
  205.8 0.2 add_convert_fusion
  206.0 2.1 add_convert_fusion.2
  208.2 1.0 pad_maximum_fusion
  209.2 10.4 %convolution_convert_fusion = bf16[4608,512]{0,1:T(8,128)(2,1)} fusion(bf16[1024,512]{0,1:T(8,128)(2,1)S(1)} %bitcast.118, bf16[1024,4608]{1,0:T(8,128)(2,1)} %bitcast.103), kind=kOutput, calls=%fused_computation.6 | convolution fusion | flops 4834197504 | bytes 15204352 | tf_op jit(solution)/shard_map/dot_general | solution.py:413
  219.6 8.4 %copy.48 = bf16[4608,1,4,128]{3,2,1,0:T(4,128)(2,1)} copy(bf16[4608,1,4,128]{0,3,2,1:T(8,128)(2,1)} %bitcast.114) | data formatting | bytes 9437184
  228.1 7.7 %convolution_convert_fusion.1 = bf16[256,4608]{1,0:T(8,128)(2,1)} fusion(bf16[1024,256]{0,1:T(8,128)(2,1)S(1)} %bitcast.120, bf16[1024,4608]{1,0:T(8,128)(2,1)} %bitcast.108), kind=kOutput, calls=%fused_computation.7 | convolution fusion | flops 2417098752 | bytes 12320768 | tf_op jit(solution)/shard_map/dot_general | solution.py:388
  235.8 4.9 %multiply_subtract_fusion = (f32[128,4608]{1,0:T(8,128)}, f32[128,4608]{1,0:T(8,128)}) fusion(f32[128,4608]{1,0:T(8,128)S(1)} %copy-done.4, bf16[128,4608]{1,0:T(8,128)(2,1)} %all-reduce.2.cloned.1.call-done, f32[128,4608]{1,0:T(8,128)} %param.18), kind=kLoop, calls=%fused_computation.13 | loop fusion | flops 4718592 | bytes 10616832 | tf_op jit(solution)/shard_map/sub | solution.py:337
  240.6 0.8 copy.65
  (21 shorter events, 0.1 us)
Async XLA Ops:
  7.2 228.6 %all-reduce.2.cloned.1.call-start = ((), (), s32[]{:S(2)}) async-start(), calls=%async_computation | async-start | bytes 2359296 | tf_op jit(solution)/shard_map/psum | solution.py:420
  8.7 13.1 %copy-start.2 = (bf16[64,4608]{1,0:T(8,128)(2,1)S(1)}, bf16[64,4608]{1,0:T(8,128)(2,1)}, u32[]{:S(2)}) copy-start(bf16[64,4608]{1,0:T(8,128)(2,1)} %tokens.1) | copy-start | bytes 1769476
  20.8 52.8 %slice-start = ((s8[4718592]{0:T(1024)(128)(4,1)}), s8[4194304]{0:T(1024)(128)(4,1)S(1)}, s32[]{:S(2)}) async-start(s8[4718592]{0:T(1024)(128)(4,1)} %bitcast.111), calls=%async_computation.1 | async-start | bytes 8388608
  21.8 58.8 %copy-start.5 = (f32[1024,64]{0,1:T(8,128)}, f32[1024,64]{0,1:T(8,128)S(1)}, u32[]{:S(2)}) copy-start(f32[1024,64]{0,1:T(8,128)S(1)} %get-tuple-element.35) | copy-start | bytes 786436
  21.8 51.8 %slice-start.1 = ((s8[4718592]{0:T(1024)(128)(4,1)}), s8[524288]{0:T(1024)(128)(4,1)S(1)}, s32[]{:S(2)}) async-start(s8[4718592]{0:T(1024)(128)(4,1)} %bitcast.111), calls=%async_computation.2 | async-start | bytes 1048576
  73.6 5.1 %copy-start = (bf16[16,64,4608]{2,1,0:T(8,128)(2,1)}, bf16[16,64,4608]{2,1,0:T(8,128)(2,1)S(1)}, u32[]{:S(2)}) copy-start(bf16[16,64,4608]{2,1,0:T(8,128)(2,1)S(1)} %gather_normed.1) | copy-start | bytes 28311556
  73.6 6.3 %copy-start.17 = (s32[1024]{0:T(1024)S(1)}, s32[1024]{0:T(1024)}, u32[]{:S(2)}) copy-start(s32[1024]{0:T(1024)} %param.15) | copy-start | bytes 12292
  78.7 4.7 %copy-start.7 = (f32[1024,1,4,128]{0,3,2,1:T(8,128)}, f32[1024,1,4,128]{0,3,2,1:T(8,128)S(1)}, u32[]{:S(2)}) copy-start(f32[1024,1,4,128]{0,3,2,1:T(8,128)S(1)} %convolution_bitcast_fusion) | copy-start | bytes 6291460
  80.0 3.4 %copy-start.15 = (bf16[1024,1,64]{0,2,1:T(8,128)(2,1)}, bf16[1024,1,64]{0,2,1:T(8,128)(2,1)S(1)}, u32[]{:S(2)}) copy-start(bf16[1024,1,64]{0,2,1:T(8,128)(2,1)S(1)} %get-tuple-element.33) | copy-start | bytes 393220
  80.6 2.8 %copy-start.8 = (pred[1024,1024]{0,1:T(8,128)(4,1)}, pred[1024,1024]{0,1:T(8,128)(4,1)S(1)}, u32[]{:S(2)}) copy-start(pred[1024,1024]{0,1:T(8,128)(4,1)S(1)} %fusion.6) | copy-start | bytes 3145732
  80.8 2.6 %copy-start.11 = (bf16[1024,1,2,64]{0,3,2,1:T(8,128)(2,1)}, bf16[1024,1,2,64]{0,3,2,1:T(8,128)(2,1)S(1)}, u32[]{:S(2)}) copy-start(bf16[1024,1,2,64]{0,3,2,1:T(8,128)(2,1)S(1)} %get-tuple-element.26) | copy-start | bytes 786436
  80.8 2.6 %copy-start.13 = (bf16[1024,1,2,64]{0,3,2,1:T(8,128)(2,1)}, bf16[1024,1,2,64]{0,3,2,1:T(8,128)(2,1)S(1)}, u32[]{:S(2)}) copy-start(bf16[1024,1,2,64]{0,3,2,1:T(8,128)(2,1)S(1)} %get-tuple-element.27) | copy-start | bytes 786436
  83.4 4.1 %copy-start.18 = (f32[2,1024,1024]{1,2,0:T(8,128)}, f32[2,1024,1024]{1,2,0:T(8,128)S(1)}, u32[]{:S(2)}) copy-start(f32[2,1024,1024]{1,2,0:T(8,128)S(1)} %get-tuple-element.37) | copy-start | bytes 25165828
  83.4 9.1 %copy-start.16 = (f32[4608]{0:T(1024)S(1)}, f32[4608]{0:T(1024)}, u32[]{:S(2)}) copy-start(f32[4608]{0:T(1024)} %param.12) | copy-start | bytes 55300
  83.4 10.0 %copy-start.1 = (bf16[1,2,128,4608]{3,2,1,0:T(8,128)(2,1)S(1)}, bf16[1,2,128,4608]{3,2,1,0:T(8,128)(2,1)}, u32[]{:S(2)}) copy-start(bf16[1,2,128,4608]{3,2,1,0:T(8,128)(2,1)} %param.14) | copy-start | bytes 7077892
  93.4 78.6 %slice-start.2 = ((s8[8388608]{0:T(1024)(128)(4,1)}), s8[4194304]{0:T(1024)(128)(4,1)S(1)}, s32[]{:S(2)}) async-start(s8[8388608]{0:T(1024)(128)(4,1)} %bitcast.124), calls=%async_computation.3 | async-start | bytes 8388608
  161.6 4.7 %copy-start.3 = (bf16[16,64,4608]{2,1,0:T(8,128)(2,1)}, bf16[16,64,4608]{2,1,0:T(8,128)(2,1)S(1)}, u32[]{:S(2)}) copy-start(bf16[16,64,4608]{2,1,0:T(8,128)(2,1)S(1)} %get-tuple-element.8) | copy-start | bytes 28311556
  161.7 10.4 %slice-start.3 = ((s8[8388608]{0:T(1024)(128)(4,1)}), s8[4194304]{0:T(1024)(128)(4,1)S(1)}, s32[]{:S(2)}) async-start(s8[8388608]{0:T(1024)(128)(4,1)} %bitcast.124), calls=%async_computation.4 | async-start | bytes 8388608
  166.3 5.7 %copy-start.9 = (pred[1024,1024]{0,1:T(8,128)(4,1)S(1)}, pred[1024,1024]{0,1:T(8,128)(4,1)}, u32[]{:S(2)}) copy-start(pred[1024,1024]{0,1:T(8,128)(4,1)} %copy-done.8) | copy-start | bytes 3145732
  172.0 3.9 %copy-start.12 = (bf16[1024,1,2,64]{0,3,2,1:T(8,128)(2,1)S(1)}, bf16[1024,1,2,64]{0,3,2,1:T(8,128)(2,1)}, u32[]{:S(2)}) copy-start(bf16[1024,1,2,64]{0,3,2,1:T(8,128)(2,1)} %copy-done.11) | copy-start | bytes 786436
  172.0 3.9 %copy-start.14 = (bf16[1024,1,2,64]{0,3,2,1:T(8,128)(2,1)S(1)}, bf16[1024,1,2,64]{0,3,2,1:T(8,128)(2,1)}, u32[]{:S(2)}) copy-start(bf16[1024,1,2,64]{0,3,2,1:T(8,128)(2,1)} %copy-done.13) | copy-start | bytes 786436
  190.7 15.1 %copy-start.6 = (f32[1024,64]{0,1:T(8,128)S(1)}, f32[1024,64]{0,1:T(8,128)}, u32[]{:S(2)}) copy-start(f32[1024,64]{0,1:T(8,128)} %copy-done.5) | copy-start | bytes 786436
  219.6 8.4 %copy-start.10 = (bf16[2,1024,128]{1,2,0:T(8,128)(2,1)S(1)}, bf16[2,1024,128]{1,2,0:T(8,128)(2,1)}, u32[]{:S(2)}) copy-start(bf16[2,1024,128]{1,2,0:T(8,128)(2,1)} %fusion.21) | copy-start | bytes 1572868
  228.1 7.7 %copy-start.4 = (f32[128,4608]{1,0:T(8,128)S(1)}, f32[128,4608]{1,0:T(8,128)}, u32[]{:S(2)}) copy-start(f32[128,4608]{1,0:T(8,128)} %param.19) | copy-start | bytes 7077892
Sparse Core Ops, SparseCore 0:
  10.5 102.6 all-reduce.1

commit v2 on v1

--- a/solution.py
+++ b/solution.py
@@ -296,40 +296,244 @@
     return (jnp.cos(angle), jnp.sin(angle))
 
 
-def rotate(values, cosine, sine):
-    half = values.shape[-1] // 2
-    first, second = (values[..., :half], values[..., half:])
-    return jnp.concatenate(
-        [first * cosine - second * sine, second * cosine + first * sine], axis=-1
-    )
-
-
-def unrotate(grads, cosine, sine):
-    half = grads.shape[-1] // 2
-    first, second = (grads[..., :half], grads[..., half:])
-    return jnp.concatenate(
-        [first * cosine + second * sine, second * cosine - first * sine], axis=-1
-    )
-
-
-def attend(query, keyed, valued, allowed):
-    scores = jnp.dot(query, keyed.T, preferred_element_type=jnp.float32) * query_scale
-    capped = softcap * jnp.tanh(scores / softcap)
-    weights = jnp.where(allowed, jnp.exp(capped), jnp.float32(0.0))
-    probs = weights / jnp.sum(weights, axis=-1, keepdims=True)
-    rounded = probs.astype(jnp.bfloat16)
-    result = jnp.dot(rounded, valued, preferred_element_type=jnp.float32)
-    return (result, probs, rounded, capped)
-
-
-def attend_back(query, keyed, valued, probs, rounded, capped, grad_head):
-    dprob = jnp.dot(grad_head, valued.T, preferred_element_type=jnp.float32)
-    dvalue = jnp.dot(rounded.T, grad_head, preferred_element_type=jnp.float32)
-    dcap = probs * (dprob - jnp.sum(dprob * probs, axis=-1, keepdims=True))
-    dscore = (dcap * (1.0 - (capped / softcap) ** 2) * query_scale).astype(jnp.bfloat16)
-    dquery = jnp.dot(dscore, keyed, preferred_element_type=jnp.float32)
-    dkey = jnp.dot(dscore.T, query, preferred_element_type=jnp.float32)
-    return (dquery, dkey, dvalue)
+BLOCK = 256
+STEPS = 4
+
+
+def turn(values, cosine, sine):
+    return values * cosine + pltpu.roll(values, 64, 1) * sine
+
+
+def scored(keys, queries, first_key, start_row, query_row):
+    raw = lax.dot_general(keys, queries, (((1,), (1,)), ((), ())), preferred_element_type=jnp.float32)
+    soft = jnp.tanh(raw * (query_scale / softcap))
+    row = lax.broadcasted_iota(jnp.int32, raw.shape, 0) + first_key
+    allowed = (row >= start_row) & (row <= query_row)
+    return soft, jnp.where(allowed, jnp.exp(softcap * soft), 0.0)
+
+
+def forward_kernel(
+    starts, x, weight, cosine, sine, start_ref, query_ref, key_ref, value_ref, heads_ref, sums_ref, keep, keys, values_t
+):
+    i = pl.program_id(0)
+    proj = jnp.dot(x[...], weight[...], preferred_element_type=jnp.float32)
+    queries = [turn(proj[:, h * 128 : h * 128 + 128], cosine[...], sine[...]).astype(jnp.bfloat16) for h in range(2)]
+    key = turn(proj[:, 256:384], cosine[...], sine[...]).astype(jnp.bfloat16)
+    value = proj[:, 384:512]
+    query_ref[:, :128] = queries[0]
+    query_ref[:, 128:] = queries[1]
+    key_ref[...] = key
+    value_ref[...] = value.astype(jnp.bfloat16)
+    keys[i] = key
+    values_t[i] = value.T.astype(jnp.bfloat16)
+    start_row = start_ref[...]
+    query_row = lax.broadcasted_iota(jnp.int32, (1, BLOCK), 1) + i * BLOCK
+    first = starts[i * BLOCK] // BLOCK
+
+    def score(j, sums):
+        out = []
+        for h in range(2):
+            _, e = scored(keys[j], queries[h], j * BLOCK, start_row, query_row)
+            keep[h, j] = e
+            out.append(sums[h] + jnp.sum(e, axis=0, keepdims=True))
+        return tuple(out)
+
+    zero = jnp.zeros((1, BLOCK), jnp.float32)
+    sums = lax.fori_loop(first, i + 1, score, (zero, zero))
+    inverse = [1.0 / s for s in sums]
+    sums_ref[0:1, :] = inverse[0]
+    sums_ref[1:2, :] = inverse[1]
+
+    def mix(j, accs):
+        out = []
+        for h in range(2):
+            p = (keep[h, j] * inverse[h]).astype(jnp.bfloat16)
+            out.append(accs[h] + jnp.dot(values_t[j], p, preferred_element_type=jnp.float32))
+        return tuple(out)
+
+    zero = jnp.zeros((128, BLOCK), jnp.float32)
+    accs = lax.fori_loop(first, i + 1, mix, (zero, zero))
+    for h in range(2):
+        heads_ref[:, h * 128 : h * 128 + 128] = accs[h].T.astype(jnp.bfloat16)
+
+
+def forward(gathered, weight, cosine, sine, start):
+    rows = lambda n: pl.BlockSpec((BLOCK, n), lambda i, s: (i, 0))
+    return pl.pallas_call(
+        forward_kernel,
+        grid_spec=pltpu.PrefetchScalarGridSpec(
+            num_scalar_prefetch=1,
+            grid=(STEPS,),
+            in_specs=[
+                rows(WIDTH),
+                pl.BlockSpec((WIDTH, 512), lambda i, s: (0, 0)),
+                rows(128),
+                rows(128),
+                pl.BlockSpec((1, BLOCK), lambda i, s: (0, i)),
+            ],
+            out_specs=[rows(256), rows(128), rows(128), rows(256), pl.BlockSpec((8, BLOCK), lambda i, s: (0, i))],
+            scratch_shapes=[
+                pltpu.VMEM((2, STEPS, BLOCK, BLOCK), jnp.float32),
+                pltpu.VMEM((STEPS, BLOCK, 128), jnp.bfloat16),
+                pltpu.VMEM((STEPS, 128, BLOCK), jnp.bfloat16),
+            ],
+        ),
+        out_shape=[
+            jax.ShapeDtypeStruct((1024, 256), jnp.bfloat16),
+            jax.ShapeDtypeStruct((1024, 128), jnp.bfloat16),
+            jax.ShapeDtypeStruct((1024, 128), jnp.bfloat16),
+            jax.ShapeDtypeStruct((1024, 256), jnp.bfloat16),
+            jax.ShapeDtypeStruct((8, 1024), jnp.float32),
+        ],
+        compiler_params=pltpu.CompilerParams(vmem_limit_bytes=40 * 2**20),
+        name="forward",
+    )(start, gathered, weight, cosine, sine, start[None, :])
+
+
+def backward_kernel(
+    starts, grads, weight, heads, query_ref, key_ref, value_ref, inverse_ref, cosine, sine, start_ref,
+    grad_proj, grad_out, total, slope, dprob, dkey, dvalue, keys_t,
+):
+    i = pl.program_id(0)
+
+    @pl.when(i == 0)
+    def _():
+        dkey[...] = jnp.zeros_like(dkey)
+        dvalue[...] = jnp.zeros_like(dvalue)
+
+    heads_t = heads[...].astype(jnp.float32).T.astype(jnp.bfloat16)
+    for n in range(0, WIDTH, 512):
+        part = jnp.dot(heads_t, grads[:, n : n + 512], preferred_element_type=jnp.float32)
+
+        @pl.when(i == 0)
+        def _():
+            total[:, n : n + 512] = part
+
+        @pl.when((i > 0) & (i < STEPS - 1))
+        def _():
+            total[:, n : n + 512] += part
+
+        @pl.when(i == STEPS - 1)
+        def _():
+            grad_out[:, n : n + 512] = (total[:, n : n + 512] + part).astype(jnp.bfloat16)
+
+    grad_heads = lax.dot_general(
+        grads[...], weight[...], (((1,), (1,)), ((), ())), preferred_element_type=jnp.float32
+    ).astype(jnp.bfloat16)
+    own = pl.ds(i * BLOCK, BLOCK)
+    keys_t[i] = key_ref[own, :].astype(jnp.float32).T.astype(jnp.bfloat16)
+    start_row = start_ref[...]
+    query_row = lax.broadcasted_iota(jnp.int32, (1, BLOCK), 1) + i * BLOCK
+    first = starts[i * BLOCK] // BLOCK
+    head = [slice(h * 128, h * 128 + 128) for h in range(2)]
+    queries = [query_ref[own, head[h]] for h in range(2)]
+    grad = [grad_heads[:, head[h]] for h in range(2)]
+
+    def score(j, sums):
+        out = []
+        at = pl.ds(j * BLOCK, BLOCK)
+        for h in range(2):
+            soft, e = scored(key_ref[at, :], queries[h], j * BLOCK, start_row, query_row)
+            p = e * inverse_ref[h : h + 1, :]
+            dp = lax.dot_general(
+                value_ref[at, :], grad[h], (((1,), (1,)), ((), ())), preferred_element_type=jnp.float32
+            )
+            dvalue[at, :] += jnp.dot(p.astype(jnp.bfloat16), grad[h], preferred_element_type=jnp.float32)
+            out.append(sums[h] + jnp.sum(p * dp, axis=0, keepdims=True))
+            slope[h, j] = p * ((1.0 - soft * soft) * query_scale)
+            dprob[h, j] = dp
+        return tuple(out)
+
+    zero = jnp.zeros((1, BLOCK), jnp.float32)
+    sums = lax.fori_loop(first, i + 1, score, (zero, zero))
+
+    def mix(j, accs):
+        out = []
+        at = pl.ds(j * BLOCK, BLOCK)
+        for h in range(2):
+            ds = (slope[h, j] * (dprob[h, j] - sums[h])).astype(jnp.bfloat16)
+            dkey[at, :] += jnp.dot(ds, queries[h], preferred_element_type=jnp.float32)
+            out.append(accs[h] + jnp.dot(keys_t[j], ds, preferred_element_type=jnp.float32))
+        return tuple(out)
+
+    zero = jnp.zeros((128, BLOCK), jnp.float32)
+    accs = lax.fori_loop(first, i + 1, mix, (zero, zero))
+    for h in range(2):
+        grad_proj[own, head[h]] = turn(accs[h].T, cosine[own, :], -sine[own, :]).astype(jnp.bfloat16)
+
+    @pl.when(i == STEPS - 1)
+    def _():
+        grad_proj[:, 256:384] = turn(dkey[...], cosine[...], -sine[...]).astype(jnp.bfloat16)
+        grad_proj[:, 384:512] = dvalue[...].astype(jnp.bfloat16)
+
+
+def backward(grads, weight, heads, query, key, value, inverse, cosine, sine, start):
+    rows = lambda n: pl.BlockSpec((BLOCK, n), lambda i, s: (i, 0))
+    whole = lambda *shape: pl.BlockSpec(shape, lambda i, s: (0, 0))
+    return pl.pallas_call(
+        backward_kernel,
+        grid_spec=pltpu.PrefetchScalarGridSpec(
+            num_scalar_prefetch=1,
+            grid=(STEPS,),
+            in_specs=[
+                rows(WIDTH),
+                whole(256, WIDTH),
+                rows(256),
+                whole(1024, 256),
+                whole(1024, 128),
+                whole(1024, 128),
+                pl.BlockSpec((8, BLOCK), lambda i, s: (0, i)),
+                whole(1024, 128),
+                whole(1024, 128),
+                pl.BlockSpec((1, BLOCK), lambda i, s: (0, i)),
+            ],
+            out_specs=[whole(1024, 512), whole(256, WIDTH)],
+            scratch_shapes=[
+                pltpu.VMEM((256, WIDTH), jnp.float32),
+                pltpu.VMEM((2, STEPS, BLOCK, BLOCK), jnp.float32),
+                pltpu.VMEM((2, STEPS, BLOCK, BLOCK), jnp.float32),
+                pltpu.VMEM((1024, 128), jnp.float32),
+                pltpu.VMEM((1024, 128), jnp.float32),
+                pltpu.VMEM((STEPS, 128, BLOCK), jnp.bfloat16),
+            ],
+        ),
+        out_shape=[
+            jax.ShapeDtypeStruct((1024, 512), jnp.bfloat16),
+            jax.ShapeDtypeStruct((256, WIDTH), jnp.bfloat16),
+        ],
+        compiler_params=pltpu.CompilerParams(vmem_limit_bytes=50 * 2**20),
+        name="backward",
+    )(start, grads, weight, heads, query, key, value, inverse, cosine, sine, start[None, :])
+
+
+CHUNK = 512
+
+
+def weight_grad_kernel(grad_proj, x, out, turned, mixed):
+    @pl.when(pl.program_id(0) == 0)
+    def _():
+        turned[...] = grad_proj[...].astype(jnp.float32).T.astype(jnp.bfloat16)
+
+    for j in range(4):
+        part = jnp.dot(turned[j * 128 : j * 128 + 128, :], x[...], preferred_element_type=jnp.float32)
+        mixed[pl.ds(j, CHUNK, stride=4), :] = part.T
+    out[...] = mixed[...].astype(jnp.bfloat16)
+
+
+def weight_grad(grad_proj, gathered):
+    return pl.pallas_call(
+        weight_grad_kernel,
+        grid=(WIDTH // CHUNK,),
+        in_specs=[
+            pl.BlockSpec((1024, 512), lambda n: (0, 0)),
+            pl.BlockSpec((1024, CHUNK), lambda n: (0, n)),
+        ],
+        out_specs=pl.BlockSpec((4 * CHUNK, 128), lambda n: (n, 0)),
+        out_shape=jax.ShapeDtypeStruct((4 * WIDTH, 128), jnp.bfloat16),
+        scratch_shapes=[pltpu.VMEM((512, 1024), jnp.bfloat16), pltpu.VMEM((4 * CHUNK, 128), jnp.float32)],
+        compiler_params=pltpu.CompilerParams(vmem_limit_bytes=40 * 2**20),
+        name="weight_grad",
+    )(grad_proj, gathered)
 
 
 def nesterov(mean_delta, moment_part, params_part):
@@ -352,71 +556,25 @@
     group = lax.axis_index("group")
     gathered = gather_normed(tokens, pre_gain[None, :]).reshape(16 * ROWS, WIDTH)
     length, width = gathered.shape
-    key_heads, parts, head_dim = (qkv_weight.shape[1], qkv_weight.shape[2], qkv_weight.shape[3])
-    query_count = parts - 2
-    proj = jnp.dot(
-        gathered,
-        qkv_weight.reshape(width, key_heads * parts * head_dim),
-        preferred_element_type=jnp.float32,
+    cosine, sine = tables(length, 128)
+    cosine = jnp.concatenate([cosine, cosine], axis=1)
+    sine = jnp.concatenate([-sine, sine], axis=1)
+    start = jnp.sum((doc_ids[None, :] < doc_ids[:, None]).astype(jnp.int32), axis=1)
+    query, key, value, head_flat, inverse = forward(
+        gathered, qkv_weight.reshape(width, 512), cosine, sine, start
     )
-    proj = proj.reshape(length, key_heads, parts, head_dim)
-    cosine, sine = tables(length, head_dim)
-    cosine_four, sine_four = (cosine[:, None, None, :], sine[:, None, None, :])
-    cosine_three, sine_three = (cosine[:, None, :], sine[:, None, :])
-    queries = rotate(proj[:, :, :query_count], cosine_four, sine_four).astype(jnp.bfloat16)
-    keys = rotate(proj[:, :, query_count], cosine_three, sine_three).astype(jnp.bfloat16)
-    values = proj[:, :, query_count + 1].astype(jnp.bfloat16)
-    position = jnp.arange(length, dtype=jnp.int32)
-    allowed = (position[None, :] <= position[:, None]) & (doc_ids[None, :] == doc_ids[:, None])
-    qhead = jnp.transpose(queries, (1, 2, 0, 3))
-    khead = jnp.transpose(keys, (1, 0, 2))
-    vhead = jnp.transpose(values, (1, 0, 2))
-
-    def forward_group(query_set, keyed, valued):
-        return jax.vmap(attend, in_axes=(0, None, None, None))(query_set, keyed, valued, allowed)
-
-    result, probs, rounded, capped = jax.vmap(forward_group)(qhead, khead, vhead)
-    heads = jnp.transpose(result.astype(jnp.bfloat16), (2, 0, 1, 3))
-    head_flat = heads.reshape(length, key_heads * query_count * head_dim)
-    out_flat = out_weight.reshape(key_heads * query_count * head_dim, width)
+    out_flat = out_weight.reshape(256, width)
     share = lax.dynamic_slice_in_dim(head_flat.reshape(8, 2, 8, 8, 256), group, 1, axis=2)
     share = jnp.transpose(share[:, :, 0], (1, 0, 2, 3)).reshape(128, 256)
     own_tokens = lax.dynamic_slice_in_dim(tokens, group * 8, 8, axis=0).astype(jnp.float32)
     own_cotangent = lax.dynamic_slice_in_dim(cotangent, group * 8, 8, axis=0).astype(jnp.float32)
     output, grad_rows = middle(share, out_flat, own_tokens, own_cotangent, post_gain[None, :])
     grad_rows = grad_rows.reshape(length, width)
-    grad_out = lax.dot_general(
-        head_flat, grad_rows, (((0,), (0,)), ((), ())), preferred_element_type=jnp.float32
+    grad_proj, grad_out = backward(
+        grad_rows, out_flat, head_flat, query, key, value, inverse, cosine, sine, start
     )
-    grad_out = grad_out.astype(jnp.bfloat16).reshape(out_weight.shape)
-    grad_heads = lax.dot_general(
-        grad_rows, out_flat, (((1,), (1,)), ((), ())), preferred_element_type=jnp.float32
-    )
-    grad_heads = grad_heads.astype(jnp.bfloat16).reshape(length, key_heads, query_count, head_dim)
-    grad_heads = jnp.transpose(grad_heads, (1, 2, 0, 3))
-
-    def backward_group(query_set, keyed, valued, prob_set, round_set, cap_set, grad_set):
-        dquery, dkey, dvalue = jax.vmap(attend_back, in_axes=(0, None, None, 0, 0, 0, 0))(
-            query_set, keyed, valued, prob_set, round_set, cap_set, grad_set
-        )
-        return (dquery, jnp.sum(dkey, axis=0), jnp.sum(dvalue, axis=0))
-
-    dquery, dkey, dvalue = jax.vmap(backward_group)(
-        qhead, khead, vhead, probs, rounded, capped, grad_heads
-    )
-    dquery = unrotate(jnp.transpose(dquery, (2, 0, 1, 3)), cosine_four, sine_four)
-    dkey = unrotate(jnp.transpose(dkey, (1, 0, 2)), cosine_three, sine_three)
-    dvalue = jnp.transpose(dvalue, (1, 0, 2))
-    grad_proj = jnp.concatenate([dquery, dkey[:, :, None], dvalue[:, :, None]], axis=2).astype(
-        jnp.bfloat16
-    )
-    grad_qkv = lax.dot_general(
-        gathered,
-        grad_proj.reshape(length, key_heads * parts * head_dim),
-        (((0,), (0,)), ((), ())),
-        preferred_element_type=jnp.float32,
-    )
-    grad_qkv = grad_qkv.astype(jnp.bfloat16).reshape(qkv_weight.shape)
+    grad_out = grad_out.reshape(out_weight.shape)
+    grad_qkv = weight_grad(grad_proj, gathered).reshape(qkv_weight.shape)
     total = lax.psum(outer_delta[0], "group").astype(jnp.float32)
     new_momentum, new_fragment = nesterov(total / lax.axis_size("group"), momentum, fragment)
     return (output, grad_qkv, grad_out, new_momentum, new_fragment)

time: 250 us -> 224 us (0.90)
  matrix products: 71.8 us -> 0 us
  Pallas kernels: 120 us -> 174 us
  local copies, waits for them, and re-layouts: 29.3 us -> 24.2 us
  other arithmetic: 12.1 us -> 8.84 us
    dot_general x10 -> x0, matrix products: 71.8 us -> none  [the longest x1 15.1 us: attend_back(): dquery = jnp.dot(dscore, keyed, preferred_element_type=jnp.float32)]
    pallas_call x0 -> x3, Pallas kernels: none -> 52.3 us  [the longest x1 29.2 us: backward(): pl.pallas_call(backward_kernel, grid_spec=pltpu.PrefetchScalarGridSpec(nu...]
    dot_general x1 -> x0, local copies, waits for them, and re-layouts: 6.73 us -> none  [local(): jnp.dot(gathered, qkv_weight.reshape(width, key_heads * parts * head_dim)...]
    unnamed x49 -> x40, local copies, waits for them, and re-layouts: 16.8 us -> 23.4 us
    another operation x4 -> x0, other arithmetic: 3.66 us -> none
    transpose x3 -> x0, local copies, waits for them, and re-layouts: 2.86 us -> none  [the longest x1 2.01 us: local(): heads = jnp.transpose(result.astype(jnp.bfloat16), (2, 0, 1, 3))]
  transfers between devices with their start and end apart: 1 -> 1, of which waited for: 0 -> 0; matrix products, arithmetic and copies ran while one was open for 42% -> 5% of each run, Pallas kernels for 48% -> 78%
where the time goes in v2:
time: 224 us; the launch traced here: 222 us
  Pallas kernels  174 us (78%)
  local copies, waits for them, and re-layouts  24.2 us (11%)
  between operations  14.2 us (6%)
  other arithmetic  8.84 us (4%)
    pallas_call x1, Pallas kernels, middle(): pl.pallas_call(middle_kernel, out_shape=(jax.ShapeDtypeStruct((ROWS, WIDT...  67.4 us
    pallas_call x1, Pallas kernels, gather_normed(): pl.pallas_call(normed_kernel, out_shape=jax.ShapeDtypeStruct((16, ROWS, W...  54 us
    pallas_call x1, Pallas kernels, backward(): pl.pallas_call(backward_kernel, grid_spec=pltpu.PrefetchScalarGridSpec(nu...  29.2 us
    unnamed x40, local copies, waits for them, and re-layouts  23.4 us
    pallas_call x1, Pallas kernels, forward(): pl.pallas_call(forward_kernel, grid_spec=pltpu.PrefetchScalarGridSpec(num...  13.4 us
    pallas_call x1, Pallas kernels, weight_grad(): pl.pallas_call(weight_grad_kernel, grid=(WIDTH // CHUNK,), in_specs=[pl.B...  9.72 us
    sub x1, other arithmetic, nesterov(): return (moment_next, params_part - 0.7 * (mean_delta + 0.9 * moment_next))  4.92 us
  transfers between devices with their start and end apart: 1, of which 0 were waited for; matrix products, arithmetic and copies ran while one was open for 5% of the time, Pallas kernels for 78%

profile of v2, /device:TPU:1, one launch (start us, length us, event | category | flops | bytes accessed | tf_op | source)
XLA Modules:
  0.0 221.7 jit_solution(1549131237807754311)
XLA Ops:
  7.2 0.0 all-reduce.2.cloned.1.call-start
  7.2 0.7 all-reduce.2.cloned.1.call-update
  7.9 0.7 broadcast_in_dim.6.gain
  8.7 0.0 copy-start.5
  8.7 5.4 %copy.21 = bf16[576,8,4,128]{3,1,2,0:T(8,128)(2,1)} copy(bf16[576,8,4,128]{3,2,1,0:T(4,128)(2,1)} %bitcast.30) | data formatting | bytes 9437184
  14.1 0.0 copy-done.5
  14.1 54.0 %gather_normed.1 = bf16[16,64,4608]{2,1,0:T(8,128)(2,1)S(1)} custom-call(bf16[64,4608]{1,0:T(8,128)(2,1)S(1)} %copy-done.5, f32[1,4608]{1,0:T(1,128)S(1)} %broadcast_in_dim.6.gain), custom_call_target="tpu_custom_call" | custom-call | tf_op jit(solution)/shard_map/gather_normed/pallas_call | solution.py:167
  68.1 0.0 copy-start
  68.1 3.7 %copy-done = bf16[16,64,4608]{2,1,0:T(8,128)(2,1)} copy-done((bf16[16,64,4608]{2,1,0:T(8,128)(2,1)}, bf16[16,64,4608]{2,1,0:T(8,128)(2,1)S(1)}, u32[]{:S(2)}) %copy-start) | copy-done | bytes 9437208
  71.7 0.0 copy-start.18
  71.7 2.0 fusion.3
  73.7 0.3 pad_maximum_fusion
  74.0 0.0 copy-done.18
  74.0 0.6 convert_reduce_fusion.starts
  74.6 0.0 copy-start.2
  74.6 2.4 %copy-done.2 = bf16[576,8,4,128]{3,1,2,0:T(8,128)(2,1)S(1)} copy-done((bf16[576,8,4,128]{3,1,2,0:T(8,128)(2,1)S(1)}, bf16[576,8,4,128]{3,1,2,0:T(8,128)(2,1)}, u32[]{:S(2)}) %copy-start.2) | copy-done | bytes 4718616
  77.0 0.0 copy-start.17
  77.0 0.0 copy-start.4
  77.0 13.4 %forward.1 = (bf16[1024,256]{1,0:T(8,128)(2,1)S(1)}, bf16[1024,128]{1,0:T(8,128)(2,1)S(1)}, bf16[1024,128]{1,0:T(8,128)(2,1)S(1)}, bf16[1024,256]{1,0:T(8,128)(2,1)S(1)}, f32[8,1024]{1,0:T(8,128)S(1)}) custom-call(s32[1024]{0:T(1024)S(1)} %convert_reduce_fusion.starts, bf16[1024,4608]{1,0:T(8,128)(2,1)} %bitcast.20, bf16[4608,512]{1,0:T(8,128)(2,1)S(1)} %bitcast.22, ...), custom_call_target="tpu_custom_call" | custom-call | tf_op jit(solution)/shard_map/forward/pallas_call | solution.py:362
  90.4 0.0 copy-start.10
  90.4 0.8 copy-done.10
  91.2 0.0 copy-start.12
  91.2 0.7 copy-done.12
  91.9 0.0 copy-start.14
  91.9 0.7 copy-done.14
  92.6 0.0 copy-start.6
  92.6 0.8 copy-done.6
  93.4 0.0 copy-done.17
  93.5 0.0 copy-start.7
  93.5 0.0 copy-start.11
  93.5 0.0 copy-start.13
  93.5 0.0 copy-start.15
  93.5 1.1 dynamic-slice_convert_fusion
  94.6 0.0 copy-done.4
  94.6 67.4 %middle.1 = (bf16[64,4608]{1,0:T(8,128)(2,1)S(1)}, bf16[16,64,4608]{2,1,0:T(8,128)(2,1)S(1)}) custom-call(bf16[128,256]{1,0:T(8,128)(2,1)S(1)} %bitcast.27, bf16[256,4608]{1,0:T(8,128)(2,1)S(1)} %bitcast.25, f32[8,4608]{1,0:T(8,128)S(1)} %get-tuple-element.41.tokens, f32[8,4608]{1,0:T(8,128)S(1)} %get-tuple-element.40.cotangent, ...), custom_call_target="tpu_custom_call" | custom-call | tf_op jit(solution)/shard_map/middle/pallas_call | solution.py:260
  162.0 0.0 copy-start.3
  162.0 3.6 %copy-done.3 = bf16[16,64,4608]{2,1,0:T(8,128)(2,1)} copy-done((bf16[16,64,4608]{2,1,0:T(8,128)(2,1)}, bf16[16,64,4608]{2,1,0:T(8,128)(2,1)S(1)}, u32[]{:S(2)}) %copy-start.3) | copy-done | bytes 9437208
  165.6 0.0 copy-start.8
  165.6 0.8 copy-done.8
  166.5 0.0 copy-done.7
  166.5 0.0 copy-done.11
  166.5 0.0 copy-done.13
  166.5 0.0 copy-done.15
  166.5 29.2 %backward.1 = (bf16[1024,512]{1,0:T(8,128)(2,1)S(1)}, bf16[256,4608]{1,0:T(8,128)(2,1)}) custom-call(s32[1024]{0:T(1024)S(1)} %convert_reduce_fusion.starts, bf16[1024,4608]{1,0:T(8,128)(2,1)} %bitcast.23, bf16[256,4608]{1,0:T(8,128)(2,1)} %bitcast.24, bf16[1024,256]{1,0:T(8,128)(2,1)S(1)} %copy-done.7, bf16[1024,256]{1,0:T(8,128)(2,1)S(1)} %copy-done.11, ...), custom_call_target="tpu_custom_call" | custom-call | tf_op jit(solution)/shard_map/backward/pallas_call | solution.py:473
  195.7 0.0 copy-start.1
  195.7 3.7 %copy-done.1 = bf16[16,64,4608]{2,1,0:T(8,128)(2,1)S(1)} copy-done((bf16[16,64,4608]{2,1,0:T(8,128)(2,1)S(1)}, bf16[16,64,4608]{2,1,0:T(8,128)(2,1)}, u32[]{:S(2)}) %copy-start.1) | copy-done | bytes 9437208
  199.4 0.0 copy-start.16
  199.4 9.7 %weight_grad.1 = bf16[18432,128]{1,0:T(8,128)(2,1)} custom-call(bf16[1024,512]{1,0:T(8,128)(2,1)S(1)} %get-tuple-element.21.grad_proj, bf16[1024,4608]{1,0:T(8,128)(2,1)S(1)} %bitcast.21), custom_call_target="tpu_custom_call" | custom-call | tf_op jit(solution)/shard_map/weight_grad/pallas_call | solution.py:524
  209.1 0.0 copy-start.9
  209.1 0.0 all-reduce.2.cloned.1.call-done
  209.1 0.0 copy-done.16
  209.1 4.9 %multiply_subtract_fusion = (f32[128,4608]{1,0:T(8,128)}, f32[128,4608]{1,0:T(8,128)}) fusion(f32[128,4608]{1,0:T(8,128)S(1)} %copy-done.16, bf16[128,4608]{1,0:T(8,128)(2,1)} %all-reduce.2.cloned.1.call-done, f32[128,4608]{1,0:T(8,128)} %param.18), kind=kLoop, calls=%fused_computation.2 | loop fusion | flops 4718592 | bytes 10616832 | tf_op jit(solution)/shard_map/sub | solution.py:541
  214.0 0.0 copy-done.9
  214.0 0.8 copy.25
  (4 shorter events, 0.0 us)
Async XLA Ops:
  7.2 202.0 %all-reduce.2.cloned.1.call-start = ((), (), s32[]{:S(2)}) async-start(), calls=%async_computation | async-start | bytes 2359296 | tf_op jit(solution)/shard_map/psum | solution.py:578
  8.7 5.4 %copy-start.5 = (bf16[64,4608]{1,0:T(8,128)(2,1)S(1)}, bf16[64,4608]{1,0:T(8,128)(2,1)}, u32[]{:S(2)}) copy-start(bf16[64,4608]{1,0:T(8,128)(2,1)} %tokens.1) | copy-start | bytes 1769476
  68.1 3.7 %copy-start = (bf16[16,64,4608]{2,1,0:T(8,128)(2,1)}, bf16[16,64,4608]{2,1,0:T(8,128)(2,1)S(1)}, u32[]{:S(2)}) copy-start(bf16[16,64,4608]{2,1,0:T(8,128)(2,1)S(1)} %gather_normed.1) | copy-start | bytes 28311556
  71.7 2.3 %copy-start.18 = (s32[1024]{0:T(1024)S(1)}, s32[1024]{0:T(1024)}, u32[]{:S(2)}) copy-start(s32[1024]{0:T(1024)} %param.15) | copy-start | bytes 12292
  74.6 2.4 %copy-start.2 = (bf16[576,8,4,128]{3,1,2,0:T(8,128)(2,1)S(1)}, bf16[576,8,4,128]{3,1,2,0:T(8,128)(2,1)}, u32[]{:S(2)}) copy-start(bf16[576,8,4,128]{3,1,2,0:T(8,128)(2,1)} %copy.21) | copy-start | bytes 14155780
  77.0 16.4 %copy-start.17 = (f32[4608]{0:T(1024)S(1)}, f32[4608]{0:T(1024)}, u32[]{:S(2)}) copy-start(f32[4608]{0:T(1024)} %param.12) | copy-start | bytes 55300
  77.0 17.5 %copy-start.4 = (bf16[1,2,128,4608]{3,2,1,0:T(8,128)(2,1)S(1)}, bf16[1,2,128,4608]{3,2,1,0:T(8,128)(2,1)}, u32[]{:S(2)}) copy-start(bf16[1,2,128,4608]{3,2,1,0:T(8,128)(2,1)} %param.14) | copy-start | bytes 7077892
  90.4 0.8 copy-start.10
  91.2 0.7 copy-start.12
  91.9 0.7 copy-start.14
  92.6 0.8 copy-start.6
  93.5 73.0 %copy-start.7 = (bf16[1024,256]{1,0:T(8,128)(2,1)S(1)}, bf16[1024,256]{1,0:T(8,128)(2,1)}, u32[]{:S(2)}) copy-start(bf16[1024,256]{1,0:T(8,128)(2,1)} %copy-done.6) | copy-start | bytes 1572868
  93.5 73.0 %copy-start.11 = (bf16[1024,256]{1,0:T(8,128)(2,1)S(1)}, bf16[1024,256]{1,0:T(8,128)(2,1)}, u32[]{:S(2)}) copy-start(bf16[1024,256]{1,0:T(8,128)(2,1)} %copy-done.10) | copy-start | bytes 1572868
  93.5 73.0 %copy-start.13 = (bf16[1024,128]{1,0:T(8,128)(2,1)S(1)}, bf16[1024,128]{1,0:T(8,128)(2,1)}, u32[]{:S(2)}) copy-start(bf16[1024,128]{1,0:T(8,128)(2,1)} %copy-done.12) | copy-start | bytes 786436
  93.5 73.0 %copy-start.15 = (bf16[1024,128]{1,0:T(8,128)(2,1)S(1)}, bf16[1024,128]{1,0:T(8,128)(2,1)}, u32[]{:S(2)}) copy-start(bf16[1024,128]{1,0:T(8,128)(2,1)} %copy-done.14) | copy-start | bytes 786436
  162.0 3.6 %copy-start.3 = (bf16[16,64,4608]{2,1,0:T(8,128)(2,1)}, bf16[16,64,4608]{2,1,0:T(8,128)(2,1)S(1)}, u32[]{:S(2)}) copy-start(bf16[16,64,4608]{2,1,0:T(8,128)(2,1)S(1)} %get-tuple-element.16) | copy-start | bytes 28311556
  165.6 0.8 copy-start.8
  195.7 3.7 %copy-start.1 = (bf16[16,64,4608]{2,1,0:T(8,128)(2,1)S(1)}, bf16[16,64,4608]{2,1,0:T(8,128)(2,1)}, u32[]{:S(2)}) copy-start(bf16[16,64,4608]{2,1,0:T(8,128)(2,1)} %copy-done) | copy-start | bytes 28311556
  199.4 9.7 %copy-start.16 = (f32[128,4608]{1,0:T(8,128)S(1)}, f32[128,4608]{1,0:T(8,128)}, u32[]{:S(2)}) copy-start(f32[128,4608]{1,0:T(8,128)} %param.19) | copy-start | bytes 7077892
  209.1 4.9 %copy-start.9 = (bf16[64,4608]{1,0:T(8,128)(2,1)S(1)}, bf16[64,4608]{1,0:T(8,128)(2,1)}, u32[]{:S(2)}) copy-start(bf16[64,4608]{1,0:T(8,128)(2,1)} %copy-done.8) | copy-start | bytes 1769476
Sparse Core Ops, SparseCore 0:
  10.5 96.4 all-reduce.1

commit v3 on v2

v3 whole, which is shorter than its diff:
```python
import functools

import jax
import jax.numpy as jnp
import numpy as np
from jax import lax
from jax.experimental import pallas as pl
from jax.experimental.pallas import tpu as pltpu
from jax.sharding import PartitionSpec as P

softcap = 50.0
query_scale = 1.0 / 12.0
MESH = pl.DeviceIdType.MESH
WIDTH = 4608
HALF = WIDTH // 2
ROWS = 64
N1, N2, NQ = 10 * 128, 10 * 128, 4 * 128
NP = N1 + N2


def place():
    group, fsdp = lax.axis_index("group"), lax.axis_index("fsdp")
    return group // 2, group % 2, fsdp // 8, (fsdp // 2) % 4, fsdp % 2


def device(x, zh, zl, y, c):
    return (x * 2 + zh, (zl * 4 + y) * 2 + c)


class Sender:
    def __init__(self, sems):
        self.sems, self.copies = sems, []

    def __call__(self, src, dst, recv, to):
        copy = pltpu.make_async_remote_copy(
            src_ref=src,
            dst_ref=dst,
            send_sem=self.sems.at[len(self.copies)],
            recv_sem=recv,
            device_id=to,
            device_id_type=MESH,
        )
        copy.start()
        self.copies.append(copy)

    def arrived(self, ref, recv, to):
        pltpu.make_async_remote_copy(
            src_ref=ref,
            dst_ref=ref,
            send_sem=self.sems.at[0],
            recv_sem=recv,
            device_id=to,
            device_id_type=MESH,
        ).wait_recv()

    def finish(self):
        for copy in self.copies:
            copy.wait_send()


SPREAD_SENDS = 69


def spread(own, full, send, piece_sems, pair_sems, local_sem, work=iter(()), later=None):
    x, zh, zl, y, c = place()
    k, kz = zl * 4 + y, (1 - zl) * 4 + y
    near_k, near_kz = ([b * 4 + (y + s) % 4 for s in (1, 3, 2)] for b in (zl, 1 - zl))
    to_sib = device(x, zh, zl, y, 1 - c)
    to_z = device(x, zh, 1 - zl, y, c)
    to_y = [device(x, zh, zl, (y + s) % 4, c) for s in (1, 3)]
    to_x = [device((x + s) % 4, zh, zl, y, c) for s in (1, 3)]
    quarters = [x, (x + 1) % 4, (x + 3) % 4, (x + 2) % 4]
    starts = {"a": 0, "b": N1} | {w: NP + quarters[w] * NQ for w in range(4)}
    sizes = {"a": N1, "b": N2} | {w: NQ for w in range(4)}
    index = {"a": 0, "b": 1} | {w: 2 + quarters[w] for w in range(4)}

    def cols(t, half):
        lo, size = starts[t], sizes[t]
        if half is not None:
            size = size // 2
            lo = lo + half * size
        if not isinstance(lo, int):
            lo = pl.multiple_of(lo, 128)
        return pl.ds(lo, size)

    def push(kk, t, to, half=None):
        at = cols(t, half)
        src = own.at[:, at] if kk is k else full.at[2 * kk + c, :, at]
        send(src, full.at[2 * kk + c, :, at], piece_sems.at[half or 0, index[t], kk], to)

    def here(kk, t, half=None):
        next(work, None)
        send.arrived(full.at[2 * kk + c, :, cols(t, half)], piece_sems.at[half or 0, index[t], kk], to_sib)

    def pair(kk, lo, size, slot):
        ref = full.at[2 * kk + c, :, pl.ds(lo, size)]
        send(ref, ref, pair_sems.at[kk, slot], to_sib)

    def ring(kk, t, links, side):
        push(kk, t, links[1 - side], side)

    def both(kk, t, links):
        for to in links:
            push(kk, t, to)

    keep = pltpu.make_async_copy(own, full.at[2 * k + c], local_sem)
    keep.start()
    push(k, 0, to_z)
    both(k, 0, to_y)
    push(k, "a", to_z)
    both(k, "b", to_y)
    push(k, "b", to_z)
    both(k, "a", to_y)
    send(own, full.at[2 * k + c], pair_sems.at[k, 0], to_sib)

    here(kz, 0)
    both(kz, 0, to_y)
    both(kz, 0, to_x)
    for side in range(2):
        kk = near_k[side]
        here(kk, 0)
        ring(kk, 0, to_y, side)
        both(kk, 0, to_x)
    here(kz, "a")
    both(kz, "a", to_y)
    for side in range(2):
        kk = near_k[side]
        here(kk, "b")
        push(kk, "b", to_z)
        ring(kk, "b", to_y, side)
    for side in range(2):
        kk = near_kz[side]
        here(kk, 0)
        ring(kk, 0, to_y, side)
        both(kk, 0, to_x)
    here(near_k[2], 0, 0)
    here(near_k[2], 0, 1)
    both(near_k[2], 0, to_x)
    for side in range(2):
        kk = near_k[side]
        here(kk, "a")
        ring(kk, "a", to_y, side)
        pair(kk, 0, NP, 0)
    here(near_k[2], "b", 0)
    here(near_k[2], "b", 1)
    push(near_k[2], "b", to_z)
    here(near_kz[2], 0, 0)
    here(near_kz[2], 0, 1)
    both(near_kz[2], 0, to_x)
    for side in range(2):
        here(near_kz[side], "a")
        ring(near_kz[side], "a", to_y, side)
    others = [kz, near_k[0], near_k[1], near_kz[0], near_kz[1], near_k[2], near_kz[2]]
    for kk in others[:5]:
        for side in range(2):
            here(kk, 1 + side)
            ring(kk, 1 + side, to_x, side)
    here(kz, "b")
    pair(kz, 0, NP, 0)
    for kk in others[5:]:
        for side in range(2):
            here(kk, 1 + side)
            ring(kk, 1 + side, to_x, side)
    if later is not None:
        later()
    here(near_k[2], "a", 0)
    here(near_k[2], "a", 1)
    pair(near_k[2], 0, NP, 0)
    for side in range(2):
        here(near_kz[side], "b")
        pair(near_kz[side], 0, NP, 0)
    for kk in others[:5]:
        here(kk, 3, 0)
        here(kk, 3, 1)
        pair(kk, NP, 4 * NQ, 1)
    here(near_kz[2], "a", 0)
    here(near_kz[2], "a", 1)
    here(near_kz[2], "b")
    pair(near_kz[2], 0, NP, 0)
    for kk in others[5:]:
        here(kk, 3, 0)
        here(kk, 3, 1)
        pair(kk, NP, 4 * NQ, 1)
    for _ in work:
        pass
    send.arrived(full.at[2 * k + 1 - c], pair_sems.at[k, 0], to_sib)
    for kk in others:
        send.arrived(full.at[2 * kk + 1 - c, :, pl.ds(0, NP)], pair_sems.at[kk, 0], to_sib)
        send.arrived(full.at[2 * kk + 1 - c, :, pl.ds(NP, 4 * NQ)], pair_sems.at[kk, 1], to_sib)
    keep.wait()


def near():
    x, zh, zl, y, c = place()
    out = [device(x, zh, zl, y, 1 - c), device(x, zh, 1 - zl, y, c)]
    out += [device(x, zh, zl, (y + s) % 4, c) for s in (1, 3)]
    return out + [device((x + s) % 4, zh, zl, y, c) for s in (1, 3)]


def greet(devices):
    barrier = pltpu.get_barrier_semaphore()
    for to in devices:
        pl.semaphore_signal(barrier, inc=1, device_id=to, device_id_type=MESH)


def met(devices):
    pl.semaphore_wait(pltpu.get_barrier_semaphore(), len(devices))


PARTS = 8
PART = WIDTH // PARTS


def weight_parts(weight, wide, rough, mixed, flat, in_sems, out_sems):
    def load(n):
        return pltpu.make_async_copy(weight.at[pl.ds(4 * PART * n, 4 * PART), :], rough.at[n % 2], in_sems.at[n])

    def store(n):
        return pltpu.make_async_copy(flat.at[n % 2], wide.at[pl.ds(PART * n, PART), :], out_sems.at[n])

    load(0).start()
    for n in range(PARTS):
        if n + 1 < PARTS:
            load(n + 1).start()
        yield
        load(n).wait()
        mixed[...] = rough[n % 2].astype(jnp.float32)
        if n >= 2:
            store(n - 2).wait()
        for j in range(4):
            flat[n % 2, :, j * 128 : j * 128 + 128] = mixed[pl.ds(j, PART, stride=4), :].astype(jnp.bfloat16)
        store(n).start()
    store(PARTS - 2).wait()
    store(PARTS - 1).wait()


def normed_kernel(
    tokens, gain, weight, full, wide, own, rough, mixed, flat,
    send_sems, piece_sems, pair_sems, local_sem, in_sems, out_sems,
):
    work = weight_parts(weight, wide, rough, mixed, flat, in_sems, out_sems)
    next(work)
    greet(near())
    values = tokens[...].astype(jnp.float32)
    scale = lax.rsqrt(jnp.mean(values * values, axis=-1, keepdims=True) + 1e-06)
    own[...] = (values * scale * gain[...]).astype(jnp.bfloat16)
    met(near())
    send = Sender(send_sems)
    spread(own, full, send, piece_sems, pair_sems, local_sem, work)
    send.finish()


def gather_normed(tokens, gain, weight):
    vmem = pl.BlockSpec(memory_space=pltpu.VMEM)
    return pl.pallas_call(
        normed_kernel,
        out_shape=(
            jax.ShapeDtypeStruct((16, ROWS, WIDTH), jnp.bfloat16),
            jax.ShapeDtypeStruct((WIDTH, 512), jnp.bfloat16),
        ),
        in_specs=[vmem, vmem, pl.BlockSpec(memory_space=pl.ANY)],
        out_specs=(pl.BlockSpec(memory_space=pl.ANY), pl.BlockSpec(memory_space=pl.ANY)),
        scratch_shapes=[
            pltpu.VMEM((ROWS, WIDTH), jnp.bfloat16),
            pltpu.VMEM((2, 4 * PART, 128), jnp.bfloat16),
            pltpu.VMEM((4 * PART, 128), jnp.float32),
            pltpu.VMEM((2, PART, 512), jnp.bfloat16),
            pltpu.SemaphoreType.DMA((SPREAD_SENDS,)),
            pltpu.SemaphoreType.DMA((2, 6, 8)),
            pltpu.SemaphoreType.DMA((8, 2)),
            pltpu.SemaphoreType.DMA,
            pltpu.SemaphoreType.DMA((PARTS,)),
            pltpu.SemaphoreType.DMA((PARTS,)),
        ],
        compiler_params=pltpu.CompilerParams(
            collective_id=0, has_side_effects=True, vmem_limit_bytes=60 * 2**20
        ),
        name="gather_normed",
    )(tokens, gain, weight)


def stacked(rows):
    return jnp.concatenate([rows[:, :HALF], rows[:, HALF:]], axis=0)


def unstacked(rows):
    return jnp.concatenate([rows[:8], rows[8:]], axis=1)


def middle_kernel(
    heads, weight, tokens, cotangent, gain, output, full,
    partial, received, mate, total, mine, group_in, own,
    send_sems, mate_sem, part_sems, group_sems, piece_sems, pair_sems, local_sem,
):
    x, zh, zl, y, c = place()
    k, g = zl * 4 + y, x * 2 + zh
    sib = device(x, zh, zl, y, 1 - c)
    chips = [(a, b) for a in range(2) for b in range(4)][1:]
    fellows = [((zl + a) % 2, (y + b) % 4) for a, b in chips]
    to_fellows = [device(x, zh, a, b, c) for a, b in fellows]
    kin = [((x + b) % 4, (zh + a) % 2) for a, b in chips]
    to_kin = [device(a, b, zl, y, c) for a, b in kin]
    greet([sib] + to_fellows + to_kin)
    for core in range(2):
        left = jnp.dot(heads[pl.ds(core * 64, 64)], weight[:, pl.ds(0, HALF)], preferred_element_type=jnp.float32)
        right = jnp.dot(heads[pl.ds(core * 64, 64)], weight[:, pl.ds(HALF, HALF)], preferred_element_type=jnp.float32)
        for kk in range(8):
            both = jnp.concatenate([left[kk * 8 : kk * 8 + 8], right[kk * 8 : kk * 8 + 8]], axis=0)
            partial[core, kk] = both.astype(jnp.bfloat16)
    met([sib] + to_fellows + to_kin)
    send = Sender(send_sems)
    send(partial.at[1 - c], mate, mate_sem, sib)
    send.arrived(mate, mate_sem, sib)
    for kk in range(8):
        total[kk] = (partial[c, kk].astype(jnp.float32) + mate[kk].astype(jnp.float32)).astype(jnp.bfloat16)
    for (a, b), to in zip(fellows, to_fellows):
        send(total.at[a * 4 + b], received.at[k], part_sems.at[k], to)
    both = partial[c, k].astype(jnp.float32) + mate[k].astype(jnp.float32)
    for a, b in fellows:
        kk = a * 4 + b
        send.arrived(received.at[kk], part_sems.at[kk], sib)
        both = both + received[kk].astype(jnp.float32)
    attn = unstacked(both)
    scale = lax.rsqrt(jnp.mean(attn * attn, axis=-1, keepdims=True) + 1e-06)
    normal = attn * scale
    out = tokens[...] + normal * gain[...]
    dnorm = cotangent[...] * gain[...]
    grad = scale * (dnorm - normal * jnp.mean(dnorm * normal, axis=-1, keepdims=True))
    mine[0] = stacked(grad).astype(jnp.bfloat16)
    mine[1] = stacked(out).astype(jnp.bfloat16)
    for to in to_kin:
        send(mine.at[0], group_in.at[0, g], group_sems.at[0, g], to)

    def later():
        for to in to_kin:
            send(mine.at[1], group_in.at[1, g], group_sems.at[1, g], to)

    group_in[0, g] = mine[0]
    group_in[1, g] = mine[1]
    for a, b in kin:
        gg = a * 2 + b
        send.arrived(group_in.at[0, gg], group_sems.at[0, gg], sib)
    for gg in range(0, 8, 2):
        first = unstacked(group_in[0, gg].astype(jnp.float32))
        second = unstacked(group_in[0, gg + 1].astype(jnp.float32))
        own[pl.ds(gg * 8, 16), :] = jnp.concatenate([first, second], axis=0).astype(jnp.bfloat16)
    spread(own, full, send, piece_sems, pair_sems, local_sem, later=later)
    for a, b in kin:
        gg = a * 2 + b
        send.arrived(group_in.at[1, gg], group_sems.at[1, gg], sib)
    for gg in range(0, 8, 2):
        first = unstacked(group_in[1, gg].astype(jnp.float32))
        second = unstacked(group_in[1, gg + 1].astype(jnp.float32))
        output[pl.ds(gg * 8, 16), :] = jnp.concatenate([first, second], axis=0).astype(jnp.bfloat16)
    send.finish()


def middle(heads, weight, tokens, cotangent, gain):
    vmem = pl.BlockSpec(memory_space=pltpu.VMEM)
    return pl.pallas_call(
        middle_kernel,
        out_shape=(
            jax.ShapeDtypeStruct((ROWS, WIDTH), jnp.bfloat16),
            jax.ShapeDtypeStruct((16, ROWS, WIDTH), jnp.bfloat16),
        ),
        in_specs=[vmem] * 5,
        out_specs=(vmem, pl.BlockSpec(memory_space=pl.ANY)),
        scratch_shapes=[
            pltpu.VMEM((2, 8, 16, HALF), jnp.bfloat16),
            pltpu.VMEM((8, 16, HALF), jnp.bfloat16),
            pltpu.VMEM((8, 16, HALF), jnp.bfloat16),
            pltpu.VMEM((8, 16, HALF), jnp.bfloat16),
            pltpu.VMEM((2, 16, HALF), jnp.bfloat16),
            pltpu.VMEM((2, 8, 16, HALF), jnp.bfloat16),
            pltpu.VMEM((ROWS, WIDTH), jnp.bfloat16),
            pltpu.SemaphoreType.DMA((1 + 7 + 14 + SPREAD_SENDS,)),
            pltpu.SemaphoreType.DMA,
            pltpu.SemaphoreType.DMA((8,)),
            pltpu.SemaphoreType.DMA((2, 8)),
            pltpu.SemaphoreType.DMA((2, 6, 8)),
            pltpu.SemaphoreType.DMA((8, 2)),
            pltpu.SemaphoreType.DMA,
        ],
        compiler_params=pltpu.CompilerParams(
            collective_id=1, has_side_effects=True, vmem_limit_bytes=60 * 2**20
        ),
        name="middle",
    )(heads, weight, tokens, cotangent, gain)


def tables(length, width):
    half = width // 2
    positions = np.arange(length, dtype=np.float32)[:, None]
    freqs = np.power(np.float32(10000.0), -(np.float32(2.0) * np.arange(half, dtype=np.float32) / np.float32(width)))
    angle = positions * freqs[None, :].astype(np.float32)
    cosine, sine = np.cos(angle), np.sin(angle)
    return (
        jnp.asarray(np.concatenate([cosine, cosine], axis=1)),
        jnp.asarray(np.concatenate([-sine, sine], axis=1)),
    )


BLOCK = 256
STEPS = 4


def turn(values, cosine, sine):
    return values * cosine + pltpu.roll(values, 64, 1) * sine


def scored(keys, queries, first_key, start_row, query_row):
    raw = lax.dot_general(keys, queries, (((1,), (1,)), ((), ())), preferred_element_type=jnp.float32)
    soft = jnp.tanh(raw * (query_scale / softcap))
    row = lax.broadcasted_iota(jnp.int32, raw.shape, 0) + first_key
    allowed = (row >= start_row) & (row <= query_row)
    return soft, jnp.where(allowed, jnp.exp(softcap * soft), 0.0)


def forward_kernel(
    starts, x, weight, cosine, sine, start_ref, query_ref, key_ref, value_ref, heads_ref, sums_ref, keep, keys, values_t
):
    i = pl.program_id(0)
    proj = jnp.dot(x[...], weight[...], preferred_element_type=jnp.float32)
    queries = [turn(proj[:, h * 128 : h * 128 + 128], cosine[...], sine[...]).astype(jnp.bfloat16) for h in range(2)]
    key = turn(proj[:, 256:384], cosine[...], sine[...]).astype(jnp.bfloat16)
    value = proj[:, 384:512]
    query_ref[:, :128] = queries[0]
    query_ref[:, 128:] = queries[1]
    key_ref[...] = key
    value_ref[...] = value.astype(jnp.bfloat16)
    keys[i] = key
    values_t[i] = value.T.astype(jnp.bfloat16)
    start_row = start_ref[...]
    query_row = lax.broadcasted_iota(jnp.int32, (1, BLOCK), 1) + i * BLOCK
    first = starts[i * BLOCK] // BLOCK

    def score(j, sums):
        out = []
        for h in range(2):
            _, e = scored(keys[j], queries[h], j * BLOCK, start_row, query_row)
            keep[h, j] = e
            out.append(sums[h] + jnp.sum(e, axis=0, keepdims=True))
        return tuple(out)

    zero = jnp.zeros((1, BLOCK), jnp.float32)
    sums = lax.fori_loop(first, i + 1, score, (zero, zero))
    inverse = [1.0 / s for s in sums]
    sums_ref[0:1, :] = inverse[0]
    sums_ref[1:2, :] = inverse[1]

    def mix(j, accs):
        out = []
        for h in range(2):
            p = (keep[h, j] * inverse[h]).astype(jnp.bfloat16)
            out.append(accs[h] + jnp.dot(values_t[j], p, preferred_element_type=jnp.float32))
        return tuple(out)

    zero = jnp.zeros((128, BLOCK), jnp.float32)
    accs = lax.fori_loop(first, i + 1, mix, (zero, zero))
    for h in range(2):
        heads_ref[:, h * 128 : h * 128 + 128] = accs[h].T.astype(jnp.bfloat16)


def forward(gathered, weight, cosine, sine, start):
    rows = lambda n: pl.BlockSpec((BLOCK, n), lambda i, s: (i, 0))
    return pl.pallas_call(
        forward_kernel,
        grid_spec=pltpu.PrefetchScalarGridSpec(
            num_scalar_prefetch=1,
            grid=(STEPS,),
            in_specs=[
                rows(WIDTH),
                pl.BlockSpec((WIDTH, 512), lambda i, s: (0, 0)),
                rows(128),
                rows(128),
                pl.BlockSpec((1, BLOCK), lambda i, s: (0, i)),
            ],
            out_specs=[rows(256), rows(128), rows(128), rows(256), pl.BlockSpec((8, BLOCK), lambda i, s: (0, i))],
            scratch_shapes=[
                pltpu.VMEM((2, STEPS, BLOCK, BLOCK), jnp.float32),
                pltpu.VMEM((STEPS, BLOCK, 128), jnp.bfloat16),
                pltpu.VMEM((STEPS, 128, BLOCK), jnp.bfloat16),
            ],
        ),
        out_shape=[
            jax.ShapeDtypeStruct((1024, 256), jnp.bfloat16),
            jax.ShapeDtypeStruct((1024, 128), jnp.bfloat16),
            jax.ShapeDtypeStruct((1024, 128), jnp.bfloat16),
            jax.ShapeDtypeStruct((1024, 256), jnp.bfloat16),
            jax.ShapeDtypeStruct((8, 1024), jnp.float32),
        ],
        compiler_params=pltpu.CompilerParams(vmem_limit_bytes=60 * 2**20),
        name="forward",
    )(start, gathered, weight, cosine, sine, start[None, :])


CHUNK = 512
CHUNKS = WIDTH // CHUNK


def backward_kernel(
    starts, grads_hbm, x_hbm, weight, heads, query_ref, key_ref, value_ref, inverse_ref, cosine, sine, start_ref,
    qkv_out, out_out, grads, x, slope, dprob, dkey, dvalue, keys_t, grad_proj, turned, heads_t, mixed, sems,
):
    i = pl.program_id(0)

    def load(n, which):
        rows = pl.ds(n * BLOCK, BLOCK)
        src, dst = ((grads_hbm, grads), (x_hbm, x))[which]
        return pltpu.make_async_copy(src.at[rows, :], dst.at[rows, :], sems.at[which, n])

    @pl.when(i == 0)
    def _():
        for which in range(2):
            for n in range(STEPS):
                load(n, which).start()
        dkey[...] = jnp.zeros_like(dkey)
        dvalue[...] = jnp.zeros_like(dvalue)

    head = [slice(h * 128, h * 128 + 128) for h in range(2)]

    @pl.when(i < STEPS)
    def _():
        load(i, 0).wait()
        own = pl.ds(pl.multiple_of(i * BLOCK, BLOCK), BLOCK)
        grad_heads = lax.dot_general(
            grads[own, :], weight[...], (((1,), (1,)), ((), ())), preferred_element_type=jnp.float32
        ).astype(jnp.bfloat16)
        keys_t[i] = key_ref[own, :].astype(jnp.float32).T.astype(jnp.bfloat16)
        start_row = start_ref[...]
        query_row = lax.broadcasted_iota(jnp.int32, (1, BLOCK), 1) + i * BLOCK
        first = starts[i * BLOCK] // BLOCK
        queries = [query_ref[own, head[h]] for h in range(2)]
        grad = [grad_heads[:, head[h]] for h in range(2)]

        def score(j, sums):
            out = []
            at = pl.ds(pl.multiple_of(j * BLOCK, BLOCK), BLOCK)
            for h in range(2):
                soft, e = scored(key_ref[at, :], queries[h], j * BLOCK, start_row, query_row)
                p = e * inverse_ref[h : h + 1, :]
                dp = lax.dot_general(
                    value_ref[at, :], grad[h], (((1,), (1,)), ((), ())), preferred_element_type=jnp.float32
                )
                dvalue[at, :] += jnp.dot(p.astype(jnp.bfloat16), grad[h], preferred_element_type=jnp.float32)
                out.append(sums[h] + jnp.sum(p * dp, axis=0, keepdims=True))
                slope[h, j] = p * ((1.0 - soft * soft) * query_scale)
                dprob[h, j] = dp
            return tuple(out)

        zero = jnp.zeros((1, BLOCK), jnp.float32)
        sums = lax.fori_loop(first, i + 1, score, (zero, zero))

        def mix(j, accs):
            out = []
            at = pl.ds(pl.multiple_of(j * BLOCK, BLOCK), BLOCK)
            for h in range(2):
                ds = (slope[h, j] * (dprob[h, j] - sums[h])).astype(jnp.bfloat16)
                dkey[at, :] += jnp.dot(ds, queries[h], preferred_element_type=jnp.float32)
                out.append(accs[h] + jnp.dot(keys_t[j], ds, preferred_element_type=jnp.float32))
            return tuple(out)

        zero = jnp.zeros((128, BLOCK), jnp.float32)
        accs = lax.fori_loop(first, i + 1, mix, (zero, zero))
        for h in range(2):
            grad_proj[own, head[h]] = turn(accs[h].T, cosine[own, :], -sine[own, :])

    @pl.when(i == STEPS)
    def _():
        grad_proj[:, 256:384] = turn(dkey[...], cosine[...], -sine[...])
        grad_proj[:, 384:512] = dvalue[...]
        turned[...] = grad_proj[...].T.astype(jnp.bfloat16)
        heads_t[...] = heads[...].astype(jnp.float32).T.astype(jnp.bfloat16)
        for n in range(STEPS):
            load(n, 1).wait()

    @pl.when(i >= STEPS)
    def _():
        at = pl.ds(pl.multiple_of((i - STEPS) * CHUNK, CHUNK), CHUNK)
        for j in range(4):
            part = jnp.dot(turned[j * 128 : j * 128 + 128, :], x[:, at], preferred_element_type=jnp.float32)
            mixed[pl.ds(j, CHUNK, stride=4), :] = part.T
        out_out[...] = jnp.dot(heads_t[...], grads[:, at], preferred_element_type=jnp.float32).astype(jnp.bfloat16)
        qkv_out[...] = mixed[...].astype(jnp.bfloat16)


def backward(grads, gathered, weight, heads, query, key, value, inverse, cosine, sine, start):
    whole = lambda *shape: pl.BlockSpec(shape, lambda i, s: (0, 0), pipeline_mode=pl.Buffered(1))
    place_of = lambda i: jnp.minimum(i, STEPS - 1)
    chunk_of = lambda i: jnp.maximum(i - STEPS, 0)
    hbm = pl.BlockSpec(memory_space=pl.ANY)
    return pl.pallas_call(
        backward_kernel,
        grid_spec=pltpu.PrefetchScalarGridSpec(
            num_scalar_prefetch=1,
            grid=(STEPS + CHUNKS,),
            in_specs=[
                hbm,
                hbm,
                whole(256, WIDTH),
                whole(1024, 256),
                whole(1024, 256),
                whole(1024, 128),
                whole(1024, 128),
                pl.BlockSpec((8, BLOCK), lambda i, s: (0, place_of(i))),
                whole(1024, 128),
                whole(1024, 128),
                pl.BlockSpec((1, BLOCK), lambda i, s: (0, place_of(i))),
            ],
            out_specs=[
                pl.BlockSpec((4 * CHUNK, 128), lambda i, s: (chunk_of(i), 0)),
                pl.BlockSpec((256, CHUNK), lambda i, s: (0, chunk_of(i))),
            ],
            scratch_shapes=[
                pltpu.VMEM((1024, WIDTH), jnp.bfloat16),
                pltpu.VMEM((1024, WIDTH), jnp.bfloat16),
                pltpu.VMEM((2, STEPS, BLOCK, BLOCK), jnp.float32),
                pltpu.VMEM((2, STEPS, BLOCK, BLOCK), jnp.float32),
                pltpu.VMEM((1024, 128), jnp.float32),
                pltpu.VMEM((1024, 128), jnp.float32),
                pltpu.VMEM((STEPS, 128, BLOCK), jnp.bfloat16),
                pltpu.VMEM((1024, 512), jnp.float32),
                pltpu.VMEM((512, 1024), jnp.bfloat16),
                pltpu.VMEM((256, 1024), jnp.bfloat16),
                pltpu.VMEM((4 * CHUNK, 128), jnp.float32),
                pltpu.SemaphoreType.DMA((2, STEPS)),
            ],
        ),
        out_shape=[
            jax.ShapeDtypeStruct((4 * WIDTH, 128), jnp.bfloat16),
            jax.ShapeDtypeStruct((256, WIDTH), jnp.bfloat16),
        ],
        compiler_params=pltpu.CompilerParams(vmem_limit_bytes=60 * 2**20),
        name="backward",
    )(start, grads, gathered, weight, heads, query, key, value, inverse, cosine, sine, start[None, :])


def nesterov(mean_delta, moment_part, params_part):
    moment_next = 0.9 * moment_part + mean_delta
    return (moment_next, params_part - 0.7 * (mean_delta + 0.9 * moment_next))


def over_x(values, step):
    pairs = [(x * 2 + zh, (x + step) % 4 * 2 + zh) for x in range(4) for zh in range(2)]
    return lax.ppermute(values, "group", pairs)


def delta_over_x(delta):
    x = lax.axis_index("group") // 2
    quarter = lambda n: lax.dynamic_slice_in_dim(delta, n % 4 * 32, 32, axis=0)
    summed = quarter(x).astype(jnp.float32)
    for step in (1, 2, 3):
        summed = summed + over_x(quarter(x + step), step).astype(jnp.float32)
    return summed.astype(jnp.bfloat16)


def delta_over_group(summed):
    x = lax.axis_index("group") // 2
    other = lax.ppermute(summed, "group", [(g, g ^ 1) for g in range(8)])
    total = (summed.astype(jnp.float32) + other.astype(jnp.float32)).astype(jnp.bfloat16)
    quarters = jnp.stack([total] + [over_x(total, step) for step in (1, 2, 3)])
    ordered = jnp.take(quarters, (x - jnp.arange(4)) % 4, axis=0)
    return ordered.reshape(128, WIDTH).astype(jnp.float32)


def local(
    tokens,
    pre_gain,
    post_gain,
    qkv_weight,
    out_weight,
    doc_ids,
    cotangent,
    outer_delta,
    momentum,
    fragment,
):
    group = lax.axis_index("group")
    gathered, wide = gather_normed(tokens, pre_gain[None, :], qkv_weight.reshape(4 * WIDTH, 128))
    gathered = gathered.reshape(16 * ROWS, WIDTH)
    delta, gathered = lax.optimization_barrier((outer_delta[0], gathered))
    summed = delta_over_x(delta)
    length, width = gathered.shape
    cosine, sine = tables(length, 128)
    start = jnp.sum((doc_ids[None, :] < doc_ids[:, None]).astype(jnp.int32), axis=1)
    query, key, value, head_flat, inverse = forward(
        gathered, wide, cosine, sine, start
    )
    out_flat = out_weight.reshape(256, width)
    share = lax.dynamic_slice_in_dim(head_flat.reshape(8, 2, 8, 8, 256), group, 1, axis=2)
    share = jnp.transpose(share[:, :, 0], (1, 0, 2, 3)).reshape(128, 256)
    own_tokens = lax.dynamic_slice_in_dim(tokens, group * 8, 8, axis=0).astype(jnp.float32)
    own_cotangent = lax.dynamic_slice_in_dim(cotangent, group * 8, 8, axis=0).astype(jnp.float32)
    output, grad_rows = middle(share, out_flat, own_tokens, own_cotangent, post_gain[None, :])
    grad_rows = grad_rows.reshape(length, width)
    summed, grad_rows = lax.optimization_barrier((summed, grad_rows))
    total_delta = delta_over_group(summed)
    grad_qkv, grad_out = backward(
        grad_rows, gathered, out_flat, head_flat, query, key, value, inverse, cosine, sine, start
    )
    grad_qkv, grad_out = grad_qkv.reshape(qkv_weight.shape), grad_out.reshape(out_weight.shape)
    new_momentum, new_fragment = nesterov(total_delta / lax.axis_size("group"), momentum, fragment)
    return (output, grad_qkv, grad_out, new_momentum, new_fragment)


def solution(mesh):
    placed = (
        P("fsdp", None),
        P(),
        P(),
        P(None, "fsdp", None, None),
        P("fsdp", None, None, None),
        P(),
        P("fsdp", None),
        P("group", "fsdp", None),
        P("fsdp", None),
        P("fsdp", None),
    )
    return jax.shard_map(
        local,
        mesh=mesh,
        in_specs=placed,
        out_specs=(
            P("fsdp", None),
            P(None, "fsdp", None, None),
            P("fsdp", None, None, None),
            P("fsdp", None),
            P("fsdp", None),
        ),
        check_vma=False,
    )
```

time: 224 us -> 177 us (0.79)
  Pallas kernels: 174 us -> 145 us
  local copies, waits for them, and re-layouts: 24.2 us -> 5.12 us
  between operations: 14.2 us -> 0.86 us
  starting transfers between devices: 0.04 us -> 9.5 us
  waiting for transfers between devices: 0.68 us -> 5.1 us
    pallas_call x2 -> x1, Pallas kernels: 63.7 us -> 38.7 us  [gather_normed(): pl.pallas_call(normed_kernel, out_shape=(jax.ShapeDtypeStruct((16, ROWS,...]
    unnamed x40 -> x9, local copies, waits for them, and re-layouts: 23.4 us -> 0.83 us
    ppermute x0 -> x7, starting transfers between devices: none -> 9.5 us  [the longest x6 7.43 us: over_x(): return lax.ppermute(values, 'group', pairs)]
    ppermute x0 -> x7, waiting for transfers between devices: none -> 5.1 us  [the longest x1 5.09 us: delta_over_group(): other = lax.ppermute(summed, 'group', [(g, g ^ 1) for g in range(8)])]
    pallas_call x1, Pallas kernels: 29.2 us -> 25.9 us  [backward(): pl.pallas_call(backward_kernel, grid_spec=pltpu.PrefetchScalarGridSpec(nu...]
    pallas_call x1, Pallas kernels: 67.4 us -> 64.7 us  [middle(): pl.pallas_call(middle_kernel, out_shape=(jax.ShapeDtypeStruct((ROWS, WIDT...]
  transfers between devices with their start and end apart: 1 -> 7, of which waited for: 0 -> 1; matrix products, arithmetic and copies ran while one was open for 5% -> 3% of each run, Pallas kernels for 78% -> 61%
where the time goes in v3:
time: 177 us; the launch traced here: 174 us
  Pallas kernels  145 us (82%)
  starting transfers between devices  9.5 us (5%)
  other arithmetic  8.71 us (5%)
  local copies, waits for them, and re-layouts  5.12 us (3%)
  waiting for transfers between devices  5.1 us (3%)
    pallas_call x1, Pallas kernels, middle(): pl.pallas_call(middle_kernel, out_shape=(jax.ShapeDtypeStruct((ROWS, WIDT...  64.7 us
    pallas_call x1, Pallas kernels, gather_normed(): pl.pallas_call(normed_kernel, out_shape=(jax.ShapeDtypeStruct((16, ROWS,...  38.7 us
    pallas_call x1, Pallas kernels, backward(): pl.pallas_call(backward_kernel, grid_spec=pltpu.PrefetchScalarGridSpec(nu...  25.9 us
    pallas_call x1, Pallas kernels, forward(): pl.pallas_call(forward_kernel, grid_spec=pltpu.PrefetchScalarGridSpec(num...  15.5 us
    ppermute x6, starting transfers between devices, over_x(): return lax.ppermute(values, 'group', pairs)  7.43 us
    sub x1, other arithmetic, nesterov(): return (moment_next, params_part - 0.7 * (mean_delta + 0.9 * moment_next))  5.42 us
    ppermute x1, waiting for transfers between devices, delta_over_group(): other = lax.ppermute(summed, 'group', [(g, g ^ 1) for g in range(8)])  5.09 us
  transfers between devices with their start and end apart: 7, of which 1 were waited for; matrix products, arithmetic and copies ran while one was open for 3% of the time, Pallas kernels for 61%

profile of v3, /device:TPU:1, one launch (start us, length us, event | category | flops | bytes accessed | tf_op | source)
XLA Modules:
  0.0 174.1 jit_solution(17372101292079331276)
XLA Ops:
  0.7 1.3 broadcast_in_dim.26.gain
  2.0 0.0 copy-start
  2.1 0.0 copy-start.3
  2.1 38.7 %gather_normed.1 = (bf16[16,64,4608]{2,1,0:T(8,128)(2,1)}, bf16[4608,512]{1,0:T(8,128)(2,1)}) custom-call(bf16[64,4608]{1,0:T(8,128)(2,1)} %tokens.1, f32[1,4608]{1,0:T(1,128)} %broadcast_in_dim.26.gain, bf16[18432,128]{1,0:T(8,128)(2,1)} %bitcast.34), custom_call_target="tpu_custom_call" | custom-call | tf_op jit(solution)/shard_map/gather_normed/pallas_call | solution.py:255
  40.8 0.0 copy-done
  40.8 0.1 constant_dynamic-slice_fusion.2
  40.9 1.1 collective-permute-start.2
  42.0 0.7 collective-permute-start.1
  42.7 0.3 collective-permute-start
  43.0 0.0 copy-done.3
  43.0 1.2 convert_reduce_fusion.starts
  44.3 0.0 copy-start.2
  44.3 15.5 %forward.1 = (bf16[1024,256]{1,0:T(8,128)(2,1)}, bf16[1024,128]{1,0:T(8,128)(2,1)}, bf16[1024,128]{1,0:T(8,128)(2,1)}, bf16[1024,256]{1,0:T(8,128)(2,1)}, f32[8,1024]{1,0:T(8,128)}) custom-call(s32[1024]{0:T(1024)} %convert_reduce_fusion.starts, bf16[1024,4608]{1,0:T(8,128)(2,1)} %bitcast.29, bf16[4608,512]{1,0:T(8,128)(2,1)} %get-tuple-element.22.weight, ...), custom_call_target="tpu_custom_call" | custom-call | tf_op jit(solution)/shard_map/forward/pallas_call | solution.py:466
  59.8 0.8 constant_dynamic-slice_fusion.3
  60.6 0.6 copy.19
  61.3 0.0 copy-done.2
  61.3 0.6 broadcast_in_dim.28.gain
  61.9 1.6 dynamic-slice_convert_fusion
  63.5 64.7 %middle.1 = (bf16[64,4608]{1,0:T(8,128)(2,1)}, bf16[16,64,4608]{2,1,0:T(8,128)(2,1)}) custom-call(bf16[128,256]{1,0:T(8,128)(2,1)} %bitcast.42, bf16[256,4608]{1,0:T(8,128)(2,1)} %bitcast.31, f32[8,4608]{1,0:T(8,128)} %get-tuple-element.51.tokens, f32[8,4608]{1,0:T(8,128)} %get-tuple-element.50.cotangent, f32[1,4608]{1,0:T(1,128)} %broadcast_in_dim.28.gain), custom_call_target="tpu_custom_call" | custom-call | tf_op jit(solution)/shard_map/middle/pallas_call | solution.py:360
  128.2 0.0 collective-permute-done.2
  128.2 0.0 collective-permute-done.1
  128.2 0.0 collective-permute-done
  128.3 0.2 add_convert_fusion.1
  128.4 2.1 %collective-permute-start.3 = (bf16[32,4608]{1,0:T(8,128)(2,1)S(1)}, bf16[32,4608]{1,0:T(8,128)(2,1)S(1)}, u32[]{:S(2)}, u32[]{:S(2)}) collective-permute-start(bf16[32,4608]{1,0:T(8,128)(2,1)S(1)} %add_convert_fusion.1), channel_id=1, source_target_pairs={{0,16},{16,0},{32,48},{48,32},{64,80},{80,64},{96,112},{112,96},{1... | collective-permute-start | bytes 884744 | tf_op jit(solution)/shard_map/ppermute | solution.py:659
  130.5 5.1 %collective-permute-done.3 = bf16[32,4608]{1,0:T(8,128)(2,1)S(1)} collective-permute-done((bf16[32,4608]{1,0:T(8,128)(2,1)S(1)}, bf16[32,4608]{1,0:T(8,128)(2,1)S(1)}, u32[]{:S(2)}, u32[]{:S(2)}) %collective-permute-start.3) | collective-permute-done | bytes 294944 | tf_op jit(solution)/shard_map/ppermute | solution.py:659
  135.6 0.1 add_convert_fusion
  135.6 4.6 %collective-permute-start.6 = (bf16[32,4608]{1,0:T(8,128)(2,1)S(1)}, bf16[32,4608]{1,0:T(8,128)(2,1)S(1)}, u32[]{:S(2)}, u32[]{:S(2)}) collective-permute-start(bf16[32,4608]{1,0:T(8,128)(2,1)S(1)} %add_convert_fusion), channel_id=1, source_target_pairs={{0,96},{16,112},{32,0},{48,16},{64,32},{80,48},{96,64},{112,80},{1... | collective-permute-start | bytes 884744 | tf_op jit(solution)/shard_map/ppermute | solution.py:645
  140.3 0.0 collective-permute-start.5
  140.3 0.7 collective-permute-start.4
  140.9 0.1 broadcast_in_dim.29
  141.0 0.1 broadcast_in_dim.30
  141.1 25.9 %backward.1 = (bf16[18432,128]{1,0:T(8,128)(2,1)}, bf16[256,4608]{1,0:T(8,128)(2,1)}) custom-call(s32[1024]{0:T(1024)} %convert_reduce_fusion.starts, bf16[1024,4608]{1,0:T(8,128)(2,1)} %bitcast.33, bf16[1024,4608]{1,0:T(8,128)(2,1)} %bitcast.30, bf16[256,4608]{1,0:T(8,128)(2,1)} %bitcast.32, bf16[1024,256]{1,0:T(8,128)(2,1)} %get-tuple-element.23.heads, ...), custom_call_target="tpu_custom_call" | custom-call | tf_op jit(solution)/shard_map/backward/pallas_call | solution.py:592
  167.0 0.0 collective-permute-done.6
  167.0 0.0 collective-permute-done.5
  167.1 0.0 collective-permute-done.4
  167.1 0.2 pad_maximum_fusion
  167.2 0.6 gather_fusion
  167.9 0.0 copy-start.1
  167.9 5.4 %multiply_subtract_fusion = (f32[128,4608]{1,0:T(8,128)}, f32[128,4608]{1,0:T(8,128)}) fusion(f32[128,4608]{1,0:T(8,128)} %param.21, bf16[4,32,4608]{2,1,0:T(8,128)(2,1)S(1)} %gather_fusion, pred[128]{0:T(512)(128)(4,1)S(1)} %broadcast_in_dim.30, f32[128,4608]{1,0:T(8,128)} %param.20), kind=kLoop, calls=%fused_computation.2 | loop fusion | flops 5308416 | bytes 10616960 | tf_op jit(solution)/shard_map/sub | solution.py:640
  173.3 0.0 copy-done.1
  173.3 0.8 copy.22
  (3 shorter events, 0.0 us)
Async XLA Ops:
  2.0 38.8 %copy-start = (bf16[1,128,4608]{2,1,0:T(8,128)(2,1)S(1)}, bf16[1,128,4608]{2,1,0:T(8,128)(2,1)}, u32[]{:S(2)}) copy-start(bf16[1,128,4608]{2,1,0:T(8,128)(2,1)} %param.19) | copy-start | bytes 3538948
  2.1 41.0 %copy-start.3 = (s32[1024]{0:T(1024)S(1)}, s32[1024]{0:T(1024)}, u32[]{:S(2)}) copy-start(s32[1024]{0:T(1024)} %param.17) | copy-start | bytes 12292
  40.9 87.3 %collective-permute-start.2 = (bf16[32,4608]{1,0:T(8,128)(2,1)S(1)}, bf16[32,4608]{1,0:T(8,128)(2,1)S(1)}, u32[]{:S(2)}, u32[]{:S(2)}) collective-permute-start(bf16[32,4608]{1,0:T(8,128)(2,1)S(1)} %get-tuple-element.48), channel_id=1, source_target_pairs={{0,96},{16,112},{32,0},{48,16},{64,32},{80,48},{96,64},{112,80},{1... | collective-permute-start | bytes 884744 | tf_op jit(solution)/shard_map/ppermute | solution.py:645
  42.0 86.2 %collective-permute-start.1 = (bf16[32,4608]{1,0:T(8,128)(2,1)S(1)}, bf16[32,4608]{1,0:T(8,128)(2,1)S(1)}, u32[]{:S(2)}, u32[]{:S(2)}) collective-permute-start(bf16[32,4608]{1,0:T(8,128)(2,1)S(1)} %get-tuple-element.49), channel_id=1, source_target_pairs={{0,64},{16,80},{32,96},{48,112},{64,0},{80,16},{96,32},{112,48},{1... | collective-permute-start | bytes 884744 | tf_op jit(solution)/shard_map/ppermute | solution.py:645
  42.7 85.5 %collective-permute-start = (bf16[32,4608]{1,0:T(8,128)(2,1)S(1)}, bf16[32,4608]{1,0:T(8,128)(2,1)S(1)}, u32[]{:S(2)}, u32[]{:S(2)}) collective-permute-start(bf16[32,4608]{1,0:T(8,128)(2,1)S(1)} %get-tuple-element.47), channel_id=1, source_target_pairs={{0,32},{16,48},{32,64},{48,80},{64,96},{80,112},{96,0},{112,16},{1... | collective-permute-start | bytes 884744 | tf_op jit(solution)/shard_map/ppermute | solution.py:645
  44.3 17.0 %copy-start.2 = (f32[4608]{0:T(1024)S(1)}, f32[4608]{0:T(1024)}, u32[]{:S(2)}) copy-start(f32[4608]{0:T(1024)} %param.14) | copy-start | bytes 55300
  128.4 7.2 %collective-permute-start.3 = (bf16[32,4608]{1,0:T(8,128)(2,1)S(1)}, bf16[32,4608]{1,0:T(8,128)(2,1)S(1)}, u32[]{:S(2)}, u32[]{:S(2)}) collective-permute-start(bf16[32,4608]{1,0:T(8,128)(2,1)S(1)} %add_convert_fusion.1), channel_id=1, source_target_pairs={{0,16},{16,0},{32,48},{48,32},{64,80},{80,64},{96,112},{112,96},{1... | collective-permute-start | bytes 884744 | tf_op jit(solution)/shard_map/ppermute | solution.py:659
  135.6 31.4 %collective-permute-start.6 = (bf16[32,4608]{1,0:T(8,128)(2,1)S(1)}, bf16[32,4608]{1,0:T(8,128)(2,1)S(1)}, u32[]{:S(2)}, u32[]{:S(2)}) collective-permute-start(bf16[32,4608]{1,0:T(8,128)(2,1)S(1)} %add_convert_fusion), channel_id=1, source_target_pairs={{0,96},{16,112},{32,0},{48,16},{64,32},{80,48},{96,64},{112,80},{1... | collective-permute-start | bytes 884744 | tf_op jit(solution)/shard_map/ppermute | solution.py:645
  140.3 26.8 %collective-permute-start.5 = (bf16[32,4608]{1,0:T(8,128)(2,1)S(1)}, bf16[32,4608]{1,0:T(8,128)(2,1)S(1)}, u32[]{:S(2)}, u32[]{:S(2)}) collective-permute-start(bf16[32,4608]{1,0:T(8,128)(2,1)S(1)} %add_convert_fusion), channel_id=1, source_target_pairs={{0,64},{16,80},{32,96},{48,112},{64,0},{80,16},{96,32},{112,48},{1... | collective-permute-start | bytes 884744 | tf_op jit(solution)/shard_map/ppermute | solution.py:645
  140.3 26.8 %collective-permute-start.4 = (bf16[32,4608]{1,0:T(8,128)(2,1)S(1)}, bf16[32,4608]{1,0:T(8,128)(2,1)S(1)}, u32[]{:S(2)}, u32[]{:S(2)}) collective-permute-start(bf16[32,4608]{1,0:T(8,128)(2,1)S(1)} %add_convert_fusion), channel_id=1, source_target_pairs={{0,32},{16,48},{32,64},{48,80},{64,96},{80,112},{96,0},{112,16},{1... | collective-permute-start | bytes 884744 | tf_op jit(solution)/shard_map/ppermute | solution.py:645
  167.9 5.4 %copy-start.1 = (bf16[64,4608]{1,0:T(8,128)(2,1)S(1)}, bf16[64,4608]{1,0:T(8,128)(2,1)}, u32[]{:S(2)}) copy-start(bf16[64,4608]{1,0:T(8,128)(2,1)} %get-tuple-element.57) | copy-start | bytes 1769476

commit v4 on v3

--- a/solution.py
+++ b/solution.py
@@ -14,8 +14,8 @@
 WIDTH = 4608
 HALF = WIDTH // 2
 ROWS = 64
-N1, N2, NQ = 10 * 128, 10 * 128, 4 * 128
-NP = N1 + N2
+FIRST_SPLIT = (10 * 128, 10 * 128, 4 * 128)
+SECOND_SPLIT = (14 * 128, 14 * 128, 2 * 128)
 
 
 def place():
@@ -61,7 +61,9 @@
 SPREAD_SENDS = 69
 
 
-def spread(own, full, send, piece_sems, pair_sems, local_sem, work=iter(()), later=None):
+def spread(split, own, full, send, piece_sems, pair_sems, local_sem, work=iter(()), later=None):
+    N1, N2, NQ = split
+    NP = N1 + N2
     x, zh, zl, y, c = place()
     k, kz = zl * 4 + y, (1 - zl) * 4 + y
     near_k, near_kz = ([b * 4 + (y + s) % 4 for s in (1, 3, 2)] for b in (zl, 1 - zl))
@@ -207,6 +209,10 @@
     pl.semaphore_wait(pltpu.get_barrier_semaphore(), len(devices))
 
 
+def as_row(gain):
+    return jnp.concatenate([gain[n : n + 1, :] for n in range(WIDTH // 128)], axis=1)
+
+
 PARTS = 8
 PART = WIDTH // PARTS
 
@@ -243,10 +249,10 @@
     greet(near())
     values = tokens[...].astype(jnp.float32)
     scale = lax.rsqrt(jnp.mean(values * values, axis=-1, keepdims=True) + 1e-06)
-    own[...] = (values * scale * gain[...]).astype(jnp.bfloat16)
+    own[...] = (values * scale * as_row(gain)).astype(jnp.bfloat16)
     met(near())
     send = Sender(send_sems)
-    spread(own, full, send, piece_sems, pair_sems, local_sem, work)
+    spread(FIRST_SPLIT, own, full, send, piece_sems, pair_sems, local_sem, work)
     send.finish()
 
 
@@ -288,9 +294,9 @@
 
 
 def middle_kernel(
-    heads, weight, tokens, cotangent, gain, output, full,
-    partial, received, mate, total, mine, group_in, own,
-    send_sems, mate_sem, part_sems, group_sems, piece_sems, pair_sems, local_sem,
+    heads, weight_hbm, tokens, cotangent, gain, delta, output, full, delta_sum,
+    weight, partial, received, mate, total, mine, group_in, out_in, own, own_part, parts_in, summed, other, delta_total,
+    send_sems, mate_sems, part_sems, group_sems, out_sems, piece_sems, pair_sems, local_sems, delta_sems, sum_sems,
 ):
     x, zh, zl, y, c = place()
     k, g = zl * 4 + y, x * 2 + zh
@@ -300,22 +306,43 @@
     to_fellows = [device(x, zh, a, b, c) for a, b in fellows]
     kin = [((x + b) % 4, (zh + a) % 2) for a, b in chips]
     to_kin = [device(a, b, zl, y, c) for a, b in kin]
+    to_x = [device((x + step) % 4, zh, zl, y, c) for step in (1, 2, 3)]
+    to_zh = device(x, 1 - zh, zl, y, c)
     greet([sib] + to_fellows + to_kin)
+    load = pltpu.make_async_copy(weight_hbm, weight, local_sems.at[1])
+    load.start()
+    load_part = pltpu.make_async_copy(delta.at[pl.ds(pl.multiple_of(x * 32, 32), 32), :], own_part, local_sems.at[2])
+    load_part.start()
+    share = heads[:, pl.ds(pl.multiple_of(g * 8, 8), 8), :]
+    load.wait()
     for core in range(2):
-        left = jnp.dot(heads[pl.ds(core * 64, 64)], weight[:, pl.ds(0, HALF)], preferred_element_type=jnp.float32)
-        right = jnp.dot(heads[pl.ds(core * 64, 64)], weight[:, pl.ds(HALF, HALF)], preferred_element_type=jnp.float32)
+        rows = jnp.concatenate([share[2 * kk + core] for kk in range(8)], axis=0).astype(jnp.bfloat16)
+        left = jnp.dot(rows, weight[:, :HALF], preferred_element_type=jnp.float32)
+        right = jnp.dot(rows, weight[:, HALF:], preferred_element_type=jnp.float32)
         for kk in range(8):
             both = jnp.concatenate([left[kk * 8 : kk * 8 + 8], right[kk * 8 : kk * 8 + 8]], axis=0)
             partial[core, kk] = both.astype(jnp.bfloat16)
     met([sib] + to_fellows + to_kin)
     send = Sender(send_sems)
-    send(partial.at[1 - c], mate, mate_sem, sib)
-    send.arrived(mate, mate_sem, sib)
-    for kk in range(8):
+    for n, (a, b) in enumerate(fellows):
+        kk = a * 4 + b
+        send(partial.at[1 - c, kk], mate.at[kk], mate_sems.at[kk], sib)
+    send(partial.at[1 - c, k], mate.at[k], mate_sems.at[k], sib)
+    for n, step in enumerate((1, 2, 3)):
+        rows = pl.ds(pl.multiple_of((x + step) % 4 * 32, 32), 32)
+        send(delta.at[rows, :], parts_in.at[n], delta_sems.at[n], to_x[n])
+    for (a, b), to in zip(fellows, to_fellows):
+        kk = a * 4 + b
+        send.arrived(mate.at[kk], mate_sems.at[kk], sib)
         total[kk] = (partial[c, kk].astype(jnp.float32) + mate[kk].astype(jnp.float32)).astype(jnp.bfloat16)
-    for (a, b), to in zip(fellows, to_fellows):
-        send(total.at[a * 4 + b], received.at[k], part_sems.at[k], to)
+        send(total.at[kk], received.at[k], part_sems.at[k], to)
+    send.arrived(mate.at[k], mate_sems.at[k], sib)
     both = partial[c, k].astype(jnp.float32) + mate[k].astype(jnp.float32)
+    gain_row = as_row(gain)
+    pick = lambda rows: jnp.where(g % 2 == 0, rows[:8], rows[8:])
+    near_rows = pl.ds(pl.multiple_of(g // 2 * 16, 16), 16)
+    own_tokens = pick(tokens[near_rows, :].astype(jnp.float32))
+    dnorm = pick(cotangent[near_rows, :].astype(jnp.float32)) * gain_row
     for a, b in fellows:
         kk = a * 4 + b
         send.arrived(received.at[kk], part_sems.at[kk], sib)
@@ -323,69 +350,110 @@
     attn = unstacked(both)
     scale = lax.rsqrt(jnp.mean(attn * attn, axis=-1, keepdims=True) + 1e-06)
     normal = attn * scale
-    out = tokens[...] + normal * gain[...]
-    dnorm = cotangent[...] * gain[...]
     grad = scale * (dnorm - normal * jnp.mean(dnorm * normal, axis=-1, keepdims=True))
-    mine[0] = stacked(grad).astype(jnp.bfloat16)
-    mine[1] = stacked(out).astype(jnp.bfloat16)
+    mine[...] = stacked(grad).astype(jnp.bfloat16)
     for to in to_kin:
-        send(mine.at[0], group_in.at[0, g], group_sems.at[0, g], to)
-
-    def later():
-        for to in to_kin:
-            send(mine.at[1], group_in.at[1, g], group_sems.at[1, g], to)
-
-    group_in[0, g] = mine[0]
-    group_in[1, g] = mine[1]
+        send(mine, group_in.at[g], group_sems.at[g], to)
+    group_in[g] = mine[...]
+    out_in[zh, x] = stacked(own_tokens + normal * gain_row).astype(jnp.bfloat16)
+    load_part.wait()
+    for n, step in enumerate((1, 2, 3)):
+        send.arrived(parts_in.at[n], delta_sems.at[n], sib)
+    summed[...] = (
+        own_part[...].astype(jnp.float32)
+        + parts_in[0].astype(jnp.float32)
+        + parts_in[1].astype(jnp.float32)
+        + parts_in[2].astype(jnp.float32)
+    ).astype(jnp.bfloat16)
     for a, b in kin:
         gg = a * 2 + b
-        send.arrived(group_in.at[0, gg], group_sems.at[0, gg], sib)
+        send.arrived(group_in.at[gg], group_sems.at[gg], sib)
     for gg in range(0, 8, 2):
-        first = unstacked(group_in[0, gg].astype(jnp.float32))
-        second = unstacked(group_in[0, gg + 1].astype(jnp.float32))
+        first = unstacked(group_in[gg].astype(jnp.float32))
+        second = unstacked(group_in[gg + 1].astype(jnp.float32))
         own[pl.ds(gg * 8, 16), :] = jnp.concatenate([first, second], axis=0).astype(jnp.bfloat16)
-    spread(own, full, send, piece_sems, pair_sems, local_sem, later=later)
-    for a, b in kin:
-        gg = a * 2 + b
-        send.arrived(group_in.at[1, gg], group_sems.at[1, gg], sib)
+
+    def later():
+        yield
+        send(summed, other, sum_sems.at[0, 0], to_zh)
+        for n, to in enumerate(to_x):
+            send(out_in.at[zh, x], out_in.at[zh, x], out_sems.at[x], to)
+        for _ in range(12):
+            yield
+        send.arrived(other, sum_sems.at[0, 0], sib)
+        delta_total[...] = (summed[...].astype(jnp.float32) + other[...].astype(jnp.float32)).astype(jnp.bfloat16)
+        for to in (to_x[0], to_x[2]):
+            send(delta_total, delta_sum.at[x], sum_sems.at[1, x], to)
+        for step in (1, 2, 3):
+            there = out_in.at[zh, (x + step) % 4]
+            send.arrived(there, out_sems.at[(x + step) % 4], sib)
+        send(out_in.at[zh], out_in.at[zh], out_sems.at[4], to_zh)
+        for _ in range(8):
+            yield
+        for side, step in enumerate((1, 3)):
+            n = (x + step) % 4
+            send.arrived(delta_sum.at[n], sum_sems.at[1, n], sib)
+            half = delta_sum.at[n, pl.ds(side * 16, 16), :]
+            send(half, half, sum_sems.at[2 + side, n], to_x[2 - 2 * side])
+
+    spread(SECOND_SPLIT, own, full, send, piece_sems, pair_sems, local_sems.at[0], later())
+    keep = pltpu.make_async_copy(delta_total, delta_sum.at[x], local_sems.at[1])
+    keep.start()
+    send.arrived(out_in.at[1 - zh], out_sems.at[4], sib)
     for gg in range(0, 8, 2):
-        first = unstacked(group_in[1, gg].astype(jnp.float32))
-        second = unstacked(group_in[1, gg + 1].astype(jnp.float32))
+        first = unstacked(out_in[0, gg // 2].astype(jnp.float32))
+        second = unstacked(out_in[1, gg // 2].astype(jnp.float32))
         output[pl.ds(gg * 8, 16), :] = jnp.concatenate([first, second], axis=0).astype(jnp.bfloat16)
+    n = (x + 2) % 4
+    for side in range(2):
+        send.arrived(delta_sum.at[n, pl.ds(side * 16, 16), :], sum_sems.at[2 + side, n], sib)
+    keep.wait()
     send.finish()
 
 
-def middle(heads, weight, tokens, cotangent, gain):
+def middle(heads, weight, tokens, cotangent, gain, delta):
     vmem = pl.BlockSpec(memory_space=pltpu.VMEM)
+    hbm = pl.BlockSpec(memory_space=pl.ANY)
     return pl.pallas_call(
         middle_kernel,
         out_shape=(
             jax.ShapeDtypeStruct((ROWS, WIDTH), jnp.bfloat16),
             jax.ShapeDtypeStruct((16, ROWS, WIDTH), jnp.bfloat16),
+            jax.ShapeDtypeStruct((4, 32, WIDTH), jnp.bfloat16),
         ),
-        in_specs=[vmem] * 5,
-        out_specs=(vmem, pl.BlockSpec(memory_space=pl.ANY)),
+        in_specs=[vmem, hbm, vmem, vmem, vmem, hbm],
+        out_specs=(vmem, hbm, hbm),
         scratch_shapes=[
+            pltpu.VMEM((256, WIDTH), jnp.bfloat16),
             pltpu.VMEM((2, 8, 16, HALF), jnp.bfloat16),
             pltpu.VMEM((8, 16, HALF), jnp.bfloat16),
             pltpu.VMEM((8, 16, HALF), jnp.bfloat16),
             pltpu.VMEM((8, 16, HALF), jnp.bfloat16),
-            pltpu.VMEM((2, 16, HALF), jnp.bfloat16),
-            pltpu.VMEM((2, 8, 16, HALF), jnp.bfloat16),
+            pltpu.VMEM((16, HALF), jnp.bfloat16),
+            pltpu.VMEM((8, 16, HALF), jnp.bfloat16),
+            pltpu.VMEM((2, 4, 16, HALF), jnp.bfloat16),
             pltpu.VMEM((ROWS, WIDTH), jnp.bfloat16),
-            pltpu.SemaphoreType.DMA((1 + 7 + 14 + SPREAD_SENDS,)),
-            pltpu.SemaphoreType.DMA,
+            pltpu.VMEM((32, WIDTH), jnp.bfloat16),
+            pltpu.VMEM((3, 32, WIDTH), jnp.bfloat16),
+            pltpu.VMEM((32, WIDTH), jnp.bfloat16),
+            pltpu.VMEM((32, WIDTH), jnp.bfloat16),
+            pltpu.VMEM((32, WIDTH), jnp.bfloat16),
+            pltpu.SemaphoreType.DMA((8 + 3 + 7 + 7 + 9 + SPREAD_SENDS,)),
             pltpu.SemaphoreType.DMA((8,)),
-            pltpu.SemaphoreType.DMA((2, 8)),
+            pltpu.SemaphoreType.DMA((8,)),
+            pltpu.SemaphoreType.DMA((8,)),
+            pltpu.SemaphoreType.DMA((5,)),
             pltpu.SemaphoreType.DMA((2, 6, 8)),
             pltpu.SemaphoreType.DMA((8, 2)),
-            pltpu.SemaphoreType.DMA,
+            pltpu.SemaphoreType.DMA((3,)),
+            pltpu.SemaphoreType.DMA((3,)),
+            pltpu.SemaphoreType.DMA((4, 4)),
         ],
         compiler_params=pltpu.CompilerParams(
             collective_id=1, has_side_effects=True, vmem_limit_bytes=60 * 2**20
         ),
         name="middle",
-    )(heads, weight, tokens, cotangent, gain)
+    )(heads, weight, tokens, cotangent, gain, delta)
 
 
 def tables(length, width):
@@ -408,6 +476,19 @@
     return values * cosine + pltpu.roll(values, 64, 1) * sine
 
 
+def document_starts(doc_ids, starts):
+    ids = doc_ids[...]
+    first = jnp.zeros_like(ids)
+    for n in range(3):
+        first += jnp.where(ids > n, jnp.sum((ids == n).astype(jnp.int32)), 0)
+    starts[...] = first
+
+
+def start_of(starts, i):
+    row = jnp.concatenate([starts[pl.ds(2 * i, 1), :], starts[pl.ds(2 * i + 1, 1), :]], axis=1)
+    return row, jnp.min(row) // BLOCK
+
+
 def scored(keys, queries, first_key, start_row, query_row):
     raw = lax.dot_general(keys, queries, (((1,), (1,)), ((), ())), preferred_element_type=jnp.float32)
     soft = jnp.tanh(raw * (query_scale / softcap))
@@ -417,9 +498,14 @@
 
 
 def forward_kernel(
-    starts, x, weight, cosine, sine, start_ref, query_ref, key_ref, value_ref, heads_ref, sums_ref, keep, keys, values_t
+    x, weight, cosine, sine, doc_ids, query_ref, key_ref, value_ref, heads_ref, sums_ref, keep, keys, values_t, starts
 ):
     i = pl.program_id(0)
+
+    @pl.when(i == 0)
+    def _():
+        document_starts(doc_ids, starts)
+
     proj = jnp.dot(x[...], weight[...], preferred_element_type=jnp.float32)
     queries = [turn(proj[:, h * 128 : h * 128 + 128], cosine[...], sine[...]).astype(jnp.bfloat16) for h in range(2)]
     key = turn(proj[:, 256:384], cosine[...], sine[...]).astype(jnp.bfloat16)
@@ -430,9 +516,8 @@
     value_ref[...] = value.astype(jnp.bfloat16)
     keys[i] = key
     values_t[i] = value.T.astype(jnp.bfloat16)
-    start_row = start_ref[...]
+    start_row, first = start_of(starts, i)
     query_row = lax.broadcasted_iota(jnp.int32, (1, BLOCK), 1) + i * BLOCK
-    first = starts[i * BLOCK] // BLOCK
 
     def score(j, sums):
         out = []
@@ -458,40 +543,38 @@
     zero = jnp.zeros((128, BLOCK), jnp.float32)
     accs = lax.fori_loop(first, i + 1, mix, (zero, zero))
     for h in range(2):
-        heads_ref[:, h * 128 : h * 128 + 128] = accs[h].T.astype(jnp.bfloat16)
-
-
-def forward(gathered, weight, cosine, sine, start):
-    rows = lambda n: pl.BlockSpec((BLOCK, n), lambda i, s: (i, 0))
+        heads_ref[:, h * 128 : h * 128 + 128] = accs[h].T
+
+
+def forward(gathered, weight, cosine, sine, doc_ids):
+    rows = lambda n: pl.BlockSpec((BLOCK, n), lambda i: (i, 0))
     return pl.pallas_call(
         forward_kernel,
-        grid_spec=pltpu.PrefetchScalarGridSpec(
-            num_scalar_prefetch=1,
-            grid=(STEPS,),
-            in_specs=[
-                rows(WIDTH),
-                pl.BlockSpec((WIDTH, 512), lambda i, s: (0, 0)),
-                rows(128),
-                rows(128),
-                pl.BlockSpec((1, BLOCK), lambda i, s: (0, i)),
-            ],
-            out_specs=[rows(256), rows(128), rows(128), rows(256), pl.BlockSpec((8, BLOCK), lambda i, s: (0, i))],
-            scratch_shapes=[
-                pltpu.VMEM((2, STEPS, BLOCK, BLOCK), jnp.float32),
-                pltpu.VMEM((STEPS, BLOCK, 128), jnp.bfloat16),
-                pltpu.VMEM((STEPS, 128, BLOCK), jnp.bfloat16),
-            ],
-        ),
+        grid=(STEPS,),
+        in_specs=[
+            rows(WIDTH),
+            pl.BlockSpec((WIDTH, 512), lambda i: (0, 0), pipeline_mode=pl.Buffered(1)),
+            rows(128),
+            rows(128),
+            pl.BlockSpec((8, 128), lambda i: (0, 0)),
+        ],
+        out_specs=[rows(256), rows(128), rows(128), rows(256), pl.BlockSpec((8, BLOCK), lambda i: (0, i))],
+        scratch_shapes=[
+            pltpu.VMEM((2, STEPS, BLOCK, BLOCK), jnp.float32),
+            pltpu.VMEM((STEPS, BLOCK, 128), jnp.bfloat16),
+            pltpu.VMEM((STEPS, 128, BLOCK), jnp.bfloat16),
+            pltpu.VMEM((8, 128), jnp.int32),
+        ],
         out_shape=[
             jax.ShapeDtypeStruct((1024, 256), jnp.bfloat16),
             jax.ShapeDtypeStruct((1024, 128), jnp.bfloat16),
             jax.ShapeDtypeStruct((1024, 128), jnp.bfloat16),
-            jax.ShapeDtypeStruct((1024, 256), jnp.bfloat16),
+            jax.ShapeDtypeStruct((1024, 256), jnp.float32),
             jax.ShapeDtypeStruct((8, 1024), jnp.float32),
         ],
         compiler_params=pltpu.CompilerParams(vmem_limit_bytes=60 * 2**20),
         name="forward",
-    )(start, gathered, weight, cosine, sine, start[None, :])
+    )(gathered, weight, cosine, sine, doc_ids)
 
 
 CHUNK = 512
@@ -499,8 +582,8 @@
 
 
 def backward_kernel(
-    starts, grads_hbm, x_hbm, weight, heads, query_ref, key_ref, value_ref, inverse_ref, cosine, sine, start_ref,
-    qkv_out, out_out, grads, x, slope, dprob, dkey, dvalue, keys_t, grad_proj, turned, heads_t, mixed, sems,
+    grads_hbm, x_hbm, weight, heads, query_ref, key_ref, value_ref, inverse_ref, cosine, sine, doc_ids,
+    delta, momentum, fragment, output, qkv_out, out_out, new_momentum, new_fragment, new_output, grads, x, slope, dprob, dkey, dvalue, keys_t, grad_proj, turned, heads_t, mixed, starts, sems,
 ):
     i = pl.program_id(0)
 
@@ -514,6 +597,7 @@
         for which in range(2):
             for n in range(STEPS):
                 load(n, which).start()
+        document_starts(doc_ids, starts)
         dkey[...] = jnp.zeros_like(dkey)
         dvalue[...] = jnp.zeros_like(dvalue)
 
@@ -527,9 +611,8 @@
             grads[own, :], weight[...], (((1,), (1,)), ((), ())), preferred_element_type=jnp.float32
         ).astype(jnp.bfloat16)
         keys_t[i] = key_ref[own, :].astype(jnp.float32).T.astype(jnp.bfloat16)
-        start_row = start_ref[...]
+        start_row, first = start_of(starts, i)
         query_row = lax.broadcasted_iota(jnp.int32, (1, BLOCK), 1) + i * BLOCK
-        first = starts[i * BLOCK] // BLOCK
         queries = [query_ref[own, head[h]] for h in range(2)]
         grad = [grad_heads[:, head[h]] for h in range(2)]
 
@@ -570,7 +653,7 @@
         grad_proj[:, 256:384] = turn(dkey[...], cosine[...], -sine[...])
         grad_proj[:, 384:512] = dvalue[...]
         turned[...] = grad_proj[...].T.astype(jnp.bfloat16)
-        heads_t[...] = heads[...].astype(jnp.float32).T.astype(jnp.bfloat16)
+        heads_t[...] = heads[...].T.astype(jnp.bfloat16)
         for n in range(STEPS):
             load(n, 1).wait()
 
@@ -582,85 +665,72 @@
             mixed[pl.ds(j, CHUNK, stride=4), :] = part.T
         out_out[...] = jnp.dot(heads_t[...], grads[:, at], preferred_element_type=jnp.float32).astype(jnp.bfloat16)
         qkv_out[...] = mixed[...].astype(jnp.bfloat16)
-
-
-def backward(grads, gathered, weight, heads, query, key, value, inverse, cosine, sine, start):
-    whole = lambda *shape: pl.BlockSpec(shape, lambda i, s: (0, 0), pipeline_mode=pl.Buffered(1))
-    place_of = lambda i: jnp.minimum(i, STEPS - 1)
+        mean_delta = delta[...].astype(jnp.float32) / 8.0
+        moment = 0.9 * momentum[...] + mean_delta
+        new_momentum[...] = moment
+        new_fragment[...] = fragment[...] - 0.7 * (mean_delta + 0.9 * moment)
+        new_output[...] = output[...]
+
+
+def backward(grads, gathered, weight, heads, query, key, value, inverse, cosine, sine, doc_ids, delta, momentum, fragment, output):
+    whole = lambda *shape: pl.BlockSpec(shape, lambda i: (0, 0), pipeline_mode=pl.Buffered(1))
     chunk_of = lambda i: jnp.maximum(i - STEPS, 0)
+    columns = lambda n: pl.BlockSpec((n, CHUNK), lambda i: (0, chunk_of(i)))
     hbm = pl.BlockSpec(memory_space=pl.ANY)
     return pl.pallas_call(
         backward_kernel,
-        grid_spec=pltpu.PrefetchScalarGridSpec(
-            num_scalar_prefetch=1,
-            grid=(STEPS + CHUNKS,),
-            in_specs=[
-                hbm,
-                hbm,
-                whole(256, WIDTH),
-                whole(1024, 256),
-                whole(1024, 256),
-                whole(1024, 128),
-                whole(1024, 128),
-                pl.BlockSpec((8, BLOCK), lambda i, s: (0, place_of(i))),
-                whole(1024, 128),
-                whole(1024, 128),
-                pl.BlockSpec((1, BLOCK), lambda i, s: (0, place_of(i))),
-            ],
-            out_specs=[
-                pl.BlockSpec((4 * CHUNK, 128), lambda i, s: (chunk_of(i), 0)),
-                pl.BlockSpec((256, CHUNK), lambda i, s: (0, chunk_of(i))),
-            ],
-            scratch_shapes=[
-                pltpu.VMEM((1024, WIDTH), jnp.bfloat16),
-                pltpu.VMEM((1024, WIDTH), jnp.bfloat16),
-                pltpu.VMEM((2, STEPS, BLOCK, BLOCK), jnp.float32),
-                pltpu.VMEM((2, STEPS, BLOCK, BLOCK), jnp.float32),
-                pltpu.VMEM((1024, 128), jnp.float32),
-                pltpu.VMEM((1024, 128), jnp.float32),
-                pltpu.VMEM((STEPS, 128, BLOCK), jnp.bfloat16),
-                pltpu.VMEM((1024, 512), jnp.float32),
-                pltpu.VMEM((512, 1024), jnp.bfloat16),
-                pltpu.VMEM((256, 1024), jnp.bfloat16),
-                pltpu.VMEM((4 * CHUNK, 128), jnp.float32),
-                pltpu.SemaphoreType.DMA((2, STEPS)),
-            ],
-        ),
+        grid=(STEPS + CHUNKS,),
+        in_specs=[
+            hbm,
+            hbm,
+            whole(256, WIDTH),
+            whole(1024, 256),
+            whole(1024, 256),
+            whole(1024, 128),
+            whole(1024, 128),
+            pl.BlockSpec((8, BLOCK), lambda i: (0, jnp.minimum(i, STEPS - 1))),
+            whole(1024, 128),
+            whole(1024, 128),
+            whole(8, 128),
+            columns(128),
+            columns(128),
+            columns(128),
+            columns(ROWS),
+        ],
+        out_specs=[
+            pl.BlockSpec((4 * CHUNK, 128), lambda i: (chunk_of(i), 0)),
+            columns(256),
+            columns(128),
+            columns(128),
+            columns(ROWS),
+        ],
+        scratch_shapes=[
+            pltpu.VMEM((1024, WIDTH), jnp.bfloat16),
+            pltpu.VMEM((1024, WIDTH), jnp.bfloat16),
+            pltpu.VMEM((2, STEPS, BLOCK, BLOCK), jnp.float32),
+            pltpu.VMEM((2, STEPS, BLOCK, BLOCK), jnp.float32),
+            pltpu.VMEM((1024, 128), jnp.float32),
+            pltpu.VMEM((1024, 128), jnp.float32),
+            pltpu.VMEM((STEPS, 128, BLOCK), jnp.bfloat16),
+            pltpu.VMEM((1024, 512), jnp.float32),
+            pltpu.VMEM((512, 1024), jnp.bfloat16),
+            pltpu.VMEM((256, 1024), jnp.bfloat16),
+            pltpu.VMEM((4 * CHUNK, 128), jnp.float32),
+            pltpu.VMEM((8, 128), jnp.int32),
+            pltpu.SemaphoreType.DMA((2, STEPS)),
+        ],
         out_shape=[
             jax.ShapeDtypeStruct((4 * WIDTH, 128), jnp.bfloat16),
             jax.ShapeDtypeStruct((256, WIDTH), jnp.bfloat16),
+            jax.ShapeDtypeStruct((128, WIDTH), jnp.float32),
+            jax.ShapeDtypeStruct((128, WIDTH), jnp.float32),
+            jax.ShapeDtypeStruct((ROWS, WIDTH), jnp.bfloat16),
         ],
         compiler_params=pltpu.CompilerParams(vmem_limit_bytes=60 * 2**20),
         name="backward",
-    )(start, grads, gathered, weight, heads, query, key, value, inverse, cosine, sine, start[None, :])
-
-
-def nesterov(mean_delta, moment_part, params_part):
-    moment_next = 0.9 * moment_part + mean_delta
-    return (moment_next, params_part - 0.7 * (mean_delta + 0.9 * moment_next))
-
-
-def over_x(values, step):
-    pairs = [(x * 2 + zh, (x + step) % 4 * 2 + zh) for x in range(4) for zh in range(2)]
-    return lax.ppermute(values, "group", pairs)
-
-
-def delta_over_x(delta):
-    x = lax.axis_index("group") // 2
-    quarter = lambda n: lax.dynamic_slice_in_dim(delta, n % 4 * 32, 32, axis=0)
-    summed = quarter(x).astype(jnp.float32)
-    for step in (1, 2, 3):
-        summed = summed + over_x(quarter(x + step), step).astype(jnp.float32)
-    return summed.astype(jnp.bfloat16)
-
-
-def delta_over_group(summed):
-    x = lax.axis_index("group") // 2
-    other = lax.ppermute(summed, "group", [(g, g ^ 1) for g in range(8)])
-    total = (summed.astype(jnp.float32) + other.astype(jnp.float32)).astype(jnp.bfloat16)
-    quarters = jnp.stack([total] + [over_x(total, step) for step in (1, 2, 3)])
-    ordered = jnp.take(quarters, (x - jnp.arange(4)) % 4, axis=0)
-    return ordered.reshape(128, WIDTH).astype(jnp.float32)
+    )(
+        grads, gathered, weight, heads, query, key, value, inverse, cosine, sine, doc_ids, delta, momentum, fragment, output
+    )
 
 
 def local(
@@ -675,32 +745,20 @@
     momentum,
     fragment,
 ):
-    group = lax.axis_index("group")
-    gathered, wide = gather_normed(tokens, pre_gain[None, :], qkv_weight.reshape(4 * WIDTH, 128))
+    cosine, sine = tables(16 * ROWS, 128)
+    doc_ids = doc_ids.reshape(8, 128)
+    gathered, wide = gather_normed(tokens, pre_gain.reshape(36, 128), qkv_weight.reshape(4 * WIDTH, 128))
     gathered = gathered.reshape(16 * ROWS, WIDTH)
-    delta, gathered = lax.optimization_barrier((outer_delta[0], gathered))
-    summed = delta_over_x(delta)
-    length, width = gathered.shape
-    cosine, sine = tables(length, 128)
-    start = jnp.sum((doc_ids[None, :] < doc_ids[:, None]).astype(jnp.int32), axis=1)
-    query, key, value, head_flat, inverse = forward(
-        gathered, wide, cosine, sine, start
+    query, key, value, heads, inverse = forward(gathered, wide, cosine, sine, doc_ids)
+    out_flat = out_weight.reshape(256, WIDTH)
+    output, grad_rows, delta = middle(
+        heads.reshape(16, ROWS, 256), out_flat, tokens, cotangent, post_gain.reshape(36, 128), outer_delta[0]
     )
-    out_flat = out_weight.reshape(256, width)
-    share = lax.dynamic_slice_in_dim(head_flat.reshape(8, 2, 8, 8, 256), group, 1, axis=2)
-    share = jnp.transpose(share[:, :, 0], (1, 0, 2, 3)).reshape(128, 256)
-    own_tokens = lax.dynamic_slice_in_dim(tokens, group * 8, 8, axis=0).astype(jnp.float32)
-    own_cotangent = lax.dynamic_slice_in_dim(cotangent, group * 8, 8, axis=0).astype(jnp.float32)
-    output, grad_rows = middle(share, out_flat, own_tokens, own_cotangent, post_gain[None, :])
-    grad_rows = grad_rows.reshape(length, width)
-    summed, grad_rows = lax.optimization_barrier((summed, grad_rows))
-    total_delta = delta_over_group(summed)
-    grad_qkv, grad_out = backward(
-        grad_rows, gathered, out_flat, head_flat, query, key, value, inverse, cosine, sine, start
+    grad_qkv, grad_out, new_momentum, new_fragment, output = backward(
+        grad_rows.reshape(16 * ROWS, WIDTH), gathered, out_flat, heads, query, key, value, inverse, cosine, sine,
+        doc_ids, delta.reshape(128, WIDTH), momentum, fragment, output,
     )
-    grad_qkv, grad_out = grad_qkv.reshape(qkv_weight.shape), grad_out.reshape(out_weight.shape)
-    new_momentum, new_fragment = nesterov(total_delta / lax.axis_size("group"), momentum, fragment)
-    return (output, grad_qkv, grad_out, new_momentum, new_fragment)
+    return (output, grad_qkv.reshape(qkv_weight.shape), grad_out.reshape(out_weight.shape), new_momentum, new_fragment)
 
 
 def solution(mesh):

time: 177 us -> 159 us (0.90); the launches traced: 174 us -> 158 us
  Pallas kernels: 145 us -> 158 us
  starting transfers between devices: 9.5 us -> 0 us
  other arithmetic: 8.71 us -> 0 us
  local copies, waits for them, and re-layouts: 5.12 us -> 0 us
  waiting for transfers between devices: 5.1 us -> 0 us
    pallas_call x1, Pallas kernels: 64.7 us -> 76.7 us  [middle(): pl.pallas_call(middle_kernel, out_shape=(jax.ShapeDtypeStruct((ROWS, WIDT...]
    ppermute x7 -> x0, starting transfers between devices: 9.5 us -> none  [the longest x6 7.43 us: over_x(): return lax.ppermute(values, 'group', pairs)]
    sub x1 -> x0, other arithmetic: 5.42 us -> none  [nesterov(): return (moment_next, params_part - 0.7 * (mean_delta + 0.9 * moment_next))]
    ppermute x7 -> x0, waiting for transfers between devices: 5.1 us -> none  [the longest x1 5.09 us: delta_over_group(): other = lax.ppermute(summed, 'group', [(g, g ^ 1) for g in range(8)])]
    broadcast_in_dim x4 -> x0, local copies, waits for them, and re-layouts: 2.12 us -> none  [the longest x1 1.35 us: local(): pre_gain[None, :]]
    convert_element_type x3 -> x0, other arithmetic: 1.87 us -> none  [the longest x1 1.65 us: local(): lax.dynamic_slice_in_dim(cotangent, group * 8, 8, axis=0)]
  transfers between devices with their start and end apart: 7 -> 0, of which waited for: 1 -> 0; matrix products, arithmetic and copies ran while one was open for 3% -> 0% of each run, Pallas kernels for 61% -> 0%
where the time goes in v4:
time: 159 us; the launch traced here: 158 us
  Pallas kernels  158 us (99%)
    pallas_call x1, Pallas kernels, middle(): pl.pallas_call(middle_kernel, out_shape=(jax.ShapeDtypeStruct((ROWS, WIDT...  76.7 us
    pallas_call x1, Pallas kernels, gather_normed(): pl.pallas_call(normed_kernel, out_shape=(jax.ShapeDtypeStruct((16, ROWS,...  38.7 us
    pallas_call x1, Pallas kernels, backward(): pl.pallas_call(backward_kernel, grid=(STEPS + CHUNKS,), in_specs=[hbm, hb...  28 us
    pallas_call x1, Pallas kernels, forward(): pl.pallas_call(forward_kernel, grid=(STEPS,), in_specs=[rows(WIDTH), pl.B...  14.3 us

profile of v4, /device:TPU:1, one launch (start us, length us, event | category | flops | bytes accessed | tf_op | source)
XLA Modules:
  0.0 158.4 jit_solution(988322181005608257)
XLA Ops:
  0.6 38.7 %gather_normed.1 = (bf16[16,64,4608]{2,1,0:T(8,128)(2,1)}, bf16[4608,512]{1,0:T(8,128)(2,1)}) custom-call(bf16[64,4608]{1,0:T(8,128)(2,1)} %tokens.3, f32[36,128]{1,0:T(8,128)} %bitcast.23, bf16[18432,128]{1,0:T(8,128)(2,1)} %bitcast.19), custom_call_target="tpu_custom_call" | custom-call | tf_op jit(solution)/shard_map/gather_normed/pallas_call | solution.py:261
  39.3 14.3 %forward.1 = (bf16[1024,256]{1,0:T(8,128)(2,1)}, bf16[1024,128]{1,0:T(8,128)(2,1)}, bf16[1024,128]{1,0:T(8,128)(2,1)}, f32[1024,256]{1,0:T(8,128)}, f32[8,1024]{1,0:T(8,128)}) custom-call(bf16[1024,4608]{1,0:T(8,128)(2,1)} %bitcast.14, bf16[4608,512]{1,0:T(8,128)(2,1)} %get-tuple-element.21.weight, f32[1024,128]{1,0:T(8,128)} %constant.4.clone.cosine, ...), custom_call_target="tpu_custom_call" | custom-call | tf_op jit(solution)/shard_map/forward/pallas_call | solution.py:551
  53.7 76.7 %middle.1 = (bf16[64,4608]{1,0:T(8,128)(2,1)}, bf16[16,64,4608]{2,1,0:T(8,128)(2,1)}, bf16[4,32,4608]{2,1,0:T(8,128)(2,1)}) custom-call(f32[16,64,256]{2,1,0:T(8,128)} %bitcast.20, bf16[256,4608]{1,0:T(8,128)(2,1)} %bitcast.16, bf16[64,4608]{1,0:T(8,128)(2,1)} %tokens.3, bf16[64,4608]{1,0:T(8,128)(2,1)} %cotangent.1, f32[36,128]{1,0:T(8,128)} %bitcast.24, ...), custom_call_target="tpu_custom_call" | custom-call | tf_op jit(solution)/shard_map/middle/pallas_call | solution.py:417
  130.3 28.0 %backward.1 = (bf16[18432,128]{1,0:T(8,128)(2,1)}, bf16[256,4608]{1,0:T(8,128)(2,1)}, f32[128,4608]{1,0:T(8,128)}, f32[128,4608]{1,0:T(8,128)}, bf16[64,4608]{1,0:T(8,128)(2,1)}) custom-call(bf16[1024,4608]{1,0:T(8,128)(2,1)} %bitcast.18, bf16[1024,4608]{1,0:T(8,128)(2,1)} %bitcast.15, bf16[256,4608]{1,0:T(8,128)(2,1)} %bitcast.17, ...), custom_call_target="tpu_custom_call" | custom-call | tf_op jit(solution)/shard_map/backward/pallas_call | solution.py:680

commit v5 on v4

--- a/solution.py
+++ b/solution.py
@@ -14,8 +14,9 @@
 WIDTH = 4608
 HALF = WIDTH // 2
 ROWS = 64
-FIRST_SPLIT = (10 * 128, 10 * 128, 4 * 128)
-SECOND_SPLIT = (14 * 128, 14 * 128, 2 * 128)
+N1, N2, NQ = 10 * 128, 10 * 128, 4 * 128
+NP = N1 + N2
+REGIONS = {"q": (NP, 4 * NQ), "a": (0, N1), "b": (N1, N2)}
 
 
 def place():
@@ -61,9 +62,7 @@
 SPREAD_SENDS = 69
 
 
-def spread(split, own, full, send, piece_sems, pair_sems, local_sem, work=iter(()), later=None):
-    N1, N2, NQ = split
-    NP = N1 + N2
+def spread(own, full, send, piece_sems, pair_sems, local_sem, work=iter(()), ready=lambda region: None):
     x, zh, zl, y, c = place()
     k, kz = zl * 4 + y, (1 - zl) * 4 + y
     near_k, near_kz = ([b * 4 + (y + s) % 4 for s in (1, 3, 2)] for b in (zl, 1 - zl))
@@ -105,14 +104,17 @@
         for to in links:
             push(kk, t, to)
 
-    keep = pltpu.make_async_copy(own, full.at[2 * k + c], local_sem)
-    keep.start()
+    ready("q")
     push(k, 0, to_z)
     both(k, 0, to_y)
+    ready("a")
     push(k, "a", to_z)
+    ready("b")
     both(k, "b", to_y)
     push(k, "b", to_z)
     both(k, "a", to_y)
+    keep = pltpu.make_async_copy(own, full.at[2 * k + c], local_sem)
+    keep.start()
     send(own, full.at[2 * k + c], pair_sems.at[k, 0], to_sib)
 
     here(kz, 0)
@@ -163,8 +165,6 @@
         for side in range(2):
             here(kk, 1 + side)
             ring(kk, 1 + side, to_x, side)
-    if later is not None:
-        later()
     here(near_k[2], "a", 0)
     here(near_k[2], "a", 1)
     pair(near_k[2], 0, NP, 0)
@@ -241,52 +241,86 @@
 
 
 def normed_kernel(
-    tokens, gain, weight, full, wide, own, rough, mixed, flat,
-    send_sems, piece_sems, pair_sems, local_sem, in_sems, out_sems,
+    tokens, gain, weight, delta, full, wide, delta_part, own, rough, mixed, flat, own_part, parts_in, summed, other,
+    send_sems, piece_sems, pair_sems, local_sem, in_sems, out_sems, delta_sems,
 ):
-    work = weight_parts(weight, wide, rough, mixed, flat, in_sems, out_sems)
+    x, zh, zl, y, c = place()
+    sib = device(x, zh, zl, y, 1 - c)
+    to_x = [device((x + step) % 4, zh, zl, y, c) for step in (1, 2, 3)]
+    to_zh = device(x, 1 - zh, zl, y, c)
+    everyone = near() + [to_x[1], to_zh]
+    rows_of = lambda n: pl.ds(pl.multiple_of(n % 4 * 32, 32), 32)
+    load = pltpu.make_async_copy(delta.at[rows_of(x), :], own_part, delta_sems.at[4])
+    load.start()
+
+    def background():
+        for _ in weight_parts(weight, wide, rough, mixed, flat, in_sems, out_sems):
+            yield
+        load.wait()
+        total = own_part[...].astype(jnp.float32)
+        for n in range(3):
+            send.arrived(parts_in.at[n], delta_sems.at[n], sib)
+            total = total + parts_in[n].astype(jnp.float32)
+        summed[...] = total.astype(jnp.bfloat16)
+        send(summed, other, delta_sems.at[3], to_zh)
+        for _ in range(12):
+            yield
+        send.arrived(other, delta_sems.at[3], sib)
+        delta_part[...] = (summed[...].astype(jnp.float32) + other[...].astype(jnp.float32)).astype(jnp.bfloat16)
+
+    work = background()
     next(work)
-    greet(near())
+    greet(everyone)
     values = tokens[...].astype(jnp.float32)
     scale = lax.rsqrt(jnp.mean(values * values, axis=-1, keepdims=True) + 1e-06)
     own[...] = (values * scale * as_row(gain)).astype(jnp.bfloat16)
-    met(near())
+    met(everyone)
     send = Sender(send_sems)
-    spread(FIRST_SPLIT, own, full, send, piece_sems, pair_sems, local_sem, work)
+    for n, step in enumerate((1, 2, 3)):
+        send(delta.at[rows_of(x + step), :], parts_in.at[n], delta_sems.at[n], to_x[n])
+    spread(own, full, send, piece_sems, pair_sems, local_sem, work)
     send.finish()
 
 
-def gather_normed(tokens, gain, weight):
+def gather_normed(tokens, gain, weight, delta):
     vmem = pl.BlockSpec(memory_space=pltpu.VMEM)
+    hbm = pl.BlockSpec(memory_space=pl.ANY)
     return pl.pallas_call(
         normed_kernel,
         out_shape=(
             jax.ShapeDtypeStruct((16, ROWS, WIDTH), jnp.bfloat16),
             jax.ShapeDtypeStruct((WIDTH, 512), jnp.bfloat16),
+            jax.ShapeDtypeStruct((32, WIDTH), jnp.bfloat16),
         ),
-        in_specs=[vmem, vmem, pl.BlockSpec(memory_space=pl.ANY)],
-        out_specs=(pl.BlockSpec(memory_space=pl.ANY), pl.BlockSpec(memory_space=pl.ANY)),
+        in_specs=[vmem, vmem, hbm, hbm],
+        out_specs=(hbm, hbm, vmem),
         scratch_shapes=[
             pltpu.VMEM((ROWS, WIDTH), jnp.bfloat16),
             pltpu.VMEM((2, 4 * PART, 128), jnp.bfloat16),
             pltpu.VMEM((4 * PART, 128), jnp.float32),
             pltpu.VMEM((2, PART, 512), jnp.bfloat16),
-            pltpu.SemaphoreType.DMA((SPREAD_SENDS,)),
+            pltpu.VMEM((32, WIDTH), jnp.bfloat16),
+            pltpu.VMEM((3, 32, WIDTH), jnp.bfloat16),
+            pltpu.VMEM((32, WIDTH), jnp.bfloat16),
+            pltpu.VMEM((32, WIDTH), jnp.bfloat16),
+            pltpu.SemaphoreType.DMA((4 + SPREAD_SENDS,)),
             pltpu.SemaphoreType.DMA((2, 6, 8)),
             pltpu.SemaphoreType.DMA((8, 2)),
             pltpu.SemaphoreType.DMA,
             pltpu.SemaphoreType.DMA((PARTS,)),
             pltpu.SemaphoreType.DMA((PARTS,)),
+            pltpu.SemaphoreType.DMA((5,)),
         ],
         compiler_params=pltpu.CompilerParams(
             collective_id=0, has_side_effects=True, vmem_limit_bytes=60 * 2**20
         ),
         name="gather_normed",
-    )(tokens, gain, weight)
+    )(tokens, gain, weight, delta)
 
 
 def stacked(rows):
-    return jnp.concatenate([rows[:, :HALF], rows[:, HALF:]], axis=0)
+    half = rows.shape[1] // 2
+    return jnp.concatenate([rows[:, :half], rows[:, half:]], axis=0)
 
 
 def unstacked(rows):
@@ -294,9 +328,9 @@
 
 
 def middle_kernel(
-    heads, weight_hbm, tokens, cotangent, gain, delta, output, full, delta_sum,
-    weight, partial, received, mate, total, mine, group_in, out_in, own, own_part, parts_in, summed, other, delta_total,
-    send_sems, mate_sems, part_sems, group_sems, out_sems, piece_sems, pair_sems, local_sems, delta_sems, sum_sems,
+    heads, weight_hbm, tokens, cotangent, gain, delta_part, output, full, delta_sum,
+    weight, partial, received, mate, total, group_q, group_a, group_b, out_in, own,
+    send_sems, mate_sems, part_sems, group_sems, out_sems, piece_sems, pair_sems, local_sems, sum_sems,
 ):
     x, zh, zl, y, c = place()
     k, g = zl * 4 + y, x * 2 + zh
@@ -308,11 +342,12 @@
     to_kin = [device(a, b, zl, y, c) for a, b in kin]
     to_x = [device((x + step) % 4, zh, zl, y, c) for step in (1, 2, 3)]
     to_zh = device(x, 1 - zh, zl, y, c)
+    group_in = {"q": group_q, "a": group_a, "b": group_b}
     greet([sib] + to_fellows + to_kin)
     load = pltpu.make_async_copy(weight_hbm, weight, local_sems.at[1])
     load.start()
-    load_part = pltpu.make_async_copy(delta.at[pl.ds(pl.multiple_of(x * 32, 32), 32), :], own_part, local_sems.at[2])
-    load_part.start()
+    keep = pltpu.make_async_copy(delta_part, delta_sum.at[x], local_sems.at[2])
+    keep.start()
     share = heads[:, pl.ds(pl.multiple_of(g * 8, 8), 8), :]
     load.wait()
     for core in range(2):
@@ -328,9 +363,8 @@
         kk = a * 4 + b
         send(partial.at[1 - c, kk], mate.at[kk], mate_sems.at[kk], sib)
     send(partial.at[1 - c, k], mate.at[k], mate_sems.at[k], sib)
-    for n, step in enumerate((1, 2, 3)):
-        rows = pl.ds(pl.multiple_of((x + step) % 4 * 32, 32), 32)
-        send(delta.at[rows, :], parts_in.at[n], delta_sems.at[n], to_x[n])
+    for to in (to_x[0], to_x[2]):
+        send(delta_part, delta_sum.at[x], sum_sems.at[0, x], to)
     for (a, b), to in zip(fellows, to_fellows):
         kk = a * 4 + b
         send.arrived(mate.at[kk], mate_sems.at[kk], sib)
@@ -351,54 +385,42 @@
     scale = lax.rsqrt(jnp.mean(attn * attn, axis=-1, keepdims=True) + 1e-06)
     normal = attn * scale
     grad = scale * (dnorm - normal * jnp.mean(dnorm * normal, axis=-1, keepdims=True))
-    mine[...] = stacked(grad).astype(jnp.bfloat16)
-    for to in to_kin:
-        send(mine, group_in.at[g], group_sems.at[g], to)
-    group_in[g] = mine[...]
+    for t, (region, (lo, size)) in enumerate(REGIONS.items()):
+        into = group_in[region]
+        into[g] = stacked(grad[:, lo : lo + size]).astype(jnp.bfloat16)
+        for to in to_kin:
+            send(into.at[g], into.at[g], group_sems.at[t, g], to)
     out_in[zh, x] = stacked(own_tokens + normal * gain_row).astype(jnp.bfloat16)
-    load_part.wait()
-    for n, step in enumerate((1, 2, 3)):
-        send.arrived(parts_in.at[n], delta_sems.at[n], sib)
-    summed[...] = (
-        own_part[...].astype(jnp.float32)
-        + parts_in[0].astype(jnp.float32)
-        + parts_in[1].astype(jnp.float32)
-        + parts_in[2].astype(jnp.float32)
-    ).astype(jnp.bfloat16)
-    for a, b in kin:
-        gg = a * 2 + b
-        send.arrived(group_in.at[gg], group_sems.at[gg], sib)
-    for gg in range(0, 8, 2):
-        first = unstacked(group_in[gg].astype(jnp.float32))
-        second = unstacked(group_in[gg + 1].astype(jnp.float32))
-        own[pl.ds(gg * 8, 16), :] = jnp.concatenate([first, second], axis=0).astype(jnp.bfloat16)
-
-    def later():
-        yield
-        send(summed, other, sum_sems.at[0, 0], to_zh)
-        for n, to in enumerate(to_x):
+    for side, step in enumerate((1, 3)):
+        n = (x + step) % 4
+        send.arrived(delta_sum.at[n], sum_sems.at[0, n], sib)
+        half = delta_sum.at[n, pl.ds(side * 16, 16), :]
+        send(half, half, sum_sems.at[1 + side, n], to_x[2 - 2 * side])
+
+    def ready(region):
+        t, (lo, size) = list(REGIONS).index(region), REGIONS[region]
+        into = group_in[region]
+        for a, b in kin:
+            gg = a * 2 + b
+            send.arrived(into.at[gg], group_sems.at[t, gg], sib)
+        for gg in range(0, 8, 2):
+            first = unstacked(into[gg].astype(jnp.float32))
+            second = unstacked(into[gg + 1].astype(jnp.float32))
+            own[pl.ds(gg * 8, 16), pl.ds(lo, size)] = jnp.concatenate([first, second], axis=0).astype(jnp.bfloat16)
+
+    def background():
+        for _ in range(9):
+            yield
+        for to in to_x:
             send(out_in.at[zh, x], out_in.at[zh, x], out_sems.at[x], to)
         for _ in range(12):
             yield
-        send.arrived(other, sum_sems.at[0, 0], sib)
-        delta_total[...] = (summed[...].astype(jnp.float32) + other[...].astype(jnp.float32)).astype(jnp.bfloat16)
-        for to in (to_x[0], to_x[2]):
-            send(delta_total, delta_sum.at[x], sum_sems.at[1, x], to)
         for step in (1, 2, 3):
             there = out_in.at[zh, (x + step) % 4]
             send.arrived(there, out_sems.at[(x + step) % 4], sib)
         send(out_in.at[zh], out_in.at[zh], out_sems.at[4], to_zh)
-        for _ in range(8):
-            yield
-        for side, step in enumerate((1, 3)):
-            n = (x + step) % 4
-            send.arrived(delta_sum.at[n], sum_sems.at[1, n], sib)
-            half = delta_sum.at[n, pl.ds(side * 16, 16), :]
-            send(half, half, sum_sems.at[2 + side, n], to_x[2 - 2 * side])
-
-    spread(SECOND_SPLIT, own, full, send, piece_sems, pair_sems, local_sems.at[0], later())
-    keep = pltpu.make_async_copy(delta_total, delta_sum.at[x], local_sems.at[1])
-    keep.start()
+
+    spread(own, full, send, piece_sems, pair_sems, local_sems.at[0], background(), ready)
     send.arrived(out_in.at[1 - zh], out_sems.at[4], sib)
     for gg in range(0, 8, 2):
         first = unstacked(out_in[0, gg // 2].astype(jnp.float32))
@@ -406,12 +428,12 @@
         output[pl.ds(gg * 8, 16), :] = jnp.concatenate([first, second], axis=0).astype(jnp.bfloat16)
     n = (x + 2) % 4
     for side in range(2):
-        send.arrived(delta_sum.at[n, pl.ds(side * 16, 16), :], sum_sems.at[2 + side, n], sib)
+        send.arrived(delta_sum.at[n, pl.ds(side * 16, 16), :], sum_sems.at[1 + side, n], sib)
     keep.wait()
     send.finish()
 
 
-def middle(heads, weight, tokens, cotangent, gain, delta):
+def middle(heads, weight, tokens, cotangent, gain, delta_part):
     vmem = pl.BlockSpec(memory_space=pltpu.VMEM)
     hbm = pl.BlockSpec(memory_space=pl.ANY)
     return pl.pallas_call(
@@ -429,31 +451,26 @@
             pltpu.VMEM((8, 16, HALF), jnp.bfloat16),
             pltpu.VMEM((8, 16, HALF), jnp.bfloat16),
             pltpu.VMEM((8, 16, HALF), jnp.bfloat16),
-            pltpu.VMEM((16, HALF), jnp.bfloat16),
-            pltpu.VMEM((8, 16, HALF), jnp.bfloat16),
+            pltpu.VMEM((8, 16, 2 * NQ), jnp.bfloat16),
+            pltpu.VMEM((8, 16, N1 // 2), jnp.bfloat16),
+            pltpu.VMEM((8, 16, N2 // 2), jnp.bfloat16),
             pltpu.VMEM((2, 4, 16, HALF), jnp.bfloat16),
             pltpu.VMEM((ROWS, WIDTH), jnp.bfloat16),
-            pltpu.VMEM((32, WIDTH), jnp.bfloat16),
-            pltpu.VMEM((3, 32, WIDTH), jnp.bfloat16),
-            pltpu.VMEM((32, WIDTH), jnp.bfloat16),
-            pltpu.VMEM((32, WIDTH), jnp.bfloat16),
-            pltpu.VMEM((32, WIDTH), jnp.bfloat16),
-            pltpu.SemaphoreType.DMA((8 + 3 + 7 + 7 + 9 + SPREAD_SENDS,)),
+            pltpu.SemaphoreType.DMA((8 + 2 + 7 + 21 + 2 + 4 + SPREAD_SENDS,)),
             pltpu.SemaphoreType.DMA((8,)),
             pltpu.SemaphoreType.DMA((8,)),
-            pltpu.SemaphoreType.DMA((8,)),
+            pltpu.SemaphoreType.DMA((3, 8)),
             pltpu.SemaphoreType.DMA((5,)),
             pltpu.SemaphoreType.DMA((2, 6, 8)),
             pltpu.SemaphoreType.DMA((8, 2)),
             pltpu.SemaphoreType.DMA((3,)),
-            pltpu.SemaphoreType.DMA((3,)),
-            pltpu.SemaphoreType.DMA((4, 4)),
+            pltpu.SemaphoreType.DMA((3, 4)),
         ],
         compiler_params=pltpu.CompilerParams(
             collective_id=1, has_side_effects=True, vmem_limit_bytes=60 * 2**20
         ),
         name="middle",
-    )(heads, weight, tokens, cotangent, gain, delta)
+    )(heads, weight, tokens, cotangent, gain, delta_part)
 
 
 def tables(length, width):
@@ -747,12 +764,14 @@
 ):
     cosine, sine = tables(16 * ROWS, 128)
     doc_ids = doc_ids.reshape(8, 128)
-    gathered, wide = gather_normed(tokens, pre_gain.reshape(36, 128), qkv_weight.reshape(4 * WIDTH, 128))
+    gathered, wide, delta_part = gather_normed(
+        tokens, pre_gain.reshape(36, 128), qkv_weight.reshape(4 * WIDTH, 128), outer_delta[0]
+    )
     gathered = gathered.reshape(16 * ROWS, WIDTH)
     query, key, value, heads, inverse = forward(gathered, wide, cosine, sine, doc_ids)
     out_flat = out_weight.reshape(256, WIDTH)
     output, grad_rows, delta = middle(
-        heads.reshape(16, ROWS, 256), out_flat, tokens, cotangent, post_gain.reshape(36, 128), outer_delta[0]
+        heads.reshape(16, ROWS, 256), out_flat, tokens, cotangent, post_gain.reshape(36, 128), delta_part
     )
     grad_qkv, grad_out, new_momentum, new_fragment, output = backward(
         grad_rows.reshape(16 * ROWS, WIDTH), gathered, out_flat, heads, query, key, value, inverse, cosine, sine,

time: 159 us -> 147 us (0.925)
  Pallas kernels: 158 us -> 145 us
    pallas_call x1, Pallas kernels: 76.7 us -> 58.1 us  [middle(): pl.pallas_call(middle_kernel, out_shape=(jax.ShapeDtypeStruct((ROWS, WIDT...]
    pallas_call x1, Pallas kernels: 38.7 us -> 44.9 us  [gather_normed(): pl.pallas_call(normed_kernel, out_shape=(jax.ShapeDtypeStruct((16, ROWS,...]
where the time goes in v5:
time: 147 us; the launch traced here: 146 us
  Pallas kernels  145 us (99%)
    pallas_call x1, Pallas kernels, middle(): pl.pallas_call(middle_kernel, out_shape=(jax.ShapeDtypeStruct((ROWS, WIDT...  58.1 us
    pallas_call x1, Pallas kernels, gather_normed(): pl.pallas_call(normed_kernel, out_shape=(jax.ShapeDtypeStruct((16, ROWS,...  44.9 us
    pallas_call x1, Pallas kernels, backward(): pl.pallas_call(backward_kernel, grid=(STEPS + CHUNKS,), in_specs=[hbm, hb...  28 us
    pallas_call x1, Pallas kernels, forward(): pl.pallas_call(forward_kernel, grid=(STEPS,), in_specs=[rows(WIDTH), pl.B...  14.3 us

profile of v5, /device:TPU:1, one launch (start us, length us, event | category | flops | bytes accessed | tf_op | source)
XLA Modules:
  0.0 146.1 jit_solution(3389549705218288161)
XLA Ops:
  0.6 44.9 %gather_normed.1 = (bf16[16,64,4608]{2,1,0:T(8,128)(2,1)}, bf16[4608,512]{1,0:T(8,128)(2,1)}, bf16[32,4608]{1,0:T(8,128)(2,1)}) custom-call(bf16[64,4608]{1,0:T(8,128)(2,1)} %tokens.3, f32[36,128]{1,0:T(8,128)} %bitcast.23, bf16[18432,128]{1,0:T(8,128)(2,1)} %bitcast.19, bf16[128,4608]{1,0:T(8,128)(2,1)} %bitcast.22), custom_call_target="tpu_custom_call" | custom-call | tf_op jit(solution)/shard_map/gather_normed/pallas_call | solution.py:288
  45.6 14.3 %forward.1 = (bf16[1024,256]{1,0:T(8,128)(2,1)}, bf16[1024,128]{1,0:T(8,128)(2,1)}, bf16[1024,128]{1,0:T(8,128)(2,1)}, f32[1024,256]{1,0:T(8,128)}, f32[8,1024]{1,0:T(8,128)}) custom-call(bf16[1024,4608]{1,0:T(8,128)(2,1)} %bitcast.14, bf16[4608,512]{1,0:T(8,128)(2,1)} %get-tuple-element.22.weight, f32[1024,128]{1,0:T(8,128)} %constant.4.clone.cosine, ...), custom_call_target="tpu_custom_call" | custom-call | tf_op jit(solution)/shard_map/forward/pallas_call | solution.py:568
  59.9 58.1 %middle.1 = (bf16[64,4608]{1,0:T(8,128)(2,1)}, bf16[16,64,4608]{2,1,0:T(8,128)(2,1)}, bf16[4,32,4608]{2,1,0:T(8,128)(2,1)}) custom-call(f32[16,64,256]{2,1,0:T(8,128)} %bitcast.20, bf16[256,4608]{1,0:T(8,128)(2,1)} %bitcast.16, bf16[64,4608]{1,0:T(8,128)(2,1)} %tokens.3, bf16[64,4608]{1,0:T(8,128)(2,1)} %cotangent.1, f32[36,128]{1,0:T(8,128)} %bitcast.24, ...), custom_call_target="tpu_custom_call" | custom-call | tf_op jit(solution)/shard_map/middle/pallas_call | solution.py:439
  118.0 28.0 %backward.1 = (bf16[18432,128]{1,0:T(8,128)(2,1)}, bf16[256,4608]{1,0:T(8,128)(2,1)}, f32[128,4608]{1,0:T(8,128)}, f32[128,4608]{1,0:T(8,128)}, bf16[64,4608]{1,0:T(8,128)(2,1)}) custom-call(bf16[1024,4608]{1,0:T(8,128)(2,1)} %bitcast.18, bf16[1024,4608]{1,0:T(8,128)(2,1)} %bitcast.15, bf16[256,4608]{1,0:T(8,128)(2,1)} %bitcast.17, ...), custom_call_target="tpu_custom_call" | custom-call | tf_op jit(solution)/shard_map/backward/pallas_call | solution.py:697

commit v6 on v5

--- a/solution.py
+++ b/solution.py
@@ -192,13 +192,6 @@
     keep.wait()
 
 
-def near():
-    x, zh, zl, y, c = place()
-    out = [device(x, zh, zl, y, 1 - c), device(x, zh, 1 - zl, y, c)]
-    out += [device(x, zh, zl, (y + s) % 4, c) for s in (1, 3)]
-    return out + [device((x + s) % 4, zh, zl, y, c) for s in (1, 3)]
-
-
 def greet(devices):
     barrier = pltpu.get_barrier_semaphore()
     for to in devices:
@@ -209,6 +202,56 @@
     pl.semaphore_wait(pltpu.get_barrier_semaphore(), len(devices))
 
 
+def stacked(rows):
+    half = rows.shape[1] // 2
+    return jnp.concatenate([rows[:, :half], rows[:, half:]], axis=0)
+
+
+def unstacked(rows):
+    return jnp.concatenate([rows[:8], rows[8:]], axis=1)
+
+
+def tables(length, width):
+    half = width // 2
+    positions = np.arange(length, dtype=np.float32)[:, None]
+    freqs = np.power(np.float32(10000.0), -(np.float32(2.0) * np.arange(half, dtype=np.float32) / np.float32(width)))
+    angle = positions * freqs[None, :].astype(np.float32)
+    cosine, sine = np.cos(angle), np.sin(angle)
+    return (
+        jnp.asarray(np.concatenate([cosine, cosine], axis=1)),
+        jnp.asarray(np.concatenate([-sine, sine], axis=1)),
+    )
+
+
+BLOCK = 256
+STEPS = 4
+
+
+def turn(values, cosine, sine):
+    return values * cosine + pltpu.roll(values, 64, 1) * sine
+
+
+def document_starts(doc_ids, starts):
+    ids = doc_ids[...]
+    first = jnp.zeros_like(ids)
+    for n in range(3):
+        first += jnp.where(ids > n, jnp.sum((ids == n).astype(jnp.int32)), 0)
+    starts[...] = first
+
+
+def start_of(starts, i):
+    row = jnp.concatenate([starts[pl.ds(2 * i, 1), :], starts[pl.ds(2 * i + 1, 1), :]], axis=1)
+    return row, jnp.min(row) // BLOCK
+
+
+def scored(keys, queries, first_key, start_row, query_row):
+    raw = lax.dot_general(keys, queries, (((1,), (1,)), ((), ())), preferred_element_type=jnp.float32)
+    soft = jnp.tanh(raw * (query_scale / softcap))
+    row = lax.broadcasted_iota(jnp.int32, raw.shape, 0) + first_key
+    allowed = (row >= start_row) & (row <= query_row)
+    return soft, jnp.where(allowed, jnp.exp(softcap * soft), 0.0)
+
+
 def as_row(gain):
     return jnp.concatenate([gain[n : n + 1, :] for n in range(WIDTH // 128)], axis=1)
 
@@ -217,12 +260,9 @@
 PART = WIDTH // PARTS
 
 
-def weight_parts(weight, wide, rough, mixed, flat, in_sems, out_sems):
+def weight_parts(weight, wide, rough, mixed, in_sems):
     def load(n):
         return pltpu.make_async_copy(weight.at[pl.ds(4 * PART * n, 4 * PART), :], rough.at[n % 2], in_sems.at[n])
-
-    def store(n):
-        return pltpu.make_async_copy(flat.at[n % 2], wide.at[pl.ds(PART * n, PART), :], out_sems.at[n])
 
     load(0).start()
     for n in range(PARTS):
@@ -231,106 +271,17 @@
         yield
         load(n).wait()
         mixed[...] = rough[n % 2].astype(jnp.float32)
-        if n >= 2:
-            store(n - 2).wait()
         for j in range(4):
-            flat[n % 2, :, j * 128 : j * 128 + 128] = mixed[pl.ds(j, PART, stride=4), :].astype(jnp.bfloat16)
-        store(n).start()
-    store(PARTS - 2).wait()
-    store(PARTS - 1).wait()
-
-
-def normed_kernel(
-    tokens, gain, weight, delta, full, wide, delta_part, own, rough, mixed, flat, own_part, parts_in, summed, other,
-    send_sems, piece_sems, pair_sems, local_sem, in_sems, out_sems, delta_sems,
-):
-    x, zh, zl, y, c = place()
-    sib = device(x, zh, zl, y, 1 - c)
-    to_x = [device((x + step) % 4, zh, zl, y, c) for step in (1, 2, 3)]
-    to_zh = device(x, 1 - zh, zl, y, c)
-    everyone = near() + [to_x[1], to_zh]
-    rows_of = lambda n: pl.ds(pl.multiple_of(n % 4 * 32, 32), 32)
-    load = pltpu.make_async_copy(delta.at[rows_of(x), :], own_part, delta_sems.at[4])
-    load.start()
-
-    def background():
-        for _ in weight_parts(weight, wide, rough, mixed, flat, in_sems, out_sems):
-            yield
-        load.wait()
-        total = own_part[...].astype(jnp.float32)
-        for n in range(3):
-            send.arrived(parts_in.at[n], delta_sems.at[n], sib)
-            total = total + parts_in[n].astype(jnp.float32)
-        summed[...] = total.astype(jnp.bfloat16)
-        send(summed, other, delta_sems.at[3], to_zh)
-        for _ in range(12):
-            yield
-        send.arrived(other, delta_sems.at[3], sib)
-        delta_part[...] = (summed[...].astype(jnp.float32) + other[...].astype(jnp.float32)).astype(jnp.bfloat16)
-
-    work = background()
-    next(work)
-    greet(everyone)
-    values = tokens[...].astype(jnp.float32)
-    scale = lax.rsqrt(jnp.mean(values * values, axis=-1, keepdims=True) + 1e-06)
-    own[...] = (values * scale * as_row(gain)).astype(jnp.bfloat16)
-    met(everyone)
-    send = Sender(send_sems)
-    for n, step in enumerate((1, 2, 3)):
-        send(delta.at[rows_of(x + step), :], parts_in.at[n], delta_sems.at[n], to_x[n])
-    spread(own, full, send, piece_sems, pair_sems, local_sem, work)
-    send.finish()
-
-
-def gather_normed(tokens, gain, weight, delta):
-    vmem = pl.BlockSpec(memory_space=pltpu.VMEM)
-    hbm = pl.BlockSpec(memory_space=pl.ANY)
-    return pl.pallas_call(
-        normed_kernel,
-        out_shape=(
-            jax.ShapeDtypeStruct((16, ROWS, WIDTH), jnp.bfloat16),
-            jax.ShapeDtypeStruct((WIDTH, 512), jnp.bfloat16),
-            jax.ShapeDtypeStruct((32, WIDTH), jnp.bfloat16),
-        ),
-        in_specs=[vmem, vmem, hbm, hbm],
-        out_specs=(hbm, hbm, vmem),
-        scratch_shapes=[
-            pltpu.VMEM((ROWS, WIDTH), jnp.bfloat16),
-            pltpu.VMEM((2, 4 * PART, 128), jnp.bfloat16),
-            pltpu.VMEM((4 * PART, 128), jnp.float32),
-            pltpu.VMEM((2, PART, 512), jnp.bfloat16),
-            pltpu.VMEM((32, WIDTH), jnp.bfloat16),
-            pltpu.VMEM((3, 32, WIDTH), jnp.bfloat16),
-            pltpu.VMEM((32, WIDTH), jnp.bfloat16),
-            pltpu.VMEM((32, WIDTH), jnp.bfloat16),
-            pltpu.SemaphoreType.DMA((4 + SPREAD_SENDS,)),
-            pltpu.SemaphoreType.DMA((2, 6, 8)),
-            pltpu.SemaphoreType.DMA((8, 2)),
-            pltpu.SemaphoreType.DMA,
-            pltpu.SemaphoreType.DMA((PARTS,)),
-            pltpu.SemaphoreType.DMA((PARTS,)),
-            pltpu.SemaphoreType.DMA((5,)),
-        ],
-        compiler_params=pltpu.CompilerParams(
-            collective_id=0, has_side_effects=True, vmem_limit_bytes=60 * 2**20
-        ),
-        name="gather_normed",
-    )(tokens, gain, weight, delta)
-
-
-def stacked(rows):
-    half = rows.shape[1] // 2
-    return jnp.concatenate([rows[:, :half], rows[:, half:]], axis=0)
-
-
-def unstacked(rows):
-    return jnp.concatenate([rows[:8], rows[8:]], axis=1)
-
-
-def middle_kernel(
-    heads, weight_hbm, tokens, cotangent, gain, delta_part, output, full, delta_sum,
-    weight, partial, received, mate, total, group_q, group_a, group_b, out_in, own,
-    send_sems, mate_sems, part_sems, group_sems, out_sems, piece_sems, pair_sems, local_sems, sum_sems,
+            wide[pl.ds(PART * n, PART), j * 128 : j * 128 + 128] = mixed[pl.ds(j, PART, stride=4), :].astype(jnp.bfloat16)
+
+
+def front_kernel(
+    tokens, pre_gain, post_gain, qkv_hbm, weight_hbm, doc_ids, cotangent, delta, cosine, sine,
+    output, gathered, full, delta_sum, query_ref, key_ref, value_ref, sums_ref, heads_ref,
+    everything, own, own_grad, wide, rough, mixed, own_part, parts_in, summed, other, delta_part, starts, scores, values_t,
+    weight, partial, received, mate, total, group_q, group_a, group_b, out_in,
+    send_sems, piece_sems, pair_sems, local_sems, in_sems, delta_sems,
+    mate_sems, part_sems, group_sems, out_sems, sum_sems,
 ):
     x, zh, zl, y, c = place()
     k, g = zl * 4 + y, x * 2 + zh
@@ -344,12 +295,69 @@
     to_zh = device(x, 1 - zh, zl, y, c)
     group_in = {"q": group_q, "a": group_a, "b": group_b}
     greet([sib] + to_fellows + to_kin)
-    load = pltpu.make_async_copy(weight_hbm, weight, local_sems.at[1])
-    load.start()
-    keep = pltpu.make_async_copy(delta_part, delta_sum.at[x], local_sems.at[2])
-    keep.start()
-    share = heads[:, pl.ds(pl.multiple_of(g * 8, 8), 8), :]
-    load.wait()
+    send = Sender(send_sems)
+    rows_of = lambda n: pl.ds(pl.multiple_of(n % 4 * 32, 32), 32)
+    load_part = pltpu.make_async_copy(delta.at[rows_of(x), :], own_part, delta_sems.at[4])
+    load_part.start()
+
+    def background():
+        for _ in weight_parts(qkv_hbm, wide, rough, mixed, in_sems):
+            yield
+        load_weight.start()
+        for _ in range(12):
+            yield
+        for n, step in enumerate((1, 2, 3)):
+            send(delta.at[rows_of(x + step), :], parts_in.at[n], delta_sems.at[n], to_x[n])
+
+    load_weight = pltpu.make_async_copy(weight_hbm, weight, local_sems.at[1])
+    work = background()
+    next(work)
+    values = tokens[...].astype(jnp.float32)
+    scale = lax.rsqrt(jnp.mean(values * values, axis=-1, keepdims=True) + 1e-06)
+    own[...] = (values * scale * as_row(pre_gain)).astype(jnp.bfloat16)
+    document_starts(doc_ids, starts)
+    met([sib] + to_fellows + to_kin)
+    spread(own, everything, send, piece_sems.at[0], pair_sems.at[0], local_sems.at[0], work)
+    store = pltpu.make_async_copy(everything, gathered, local_sems.at[3])
+    store.start()
+
+    for i in range(STEPS):
+        at = pl.ds(i * BLOCK, BLOCK)
+        rows = everything[pl.ds(4 * i, 4)].reshape(BLOCK, WIDTH)
+        proj = jnp.dot(rows, wide[...], preferred_element_type=jnp.float32)
+        queries = [turn(proj[:, h * 128 : h * 128 + 128], cosine[at, :], sine[at, :]).astype(jnp.bfloat16) for h in range(2)]
+        query_ref[at, :128] = queries[0]
+        query_ref[at, 128:] = queries[1]
+        key_ref[at, :] = turn(proj[:, 256:384], cosine[at, :], sine[at, :]).astype(jnp.bfloat16)
+        value_ref[at, :] = proj[:, 384:].astype(jnp.bfloat16)
+        values_t[i] = proj[:, 384:].T.astype(jnp.bfloat16)
+        start_row, _ = start_of(starts, i)
+        query_row = lax.broadcasted_iota(jnp.int32, (1, BLOCK), 1) + i * BLOCK
+        blocks = range(max(0, i - 2), i + 1)
+        for h in range(2):
+            sums = jnp.zeros((1, BLOCK), jnp.float32)
+            for n, j in enumerate(blocks):
+                _, e = scored(key_ref[j * BLOCK : j * BLOCK + BLOCK, :], queries[h], j * BLOCK, start_row, query_row)
+                scores[h, n] = e
+                sums = sums + jnp.sum(e, axis=0, keepdims=True)
+            inverse = 1.0 / sums
+            sums_ref[h : h + 1, at] = inverse
+            acc = jnp.zeros((128, BLOCK), jnp.float32)
+            for n, j in enumerate(blocks):
+                p = (scores[h, n] * inverse).astype(jnp.bfloat16)
+                acc = acc + jnp.dot(values_t[j], p, preferred_element_type=jnp.float32)
+            heads_ref[pl.ds(4 * i, 4), :, h * 128 : h * 128 + 128] = acc.T.reshape(4, ROWS, 128)
+        if i == 2:
+            load_part.wait()
+            delta_total = own_part[...].astype(jnp.float32)
+            for n in range(3):
+                send.arrived(parts_in.at[n], delta_sems.at[n], sib)
+                delta_total = delta_total + parts_in[n].astype(jnp.float32)
+            summed[...] = delta_total.astype(jnp.bfloat16)
+            send(summed, other, delta_sems.at[3], to_zh)
+
+    share = heads_ref[:, pl.ds(pl.multiple_of(g * 8, 8), 8), :]
+    load_weight.wait()
     for core in range(2):
         rows = jnp.concatenate([share[2 * kk + core] for kk in range(8)], axis=0).astype(jnp.bfloat16)
         left = jnp.dot(rows, weight[:, :HALF], preferred_element_type=jnp.float32)
@@ -357,12 +365,14 @@
         for kk in range(8):
             both = jnp.concatenate([left[kk * 8 : kk * 8 + 8], right[kk * 8 : kk * 8 + 8]], axis=0)
             partial[core, kk] = both.astype(jnp.bfloat16)
-    met([sib] + to_fellows + to_kin)
-    send = Sender(send_sems)
     for n, (a, b) in enumerate(fellows):
         kk = a * 4 + b
         send(partial.at[1 - c, kk], mate.at[kk], mate_sems.at[kk], sib)
     send(partial.at[1 - c, k], mate.at[k], mate_sems.at[k], sib)
+    send.arrived(other, delta_sems.at[3], sib)
+    delta_part[...] = (summed[...].astype(jnp.float32) + other[...].astype(jnp.float32)).astype(jnp.bfloat16)
+    keep = pltpu.make_async_copy(delta_part, delta_sum.at[x], local_sems.at[2])
+    keep.start()
     for to in (to_x[0], to_x[2]):
         send(delta_part, delta_sum.at[x], sum_sems.at[0, x], to)
     for (a, b), to in zip(fellows, to_fellows):
@@ -372,7 +382,7 @@
         send(total.at[kk], received.at[k], part_sems.at[k], to)
     send.arrived(mate.at[k], mate_sems.at[k], sib)
     both = partial[c, k].astype(jnp.float32) + mate[k].astype(jnp.float32)
-    gain_row = as_row(gain)
+    gain_row = as_row(post_gain)
     pick = lambda rows: jnp.where(g % 2 == 0, rows[:8], rows[8:])
     near_rows = pl.ds(pl.multiple_of(g // 2 * 16, 16), 16)
     own_tokens = pick(tokens[near_rows, :].astype(jnp.float32))
@@ -406,9 +416,9 @@
         for gg in range(0, 8, 2):
             first = unstacked(into[gg].astype(jnp.float32))
             second = unstacked(into[gg + 1].astype(jnp.float32))
-            own[pl.ds(gg * 8, 16), pl.ds(lo, size)] = jnp.concatenate([first, second], axis=0).astype(jnp.bfloat16)
-
-    def background():
+            own_grad[pl.ds(gg * 8, 16), pl.ds(lo, size)] = jnp.concatenate([first, second], axis=0).astype(jnp.bfloat16)
+
+    def returning():
         for _ in range(9):
             yield
         for to in to_x:
@@ -420,7 +430,7 @@
             send.arrived(there, out_sems.at[(x + step) % 4], sib)
         send(out_in.at[zh], out_in.at[zh], out_sems.at[4], to_zh)
 
-    spread(own, full, send, piece_sems, pair_sems, local_sems.at[0], background(), ready)
+    spread(own_grad, full, send, piece_sems.at[1], pair_sems.at[1], local_sems.at[0], returning(), ready)
     send.arrived(out_in.at[1 - zh], out_sems.at[4], sib)
     for gg in range(0, 8, 2):
         first = unstacked(out_in[0, gg // 2].astype(jnp.float32))
@@ -430,168 +440,71 @@
     for side in range(2):
         send.arrived(delta_sum.at[n, pl.ds(side * 16, 16), :], sum_sems.at[1 + side, n], sib)
     keep.wait()
+    store.wait()
     send.finish()
 
 
-def middle(heads, weight, tokens, cotangent, gain, delta_part):
+def front(tokens, pre_gain, post_gain, qkv_weight, weight, doc_ids, cotangent, delta, cosine, sine):
     vmem = pl.BlockSpec(memory_space=pltpu.VMEM)
     hbm = pl.BlockSpec(memory_space=pl.ANY)
+    shape = jax.ShapeDtypeStruct
+    bf16, f32 = jnp.bfloat16, jnp.float32
     return pl.pallas_call(
-        middle_kernel,
+        front_kernel,
         out_shape=(
-            jax.ShapeDtypeStruct((ROWS, WIDTH), jnp.bfloat16),
-            jax.ShapeDtypeStruct((16, ROWS, WIDTH), jnp.bfloat16),
-            jax.ShapeDtypeStruct((4, 32, WIDTH), jnp.bfloat16),
+            shape((ROWS, WIDTH), bf16),
+            shape((16, ROWS, WIDTH), bf16),
+            shape((16, ROWS, WIDTH), bf16),
+            shape((4, 32, WIDTH), bf16),
+            shape((1024, 256), bf16),
+            shape((1024, 128), bf16),
+            shape((1024, 128), bf16),
+            shape((8, 1024), f32),
+            shape((16, ROWS, 256), f32),
         ),
-        in_specs=[vmem, hbm, vmem, vmem, vmem, hbm],
-        out_specs=(vmem, hbm, hbm),
+        in_specs=[vmem, vmem, vmem, hbm, hbm, vmem, vmem, hbm, vmem, vmem],
+        out_specs=(vmem, hbm, hbm, hbm, vmem, vmem, vmem, vmem, vmem),
         scratch_shapes=[
-            pltpu.VMEM((256, WIDTH), jnp.bfloat16),
-            pltpu.VMEM((2, 8, 16, HALF), jnp.bfloat16),
-            pltpu.VMEM((8, 16, HALF), jnp.bfloat16),
-            pltpu.VMEM((8, 16, HALF), jnp.bfloat16),
-            pltpu.VMEM((8, 16, HALF), jnp.bfloat16),
-            pltpu.VMEM((8, 16, 2 * NQ), jnp.bfloat16),
-            pltpu.VMEM((8, 16, N1 // 2), jnp.bfloat16),
-            pltpu.VMEM((8, 16, N2 // 2), jnp.bfloat16),
-            pltpu.VMEM((2, 4, 16, HALF), jnp.bfloat16),
-            pltpu.VMEM((ROWS, WIDTH), jnp.bfloat16),
-            pltpu.SemaphoreType.DMA((8 + 2 + 7 + 21 + 2 + 4 + SPREAD_SENDS,)),
+            pltpu.VMEM((16, ROWS, WIDTH), bf16),
+            pltpu.VMEM((ROWS, WIDTH), bf16),
+            pltpu.VMEM((ROWS, WIDTH), bf16),
+            pltpu.VMEM((WIDTH, 512), bf16),
+            pltpu.VMEM((2, 4 * PART, 128), bf16),
+            pltpu.VMEM((4 * PART, 128), f32),
+            pltpu.VMEM((32, WIDTH), bf16),
+            pltpu.VMEM((3, 32, WIDTH), bf16),
+            pltpu.VMEM((32, WIDTH), bf16),
+            pltpu.VMEM((32, WIDTH), bf16),
+            pltpu.VMEM((32, WIDTH), bf16),
+            pltpu.VMEM((8, 128), jnp.int32),
+            pltpu.VMEM((2, 3, BLOCK, BLOCK), f32),
+            pltpu.VMEM((STEPS, 128, BLOCK), bf16),
+            pltpu.VMEM((256, WIDTH), bf16),
+            pltpu.VMEM((2, 8, 16, HALF), bf16),
+            pltpu.VMEM((8, 16, HALF), bf16),
+            pltpu.VMEM((8, 16, HALF), bf16),
+            pltpu.VMEM((8, 16, HALF), bf16),
+            pltpu.VMEM((8, 16, 2 * NQ), bf16),
+            pltpu.VMEM((8, 16, N1 // 2), bf16),
+            pltpu.VMEM((8, 16, N2 // 2), bf16),
+            pltpu.VMEM((2, 4, 16, HALF), bf16),
+            pltpu.SemaphoreType.DMA((4 + 8 + 2 + 7 + 21 + 2 + 4 + 2 * SPREAD_SENDS,)),
+            pltpu.SemaphoreType.DMA((2, 2, 6, 8)),
+            pltpu.SemaphoreType.DMA((2, 8, 2)),
+            pltpu.SemaphoreType.DMA((4,)),
+            pltpu.SemaphoreType.DMA((PARTS,)),
+            pltpu.SemaphoreType.DMA((5,)),
             pltpu.SemaphoreType.DMA((8,)),
             pltpu.SemaphoreType.DMA((8,)),
             pltpu.SemaphoreType.DMA((3, 8)),
             pltpu.SemaphoreType.DMA((5,)),
-            pltpu.SemaphoreType.DMA((2, 6, 8)),
-            pltpu.SemaphoreType.DMA((8, 2)),
-            pltpu.SemaphoreType.DMA((3,)),
             pltpu.SemaphoreType.DMA((3, 4)),
         ],
         compiler_params=pltpu.CompilerParams(
-            collective_id=1, has_side_effects=True, vmem_limit_bytes=60 * 2**20
+            collective_id=0, has_side_effects=True, vmem_limit_bytes=60 * 2**20
         ),
-        name="middle",
-    )(heads, weight, tokens, cotangent, gain, delta_part)
-
-
-def tables(length, width):
-    half = width // 2
-    positions = np.arange(length, dtype=np.float32)[:, None]
-    freqs = np.power(np.float32(10000.0), -(np.float32(2.0) * np.arange(half, dtype=np.float32) / np.float32(width)))
-    angle = positions * freqs[None, :].astype(np.float32)
-    cosine, sine = np.cos(angle), np.sin(angle)
-    return (
-        jnp.asarray(np.concatenate([cosine, cosine], axis=1)),
-        jnp.asarray(np.concatenate([-sine, sine], axis=1)),
-    )
-
-
-BLOCK = 256
-STEPS = 4
-
-
-def turn(values, cosine, sine):
-    return values * cosine + pltpu.roll(values, 64, 1) * sine
-
-
-def document_starts(doc_ids, starts):
-    ids = doc_ids[...]
-    first = jnp.zeros_like(ids)
-    for n in range(3):
-        first += jnp.where(ids > n, jnp.sum((ids == n).astype(jnp.int32)), 0)
-    starts[...] = first
-
-
-def start_of(starts, i):
-    row = jnp.concatenate([starts[pl.ds(2 * i, 1), :], starts[pl.ds(2 * i + 1, 1), :]], axis=1)
-    return row, jnp.min(row) // BLOCK
-
-
-def scored(keys, queries, first_key, start_row, query_row):
-    raw = lax.dot_general(keys, queries, (((1,), (1,)), ((), ())), preferred_element_type=jnp.float32)
-    soft = jnp.tanh(raw * (query_scale / softcap))
-    row = lax.broadcasted_iota(jnp.int32, raw.shape, 0) + first_key
-    allowed = (row >= start_row) & (row <= query_row)
-    return soft, jnp.where(allowed, jnp.exp(softcap * soft), 0.0)
-
-
-def forward_kernel(
-    x, weight, cosine, sine, doc_ids, query_ref, key_ref, value_ref, heads_ref, sums_ref, keep, keys, values_t, starts
-):
-    i = pl.program_id(0)
-
-    @pl.when(i == 0)
-    def _():
-        document_starts(doc_ids, starts)
-
-    proj = jnp.dot(x[...], weight[...], preferred_element_type=jnp.float32)
-    queries = [turn(proj[:, h * 128 : h * 128 + 128], cosine[...], sine[...]).astype(jnp.bfloat16) for h in range(2)]
-    key = turn(proj[:, 256:384], cosine[...], sine[...]).astype(jnp.bfloat16)
-    value = proj[:, 384:512]
-    query_ref[:, :128] = queries[0]
-    query_ref[:, 128:] = queries[1]
-    key_ref[...] = key
-    value_ref[...] = value.astype(jnp.bfloat16)
-    keys[i] = key
-    values_t[i] = value.T.astype(jnp.bfloat16)
-    start_row, first = start_of(starts, i)
-    query_row = lax.broadcasted_iota(jnp.int32, (1, BLOCK), 1) + i * BLOCK
-
-    def score(j, sums):
-        out = []
-        for h in range(2):
-            _, e = scored(keys[j], queries[h], j * BLOCK, start_row, query_row)
-            keep[h, j] = e
-            out.append(sums[h] + jnp.sum(e, axis=0, keepdims=True))
-        return tuple(out)
-
-    zero = jnp.zeros((1, BLOCK), jnp.float32)
-    sums = lax.fori_loop(first, i + 1, score, (zero, zero))
-    inverse = [1.0 / s for s in sums]
-    sums_ref[0:1, :] = inverse[0]
-    sums_ref[1:2, :] = inverse[1]
-
-    def mix(j, accs):
-        out = []
-        for h in range(2):
-            p = (keep[h, j] * inverse[h]).astype(jnp.bfloat16)
-            out.append(accs[h] + jnp.dot(values_t[j], p, preferred_element_type=jnp.float32))
-        return tuple(out)
-
-    zero = jnp.zeros((128, BLOCK), jnp.float32)
-    accs = lax.fori_loop(first, i + 1, mix, (zero, zero))
-    for h in range(2):
-        heads_ref[:, h * 128 : h * 128 + 128] = accs[h].T
-
-
-def forward(gathered, weight, cosine, sine, doc_ids):
-    rows = lambda n: pl.BlockSpec((BLOCK, n), lambda i: (i, 0))
-    return pl.pallas_call(
-        forward_kernel,
-        grid=(STEPS,),
-        in_specs=[
-            rows(WIDTH),
-            pl.BlockSpec((WIDTH, 512), lambda i: (0, 0), pipeline_mode=pl.Buffered(1)),
-            rows(128),
-            rows(128),
-            pl.BlockSpec((8, 128), lambda i: (0, 0)),
-        ],
-        out_specs=[rows(256), rows(128), rows(128), rows(256), pl.BlockSpec((8, BLOCK), lambda i: (0, i))],
-        scratch_shapes=[
-            pltpu.VMEM((2, STEPS, BLOCK, BLOCK), jnp.float32),
-            pltpu.VMEM((STEPS, BLOCK, 128), jnp.bfloat16),
-            pltpu.VMEM((STEPS, 128, BLOCK), jnp.bfloat16),
-            pltpu.VMEM((8, 128), jnp.int32),
-        ],
-        out_shape=[
-            jax.ShapeDtypeStruct((1024, 256), jnp.bfloat16),
-            jax.ShapeDtypeStruct((1024, 128), jnp.bfloat16),
-            jax.ShapeDtypeStruct((1024, 128), jnp.bfloat16),
-            jax.ShapeDtypeStruct((1024, 256), jnp.float32),
-            jax.ShapeDtypeStruct((8, 1024), jnp.float32),
-        ],
-        compiler_params=pltpu.CompilerParams(vmem_limit_bytes=60 * 2**20),
-        name="forward",
-    )(gathered, weight, cosine, sine, doc_ids)
+        name="front",
+    )(tokens, pre_gain, post_gain, qkv_weight, weight, doc_ids, cotangent, delta, cosine, sine)
 
 
 CHUNK = 512
@@ -764,15 +677,12 @@
 ):
     cosine, sine = tables(16 * ROWS, 128)
     doc_ids = doc_ids.reshape(8, 128)
-    gathered, wide, delta_part = gather_normed(
-        tokens, pre_gain.reshape(36, 128), qkv_weight.reshape(4 * WIDTH, 128), outer_delta[0]
+    out_flat = out_weight.reshape(256, WIDTH)
+    output, gathered, grad_rows, delta, query, key, value, inverse, heads = front(
+        tokens, pre_gain.reshape(36, 128), post_gain.reshape(36, 128), qkv_weight.reshape(4 * WIDTH, 128), out_flat,
+        doc_ids, cotangent, outer_delta[0], cosine, sine,
     )
-    gathered = gathered.reshape(16 * ROWS, WIDTH)
-    query, key, value, heads, inverse = forward(gathered, wide, cosine, sine, doc_ids)
-    out_flat = out_weight.reshape(256, WIDTH)
-    output, grad_rows, delta = middle(
-        heads.reshape(16, ROWS, 256), out_flat, tokens, cotangent, post_gain.reshape(36, 128), delta_part
-    )
+    gathered, heads = gathered.reshape(16 * ROWS, WIDTH), heads.reshape(16 * ROWS, 256)
     grad_qkv, grad_out, new_momentum, new_fragment, output = backward(
         grad_rows.reshape(16 * ROWS, WIDTH), gathered, out_flat, heads, query, key, value, inverse, cosine, sine,
         doc_ids, delta.reshape(128, WIDTH), momentum, fragment, output,

time: 147 us -> 149 us (1.014)
  Pallas kernels: 145 us -> 148 us
    pallas_call x3 -> x1, Pallas kernels: 117 us -> 120 us  [front(): pl.pallas_call(front_kernel, out_shape=(shape((ROWS, WIDTH), bf16), shape...]
where the time goes in v6:
time: 149 us
  Pallas kernels  148 us (99%)
    pallas_call x1, Pallas kernels, front(): pl.pallas_call(front_kernel, out_shape=(shape((ROWS, WIDTH), bf16), shape...  120 us
    pallas_call x1, Pallas kernels, backward(): pl.pallas_call(backward_kernel, grid=(STEPS + CHUNKS,), in_specs=[hbm, hb...  28 us

profile of v6, /device:TPU:1, one launch (start us, length us, event | category | flops | bytes accessed | tf_op | source)
XLA Modules:
  0.0 148.9 jit_solution(7948502188835594649)
XLA Ops:
  0.6 120.1 %front.1 = (bf16[64,4608]{1,0:T(8,128)(2,1)}, bf16[16,64,4608]{2,1,0:T(8,128)(2,1)}, bf16[16,64,4608]{2,1,0:T(8,128)(2,1)}, bf16[4,32,4608]{2,1,0:T(8,128)(2,1)}...) custom-call(bf16[64,4608]{1,0:T(8,128)(2,1)} %tokens.1, ...), custom_call_target="tpu_custom_call" | custom-call | tf_op jit(solution)/shard_map/front/pallas_call | solution.py:452
  120.7 28.0 %backward.1 = (bf16[18432,128]{1,0:T(8,128)(2,1)}, bf16[256,4608]{1,0:T(8,128)(2,1)}, f32[128,4608]{1,0:T(8,128)}, f32[128,4608]{1,0:T(8,128)}, bf16[64,4608]{1,0:T(8,128)(2,1)}) custom-call(bf16[1024,4608]{1,0:T(8,128)(2,1)} %bitcast.15, bf16[1024,4608]{1,0:T(8,128)(2,1)} %bitcast.14, bf16[256,4608]{1,0:T(8,128)(2,1)} %bitcast.17, f32[1024,256]{1,0:T(8,128)} %bitcast.21, ...), custom_call_target="tpu_custom_call" | custom-call | tf_op jit(solution)/shard_map/backward/pallas_call | solution.py:610

commit v7 on v6

--- a/solution.py
+++ b/solution.py
@@ -304,10 +304,6 @@
         for _ in weight_parts(qkv_hbm, wide, rough, mixed, in_sems):
             yield
         load_weight.start()
-        for _ in range(12):
-            yield
-        for n, step in enumerate((1, 2, 3)):
-            send(delta.at[rows_of(x + step), :], parts_in.at[n], delta_sems.at[n], to_x[n])
 
     load_weight = pltpu.make_async_copy(weight_hbm, weight, local_sems.at[1])
     work = background()
@@ -317,6 +313,8 @@
     own[...] = (values * scale * as_row(pre_gain)).astype(jnp.bfloat16)
     document_starts(doc_ids, starts)
     met([sib] + to_fellows + to_kin)
+    for n, step in enumerate((1, 2, 3)):
+        send(delta.at[rows_of(x + step), :], parts_in.at[n], delta_sems.at[n], to_x[n])
     spread(own, everything, send, piece_sems.at[0], pair_sems.at[0], local_sems.at[0], work)
     store = pltpu.make_async_copy(everything, gathered, local_sems.at[3])
     store.start()
@@ -347,7 +345,7 @@
                 p = (scores[h, n] * inverse).astype(jnp.bfloat16)
                 acc = acc + jnp.dot(values_t[j], p, preferred_element_type=jnp.float32)
             heads_ref[pl.ds(4 * i, 4), :, h * 128 : h * 128 + 128] = acc.T.reshape(4, ROWS, 128)
-        if i == 2:
+        if i == 0:
             load_part.wait()
             delta_total = own_part[...].astype(jnp.float32)
             for n in range(3):
@@ -369,12 +367,6 @@
         kk = a * 4 + b
         send(partial.at[1 - c, kk], mate.at[kk], mate_sems.at[kk], sib)
     send(partial.at[1 - c, k], mate.at[k], mate_sems.at[k], sib)
-    send.arrived(other, delta_sems.at[3], sib)
-    delta_part[...] = (summed[...].astype(jnp.float32) + other[...].astype(jnp.float32)).astype(jnp.bfloat16)
-    keep = pltpu.make_async_copy(delta_part, delta_sum.at[x], local_sems.at[2])
-    keep.start()
-    for to in (to_x[0], to_x[2]):
-        send(delta_part, delta_sum.at[x], sum_sems.at[0, x], to)
     for (a, b), to in zip(fellows, to_fellows):
         kk = a * 4 + b
         send.arrived(mate.at[kk], mate_sems.at[kk], sib)
@@ -382,6 +374,12 @@
         send(total.at[kk], received.at[k], part_sems.at[k], to)
     send.arrived(mate.at[k], mate_sems.at[k], sib)
     both = partial[c, k].astype(jnp.float32) + mate[k].astype(jnp.float32)
+    send.arrived(other, delta_sems.at[3], sib)
+    delta_part[...] = (summed[...].astype(jnp.float32) + other[...].astype(jnp.float32)).astype(jnp.bfloat16)
+    keep = pltpu.make_async_copy(delta_part, delta_sum.at[x], local_sems.at[2])
+    keep.start()
+    for to in (to_x[0], to_x[2]):
+        send(delta_part, delta_sum.at[x], sum_sems.at[0, x], to)
     gain_row = as_row(post_gain)
     pick = lambda rows: jnp.where(g % 2 == 0, rows[:8], rows[8:])
     near_rows = pl.ds(pl.multiple_of(g // 2 * 16, 16), 16)
@@ -507,7 +505,7 @@
     )(tokens, pre_gain, post_gain, qkv_weight, weight, doc_ids, cotangent, delta, cosine, sine)
 
 
-CHUNK = 512
+CHUNK = 768
 CHUNKS = WIDTH // CHUNK
 
 
@@ -595,6 +593,9 @@
             mixed[pl.ds(j, CHUNK, stride=4), :] = part.T
         out_out[...] = jnp.dot(heads_t[...], grads[:, at], preferred_element_type=jnp.float32).astype(jnp.bfloat16)
         qkv_out[...] = mixed[...].astype(jnp.bfloat16)
+
+    @pl.when((i >= 1) & (i <= CHUNKS))
+    def _():
         mean_delta = delta[...].astype(jnp.float32) / 8.0
         moment = 0.9 * momentum[...] + mean_delta
         new_momentum[...] = moment
@@ -606,6 +607,7 @@
     whole = lambda *shape: pl.BlockSpec(shape, lambda i: (0, 0), pipeline_mode=pl.Buffered(1))
     chunk_of = lambda i: jnp.maximum(i - STEPS, 0)
     columns = lambda n: pl.BlockSpec((n, CHUNK), lambda i: (0, chunk_of(i)))
+    early = lambda n: pl.BlockSpec((n, CHUNK), lambda i: (0, jnp.clip(i - 1, 0, CHUNKS - 1)))
     hbm = pl.BlockSpec(memory_space=pl.ANY)
     return pl.pallas_call(
         backward_kernel,
@@ -622,17 +624,17 @@
             whole(1024, 128),
             whole(1024, 128),
             whole(8, 128),
-            columns(128),
-            columns(128),
-            columns(128),
-            columns(ROWS),
+            early(128),
+            early(128),
+            early(128),
+            early(ROWS),
         ],
         out_specs=[
             pl.BlockSpec((4 * CHUNK, 128), lambda i: (chunk_of(i), 0)),
             columns(256),
-            columns(128),
-            columns(128),
-            columns(ROWS),
+            early(128),
+            early(128),
+            early(ROWS),
         ],
         scratch_shapes=[
             pltpu.VMEM((1024, WIDTH), jnp.bfloat16),

time: 149 us -> 133 us (0.89)
  Pallas kernels: 148 us -> 132 us
    pallas_call x1, Pallas kernels: 120 us -> 105 us  [front(): pl.pallas_call(front_kernel, out_shape=(shape((ROWS, WIDTH), bf16), shape...]
where the time goes in v7:
time: 133 us
  Pallas kernels  132 us (99%)
    pallas_call x1, Pallas kernels, front(): pl.pallas_call(front_kernel, out_shape=(shape((ROWS, WIDTH), bf16), shape...  105 us
    pallas_call x1, Pallas kernels, backward(): pl.pallas_call(backward_kernel, grid=(STEPS + CHUNKS,), in_specs=[hbm, hb...  27.2 us

profile of v7, /device:TPU:1, one launch (start us, length us, event | category | flops | bytes accessed | tf_op | source)
XLA Modules:
  0.0 132.8 jit_solution(2806128542185951857)
XLA Ops:
  0.6 104.7 %front.1 = (bf16[64,4608]{1,0:T(8,128)(2,1)}, bf16[16,64,4608]{2,1,0:T(8,128)(2,1)}, bf16[16,64,4608]{2,1,0:T(8,128)(2,1)}, bf16[4,32,4608]{2,1,0:T(8,128)(2,1)}...) custom-call(bf16[64,4608]{1,0:T(8,128)(2,1)} %tokens.1, ...), custom_call_target="tpu_custom_call" | custom-call | tf_op jit(solution)/shard_map/front/pallas_call | solution.py:450
  105.4 27.2 %backward.1 = (bf16[18432,128]{1,0:T(8,128)(2,1)}, bf16[256,4608]{1,0:T(8,128)(2,1)}, f32[128,4608]{1,0:T(8,128)}, f32[128,4608]{1,0:T(8,128)}, bf16[64,4608]{1,0:T(8,128)(2,1)}) custom-call(bf16[1024,4608]{1,0:T(8,128)(2,1)} %bitcast.15, bf16[1024,4608]{1,0:T(8,128)(2,1)} %bitcast.14, bf16[256,4608]{1,0:T(8,128)(2,1)} %bitcast.17, f32[1024,256]{1,0:T(8,128)} %bitcast.21, ...), custom_call_target="tpu_custom_call" | custom-call | tf_op jit(solution)/shard_map/backward/pallas_call | solution.py:612

commit v8 on v7

--- a/solution.py
+++ b/solution.py
@@ -240,8 +240,7 @@
 
 
 def start_of(starts, i):
-    row = jnp.concatenate([starts[pl.ds(2 * i, 1), :], starts[pl.ds(2 * i + 1, 1), :]], axis=1)
-    return row, jnp.min(row) // BLOCK
+    return jnp.concatenate([starts[2 * i : 2 * i + 1, :], starts[2 * i + 1 : 2 * i + 2, :]], axis=1)
 
 
 def scored(keys, queries, first_key, start_row, query_row):
@@ -275,10 +274,14 @@
             wide[pl.ds(PART * n, PART), j * 128 : j * 128 + 128] = mixed[pl.ds(j, PART, stride=4), :].astype(jnp.bfloat16)
 
 
+KEPT = (0, 256, 768, 1536, 2304)
+
+
 def front_kernel(
     tokens, pre_gain, post_gain, qkv_hbm, weight_hbm, doc_ids, cotangent, delta, cosine, sine,
-    output, gathered, full, delta_sum, query_ref, key_ref, value_ref, sums_ref, heads_ref,
-    everything, own, own_grad, wide, rough, mixed, own_part, parts_in, summed, other, delta_part, starts, scores, values_t,
+    output, gathered, delta_sum, grad_proj_t, grad_out,
+    query_ref, key_ref, value_ref, heads_ref, full, probs, slopes, keys_t, dkey, dvalue, grad_proj, out_grad, weight_t,
+    everything, own, own_grad, wide, rough, mixed, own_part, parts_in, summed, other, delta_part, starts, values_t,
     weight, partial, received, mate, total, group_q, group_a, group_b, out_in,
     send_sems, piece_sems, pair_sems, local_sems, in_sems, delta_sems,
     mate_sems, part_sems, group_sems, out_sems, sum_sems,
@@ -324,27 +327,24 @@
         rows = everything[pl.ds(4 * i, 4)].reshape(BLOCK, WIDTH)
         proj = jnp.dot(rows, wide[...], preferred_element_type=jnp.float32)
         queries = [turn(proj[:, h * 128 : h * 128 + 128], cosine[at, :], sine[at, :]).astype(jnp.bfloat16) for h in range(2)]
-        query_ref[at, :128] = queries[0]
-        query_ref[at, 128:] = queries[1]
+        query_ref[i] = jnp.concatenate(queries, axis=0)
         key_ref[at, :] = turn(proj[:, 256:384], cosine[at, :], sine[at, :]).astype(jnp.bfloat16)
         value_ref[at, :] = proj[:, 384:].astype(jnp.bfloat16)
-        values_t[i] = proj[:, 384:].T.astype(jnp.bfloat16)
-        start_row, _ = start_of(starts, i)
-        query_row = lax.broadcasted_iota(jnp.int32, (1, BLOCK), 1) + i * BLOCK
-        blocks = range(max(0, i - 2), i + 1)
+        keys_t[:, at] = key_ref[at, :].astype(jnp.float32).T.astype(jnp.bfloat16)
+        values_t[:, at] = proj[:, 384:].T.astype(jnp.bfloat16)
+        start_row = jnp.concatenate([start_of(starts, i)] * 2, axis=1)
+        query_row = lax.broadcasted_iota(jnp.int32, (1, 2 * BLOCK), 1) % BLOCK + i * BLOCK
+        first = max(0, i - 2) * BLOCK
+        keys_at = slice(first, i * BLOCK + BLOCK)
+        soft, e = scored(key_ref[keys_at, :], query_ref[i], first, start_row, query_row)
+        p = e * (1.0 / jnp.sum(e, axis=0, keepdims=True))
+        kept = slice(KEPT[i], KEPT[i + 1])
+        probs[kept, :] = p
+        slopes[kept, :] = p * ((1.0 - soft * soft) * query_scale)
+        acc = jnp.dot(values_t[:, keys_at], p.astype(jnp.bfloat16), preferred_element_type=jnp.float32)
         for h in range(2):
-            sums = jnp.zeros((1, BLOCK), jnp.float32)
-            for n, j in enumerate(blocks):
-                _, e = scored(key_ref[j * BLOCK : j * BLOCK + BLOCK, :], queries[h], j * BLOCK, start_row, query_row)
-                scores[h, n] = e
-                sums = sums + jnp.sum(e, axis=0, keepdims=True)
-            inverse = 1.0 / sums
-            sums_ref[h : h + 1, at] = inverse
-            acc = jnp.zeros((128, BLOCK), jnp.float32)
-            for n, j in enumerate(blocks):
-                p = (scores[h, n] * inverse).astype(jnp.bfloat16)
-                acc = acc + jnp.dot(values_t[j], p, preferred_element_type=jnp.float32)
-            heads_ref[pl.ds(4 * i, 4), :, h * 128 : h * 128 + 128] = acc.T.reshape(4, ROWS, 128)
+            part = acc[:, h * BLOCK : h * BLOCK + BLOCK].T.reshape(4, ROWS, 128)
+            heads_ref[pl.ds(4 * i, 4), :, h * 128 : h * 128 + 128] = part
         if i == 0:
             load_part.wait()
             delta_total = own_part[...].astype(jnp.float32)
@@ -417,7 +417,10 @@
             own_grad[pl.ds(gg * 8, 16), pl.ds(lo, size)] = jnp.concatenate([first, second], axis=0).astype(jnp.bfloat16)
 
     def returning():
-        for _ in range(9):
+        for lo in range(0, WIDTH, 768):
+            weight_t[lo : lo + 768, :] = weight[:, lo : lo + 768].astype(jnp.float32).T.astype(jnp.bfloat16)
+            yield
+        for _ in range(3):
             yield
         for to in to_x:
             send(out_in.at[zh, x], out_in.at[zh, x], out_sems.at[x], to)
@@ -429,6 +432,35 @@
         send(out_in.at[zh], out_in.at[zh], out_sems.at[4], to_zh)
 
     spread(own_grad, full, send, piece_sems.at[1], pair_sems.at[1], local_sems.at[0], returning(), ready)
+
+    heads_t = heads_ref[...].reshape(16 * ROWS, 256).T.astype(jnp.bfloat16)
+    for lo in range(0, WIDTH, 768):
+        columns = full[:, :, lo : lo + 768].reshape(16 * ROWS, 768)
+        out_grad[:, lo : lo + 768] = jnp.dot(heads_t, columns, preferred_element_type=jnp.float32).astype(jnp.bfloat16)
+    store_out = pltpu.make_async_copy(out_grad, grad_out, local_sems.at[0])
+    store_out.start()
+    dkey[...] = jnp.zeros_like(dkey)
+    dvalue[...] = jnp.zeros_like(dvalue)
+    for i in range(STEPS):
+        at = slice(i * BLOCK, i * BLOCK + BLOCK)
+        keys_at = slice(max(0, i - 2) * BLOCK, i * BLOCK + BLOCK)
+        kept = slice(KEPT[i], KEPT[i + 1])
+        rows = full[pl.ds(4 * i, 4)].reshape(BLOCK, WIDTH)
+        grad_heads = jnp.dot(rows, weight_t[...], preferred_element_type=jnp.float32).astype(jnp.bfloat16)
+        grad = jnp.concatenate([grad_heads[:, :128], grad_heads[:, 128:]], axis=0)
+        p = probs[kept, :]
+        dp = lax.dot_general(value_ref[keys_at, :], grad, (((1,), (1,)), ((), ())), preferred_element_type=jnp.float32)
+        dvalue[keys_at, :] += jnp.dot(p.astype(jnp.bfloat16), grad, preferred_element_type=jnp.float32)
+        ds = (slopes[kept, :] * (dp - jnp.sum(p * dp, axis=0, keepdims=True))).astype(jnp.bfloat16)
+        dkey[keys_at, :] += jnp.dot(ds, query_ref[i], preferred_element_type=jnp.float32)
+        acc = jnp.dot(keys_t[:, keys_at], ds, preferred_element_type=jnp.float32)
+        for h in range(2):
+            turned_back = turn(acc[:, h * BLOCK : h * BLOCK + BLOCK].T, cosine[at, :], -sine[at, :])
+            grad_proj[at, h * 128 : h * 128 + 128] = turned_back
+    grad_proj[:, 256:384] = turn(dkey[...], cosine[...], -sine[...])
+    grad_proj[:, 384:512] = dvalue[...]
+    grad_proj_t[...] = grad_proj[...].T.astype(jnp.bfloat16)
+
     send.arrived(out_in.at[1 - zh], out_sems.at[4], sib)
     for gg in range(0, 8, 2):
         first = unstacked(out_in[0, gg // 2].astype(jnp.float32))
@@ -439,6 +471,7 @@
         send.arrived(delta_sum.at[n, pl.ds(side * 16, 16), :], sum_sems.at[1 + side, n], sib)
     keep.wait()
     store.wait()
+    store_out.wait()
     send.finish()
 
 
@@ -452,17 +485,26 @@
         out_shape=(
             shape((ROWS, WIDTH), bf16),
             shape((16, ROWS, WIDTH), bf16),
-            shape((16, ROWS, WIDTH), bf16),
             shape((4, 32, WIDTH), bf16),
-            shape((1024, 256), bf16),
-            shape((1024, 128), bf16),
-            shape((1024, 128), bf16),
-            shape((8, 1024), f32),
-            shape((16, ROWS, 256), f32),
+            shape((512, 1024), bf16),
+            shape((256, WIDTH), bf16),
         ),
         in_specs=[vmem, vmem, vmem, hbm, hbm, vmem, vmem, hbm, vmem, vmem],
-        out_specs=(vmem, hbm, hbm, hbm, vmem, vmem, vmem, vmem, vmem),
+        out_specs=(vmem, hbm, hbm, vmem, hbm),
         scratch_shapes=[
+            pltpu.VMEM((STEPS, 2 * BLOCK, 128), bf16),
+            pltpu.VMEM((1024, 128), bf16),
+            pltpu.VMEM((1024, 128), bf16),
+            pltpu.VMEM((16, ROWS, 256), f32),
+            pltpu.VMEM((16, ROWS, WIDTH), bf16),
+            pltpu.VMEM((KEPT[-1], 2 * BLOCK), f32),
+            pltpu.VMEM((KEPT[-1], 2 * BLOCK), f32),
+            pltpu.VMEM((128, 1024), bf16),
+            pltpu.VMEM((1024, 128), f32),
+            pltpu.VMEM((1024, 128), f32),
+            pltpu.VMEM((1024, 512), f32),
+            pltpu.VMEM((256, WIDTH), bf16),
+            pltpu.VMEM((WIDTH, 256), bf16),
             pltpu.VMEM((16, ROWS, WIDTH), bf16),
             pltpu.VMEM((ROWS, WIDTH), bf16),
             pltpu.VMEM((ROWS, WIDTH), bf16),
@@ -475,8 +517,7 @@
             pltpu.VMEM((32, WIDTH), bf16),
             pltpu.VMEM((32, WIDTH), bf16),
             pltpu.VMEM((8, 128), jnp.int32),
-            pltpu.VMEM((2, 3, BLOCK, BLOCK), f32),
-            pltpu.VMEM((STEPS, 128, BLOCK), bf16),
+            pltpu.VMEM((128, 1024), bf16),
             pltpu.VMEM((256, WIDTH), bf16),
             pltpu.VMEM((2, 8, 16, HALF), bf16),
             pltpu.VMEM((8, 16, HALF), bf16),
@@ -509,160 +550,76 @@
 CHUNKS = WIDTH // CHUNK
 
 
-def backward_kernel(
-    grads_hbm, x_hbm, weight, heads, query_ref, key_ref, value_ref, inverse_ref, cosine, sine, doc_ids,
-    delta, momentum, fragment, output, qkv_out, out_out, new_momentum, new_fragment, new_output, grads, x, slope, dprob, dkey, dvalue, keys_t, grad_proj, turned, heads_t, mixed, starts, sems,
+def finish_kernel(
+    x_hbm, turned, delta, momentum, fragment, output, grad_out, qkv_out, new_momentum, new_fragment, new_output, out_out,
+    x, mixed, sems,
 ):
     i = pl.program_id(0)
 
-    def load(n, which):
+    def load(n):
         rows = pl.ds(n * BLOCK, BLOCK)
-        src, dst = ((grads_hbm, grads), (x_hbm, x))[which]
-        return pltpu.make_async_copy(src.at[rows, :], dst.at[rows, :], sems.at[which, n])
+        return pltpu.make_async_copy(x_hbm.at[rows, :], x.at[rows, :], sems.at[n])
 
     @pl.when(i == 0)
     def _():
-        for which in range(2):
-            for n in range(STEPS):
-                load(n, which).start()
-        document_starts(doc_ids, starts)
-        dkey[...] = jnp.zeros_like(dkey)
-        dvalue[...] = jnp.zeros_like(dvalue)
-
-    head = [slice(h * 128, h * 128 + 128) for h in range(2)]
-
-    @pl.when(i < STEPS)
+        for n in range(STEPS):
+            load(n).start()
+
+    mean_delta = delta[...].astype(jnp.float32) / 8.0
+    moment = 0.9 * momentum[...] + mean_delta
+    new_momentum[...] = moment
+    new_fragment[...] = fragment[...] - 0.7 * (mean_delta + 0.9 * moment)
+    new_output[...] = output[...]
+    out_out[...] = grad_out[...]
+
+    @pl.when(i == 0)
     def _():
-        load(i, 0).wait()
-        own = pl.ds(pl.multiple_of(i * BLOCK, BLOCK), BLOCK)
-        grad_heads = lax.dot_general(
-            grads[own, :], weight[...], (((1,), (1,)), ((), ())), preferred_element_type=jnp.float32
-        ).astype(jnp.bfloat16)
-        keys_t[i] = key_ref[own, :].astype(jnp.float32).T.astype(jnp.bfloat16)
-        start_row, first = start_of(starts, i)
-        query_row = lax.broadcasted_iota(jnp.int32, (1, BLOCK), 1) + i * BLOCK
-        queries = [query_ref[own, head[h]] for h in range(2)]
-        grad = [grad_heads[:, head[h]] for h in range(2)]
-
-        def score(j, sums):
-            out = []
-            at = pl.ds(pl.multiple_of(j * BLOCK, BLOCK), BLOCK)
-            for h in range(2):
-                soft, e = scored(key_ref[at, :], queries[h], j * BLOCK, start_row, query_row)
-                p = e * inverse_ref[h : h + 1, :]
-                dp = lax.dot_general(
-                    value_ref[at, :], grad[h], (((1,), (1,)), ((), ())), preferred_element_type=jnp.float32
-                )
-                dvalue[at, :] += jnp.dot(p.astype(jnp.bfloat16), grad[h], preferred_element_type=jnp.float32)
-                out.append(sums[h] + jnp.sum(p * dp, axis=0, keepdims=True))
-                slope[h, j] = p * ((1.0 - soft * soft) * query_scale)
-                dprob[h, j] = dp
-            return tuple(out)
-
-        zero = jnp.zeros((1, BLOCK), jnp.float32)
-        sums = lax.fori_loop(first, i + 1, score, (zero, zero))
-
-        def mix(j, accs):
-            out = []
-            at = pl.ds(pl.multiple_of(j * BLOCK, BLOCK), BLOCK)
-            for h in range(2):
-                ds = (slope[h, j] * (dprob[h, j] - sums[h])).astype(jnp.bfloat16)
-                dkey[at, :] += jnp.dot(ds, queries[h], preferred_element_type=jnp.float32)
-                out.append(accs[h] + jnp.dot(keys_t[j], ds, preferred_element_type=jnp.float32))
-            return tuple(out)
-
-        zero = jnp.zeros((128, BLOCK), jnp.float32)
-        accs = lax.fori_loop(first, i + 1, mix, (zero, zero))
-        for h in range(2):
-            grad_proj[own, head[h]] = turn(accs[h].T, cosine[own, :], -sine[own, :])
-
-    @pl.when(i == STEPS)
-    def _():
-        grad_proj[:, 256:384] = turn(dkey[...], cosine[...], -sine[...])
-        grad_proj[:, 384:512] = dvalue[...]
-        turned[...] = grad_proj[...].T.astype(jnp.bfloat16)
-        heads_t[...] = heads[...].T.astype(jnp.bfloat16)
         for n in range(STEPS):
-            load(n, 1).wait()
-
-    @pl.when(i >= STEPS)
-    def _():
-        at = pl.ds(pl.multiple_of((i - STEPS) * CHUNK, CHUNK), CHUNK)
-        for j in range(4):
-            part = jnp.dot(turned[j * 128 : j * 128 + 128, :], x[:, at], preferred_element_type=jnp.float32)
-            mixed[pl.ds(j, CHUNK, stride=4), :] = part.T
-        out_out[...] = jnp.dot(heads_t[...], grads[:, at], preferred_element_type=jnp.float32).astype(jnp.bfloat16)
-        qkv_out[...] = mixed[...].astype(jnp.bfloat16)
-
-    @pl.when((i >= 1) & (i <= CHUNKS))
-    def _():
-        mean_delta = delta[...].astype(jnp.float32) / 8.0
-        moment = 0.9 * momentum[...] + mean_delta
-        new_momentum[...] = moment
-        new_fragment[...] = fragment[...] - 0.7 * (mean_delta + 0.9 * moment)
-        new_output[...] = output[...]
-
-
-def backward(grads, gathered, weight, heads, query, key, value, inverse, cosine, sine, doc_ids, delta, momentum, fragment, output):
-    whole = lambda *shape: pl.BlockSpec(shape, lambda i: (0, 0), pipeline_mode=pl.Buffered(1))
-    chunk_of = lambda i: jnp.maximum(i - STEPS, 0)
-    columns = lambda n: pl.BlockSpec((n, CHUNK), lambda i: (0, chunk_of(i)))
-    early = lambda n: pl.BlockSpec((n, CHUNK), lambda i: (0, jnp.clip(i - 1, 0, CHUNKS - 1)))
-    hbm = pl.BlockSpec(memory_space=pl.ANY)
+            load(n).wait()
+
+    at = pl.ds(pl.multiple_of(i * CHUNK, CHUNK), CHUNK)
+    part = jnp.dot(turned[...], x[:, at], preferred_element_type=jnp.float32)
+    for j in range(4):
+        mixed[pl.ds(j, CHUNK, stride=4), :] = part[j * 128 : j * 128 + 128].T
+    qkv_out[...] = mixed[...].astype(jnp.bfloat16)
+
+
+def finish(gathered, turned, delta, momentum, fragment, output, grad_out):
+    columns = lambda n: pl.BlockSpec((n, CHUNK), lambda i: (0, i))
     return pl.pallas_call(
-        backward_kernel,
-        grid=(STEPS + CHUNKS,),
+        finish_kernel,
+        grid=(CHUNKS,),
         in_specs=[
-            hbm,
-            hbm,
-            whole(256, WIDTH),
-            whole(1024, 256),
-            whole(1024, 256),
-            whole(1024, 128),
-            whole(1024, 128),
-            pl.BlockSpec((8, BLOCK), lambda i: (0, jnp.minimum(i, STEPS - 1))),
-            whole(1024, 128),
-            whole(1024, 128),
-            whole(8, 128),
-            early(128),
-            early(128),
-            early(128),
-            early(ROWS),
+            pl.BlockSpec(memory_space=pl.ANY),
+            pl.BlockSpec((512, 1024), lambda i: (0, 0)),
+            columns(128),
+            columns(128),
+            columns(128),
+            columns(ROWS),
+            columns(256),
         ],
         out_specs=[
-            pl.BlockSpec((4 * CHUNK, 128), lambda i: (chunk_of(i), 0)),
+            pl.BlockSpec((4 * CHUNK, 128), lambda i: (i, 0)),
+            columns(128),
+            columns(128),
+            columns(ROWS),
             columns(256),
-            early(128),
-            early(128),
-            early(ROWS),
         ],
         scratch_shapes=[
             pltpu.VMEM((1024, WIDTH), jnp.bfloat16),
-            pltpu.VMEM((1024, WIDTH), jnp.bfloat16),
-            pltpu.VMEM((2, STEPS, BLOCK, BLOCK), jnp.float32),
-            pltpu.VMEM((2, STEPS, BLOCK, BLOCK), jnp.float32),
-            pltpu.VMEM((1024, 128), jnp.float32),
-            pltpu.VMEM((1024, 128), jnp.float32),
-            pltpu.VMEM((STEPS, 128, BLOCK), jnp.bfloat16),
-            pltpu.VMEM((1024, 512), jnp.float32),
-            pltpu.VMEM((512, 1024), jnp.bfloat16),
-            pltpu.VMEM((256, 1024), jnp.bfloat16),
             pltpu.VMEM((4 * CHUNK, 128), jnp.float32),
-            pltpu.VMEM((8, 128), jnp.int32),
-            pltpu.SemaphoreType.DMA((2, STEPS)),
+            pltpu.SemaphoreType.DMA((STEPS,)),
         ],
         out_shape=[
             jax.ShapeDtypeStruct((4 * WIDTH, 128), jnp.bfloat16),
-            jax.ShapeDtypeStruct((256, WIDTH), jnp.bfloat16),
             jax.ShapeDtypeStruct((128, WIDTH), jnp.float32),
             jax.ShapeDtypeStruct((128, WIDTH), jnp.float32),
             jax.ShapeDtypeStruct((ROWS, WIDTH), jnp.bfloat16),
+            jax.ShapeDtypeStruct((256, WIDTH), jnp.bfloat16),
         ],
         compiler_params=pltpu.CompilerParams(vmem_limit_bytes=60 * 2**20),
-        name="backward",
-    )(
-        grads, gathered, weight, heads, query, key, value, inverse, cosine, sine, doc_ids, delta, momentum, fragment, output
-    )
+        name="finish",
+    )(gathered, turned, delta, momentum, fragment, output, grad_out)
 
 
 def local(
@@ -680,14 +637,12 @@
     cosine, sine = tables(16 * ROWS, 128)
     doc_ids = doc_ids.reshape(8, 128)
     out_flat = out_weight.reshape(256, WIDTH)
-    output, gathered, grad_rows, delta, query, key, value, inverse, heads = front(
+    output, gathered, delta, turned, grad_out = front(
         tokens, pre_gain.reshape(36, 128), post_gain.reshape(36, 128), qkv_weight.reshape(4 * WIDTH, 128), out_flat,
         doc_ids, cotangent, outer_delta[0], cosine, sine,
     )
-    gathered, heads = gathered.reshape(16 * ROWS, WIDTH), heads.reshape(16 * ROWS, 256)
-    grad_qkv, grad_out, new_momentum, new_fragment, output = backward(
-        grad_rows.reshape(16 * ROWS, WIDTH), gathered, out_flat, heads, query, key, value, inverse, cosine, sine,
-        doc_ids, delta.reshape(128, WIDTH), momentum, fragment, output,
+    grad_qkv, new_momentum, new_fragment, output, grad_out = finish(
+        gathered.reshape(16 * ROWS, WIDTH), turned, delta.reshape(128, WIDTH), momentum, fragment, output, grad_out
     )
     return (output, grad_qkv.reshape(qkv_weight.shape), grad_out.reshape(out_weight.shape), new_momentum, new_fragment)
 

time: 133 us -> 135 us (1.015)
  Pallas kernels: 132 us -> 134 us
    pallas_call x1, Pallas kernels: 105 us -> 117 us  [front(): pl.pallas_call(front_kernel, out_shape=(shape((ROWS, WIDTH), bf16), shape...]
    pallas_call x1, Pallas kernels: 27.2 us -> 16.4 us  [finish(): pl.pallas_call(finish_kernel, grid=(CHUNKS,), in_specs=[pl.BlockSpec(memo...]
where the time goes in v8:
time: 135 us
  Pallas kernels  134 us (99%)
    pallas_call x1, Pallas kernels, front(): pl.pallas_call(front_kernel, out_shape=(shape((ROWS, WIDTH), bf16), shape...  117 us
    pallas_call x1, Pallas kernels, finish(): pl.pallas_call(finish_kernel, grid=(CHUNKS,), in_specs=[pl.BlockSpec(memo...  16.4 us

profile of v8, /device:TPU:1, one launch (start us, length us, event | category | flops | bytes accessed | tf_op | source)
XLA Modules:
  0.0 134.7 jit_solution(10738563697818972050)
XLA Ops:
  0.6 117.5 %front.1 = (bf16[64,4608]{1,0:T(8,128)(2,1)}, bf16[16,64,4608]{2,1,0:T(8,128)(2,1)}, bf16[4,32,4608]{2,1,0:T(8,128)(2,1)}, bf16[512,1024]{1,0:T(8,128)(2,1)}, bf16[256,4608]{1,0:T(8,128)(2,1)}) custom-call(bf16[64,4608]{1,0:T(8,128)(2,1)} %tokens.1, f32[36,128]{1,0:T(8,128)} %bitcast.17, f32[36,128]{1,0:T(8,128)} %bitcast.18, bf16[18432,128]{1,0:T(8,128)(2,1)} %bitcast.13, ...), custom_call_target="tpu_custom_call" | custom-call | tf_op jit(solution)/shard_map/front/pallas_call | solution.py:483
  118.1 16.4 %finish.1 = (bf16[18432,128]{1,0:T(8,128)(2,1)}, f32[128,4608]{1,0:T(8,128)}, f32[128,4608]{1,0:T(8,128)}, bf16[64,4608]{1,0:T(8,128)(2,1)}, bf16[256,4608]{1,0:T(8,128)(2,1)}) custom-call(bf16[1024,4608]{1,0:T(8,128)(2,1)} %bitcast.12, bf16[512,1024]{1,0:T(8,128)(2,1)} %get-tuple-element.16.turned, bf16[128,4608]{1,0:T(8,128)(2,1)} %bitcast.15, ...), custom_call_target="tpu_custom_call" | custom-call | tf_op jit(solution)/shard_map/finish/pallas_call | solution.py:589

commit v9 on v8

--- a/solution.py
+++ b/solution.py
@@ -546,24 +546,15 @@
     )(tokens, pre_gain, post_gain, qkv_weight, weight, doc_ids, cotangent, delta, cosine, sine)
 
 
-CHUNK = 768
+CHUNK = 1152
 CHUNKS = WIDTH // CHUNK
 
 
 def finish_kernel(
-    x_hbm, turned, delta, momentum, fragment, output, grad_out, qkv_out, new_momentum, new_fragment, new_output, out_out,
-    x, mixed, sems,
+    x, turned, delta, momentum, fragment, output, grad_out, qkv_out, new_momentum, new_fragment, new_output, out_out,
+    mixed,
 ):
     i = pl.program_id(0)
-
-    def load(n):
-        rows = pl.ds(n * BLOCK, BLOCK)
-        return pltpu.make_async_copy(x_hbm.at[rows, :], x.at[rows, :], sems.at[n])
-
-    @pl.when(i == 0)
-    def _():
-        for n in range(STEPS):
-            load(n).start()
 
     mean_delta = delta[...].astype(jnp.float32) / 8.0
     moment = 0.9 * momentum[...] + mean_delta
@@ -572,13 +563,8 @@
     new_output[...] = output[...]
     out_out[...] = grad_out[...]
 
-    @pl.when(i == 0)
-    def _():
-        for n in range(STEPS):
-            load(n).wait()
-
     at = pl.ds(pl.multiple_of(i * CHUNK, CHUNK), CHUNK)
-    part = jnp.dot(turned[...], x[:, at], preferred_element_type=jnp.float32)
+    part = jnp.dot(turned[...], x[...], preferred_element_type=jnp.float32)
     for j in range(4):
         mixed[pl.ds(j, CHUNK, stride=4), :] = part[j * 128 : j * 128 + 128].T
     qkv_out[...] = mixed[...].astype(jnp.bfloat16)
@@ -590,7 +576,7 @@
         finish_kernel,
         grid=(CHUNKS,),
         in_specs=[
-            pl.BlockSpec(memory_space=pl.ANY),
+            columns(1024),
             pl.BlockSpec((512, 1024), lambda i: (0, 0)),
             columns(128),
             columns(128),
@@ -606,9 +592,7 @@
             columns(256),
         ],
         scratch_shapes=[
-            pltpu.VMEM((1024, WIDTH), jnp.bfloat16),
             pltpu.VMEM((4 * CHUNK, 128), jnp.float32),
-            pltpu.SemaphoreType.DMA((STEPS,)),
         ],
         out_shape=[
             jax.ShapeDtypeStruct((4 * WIDTH, 128), jnp.bfloat16),

time: 135 us -> 133 us (0.985)
  Pallas kernels: 134 us -> 132 us
    pallas_call x1, Pallas kernels: 16.4 us -> 14.8 us  [finish(): pl.pallas_call(finish_kernel, grid=(CHUNKS,), in_specs=[columns(1024), pl...]
where the time goes in v9:
time: 133 us
  Pallas kernels  132 us (99%)
    pallas_call x1, Pallas kernels, front(): pl.pallas_call(front_kernel, out_shape=(shape((ROWS, WIDTH), bf16), shape...  117 us
    pallas_call x1, Pallas kernels, finish(): pl.pallas_call(finish_kernel, grid=(CHUNKS,), in_specs=[columns(1024), pl...  14.8 us

profile of v9, /device:TPU:1, one launch (start us, length us, event | category | flops | bytes accessed | tf_op | source)
XLA Modules:
  0.0 132.9 jit_solution(14959229956596921321)
XLA Ops:
  0.6 117.5 %front.1 = (bf16[64,4608]{1,0:T(8,128)(2,1)}, bf16[16,64,4608]{2,1,0:T(8,128)(2,1)}, bf16[4,32,4608]{2,1,0:T(8,128)(2,1)}, bf16[512,1024]{1,0:T(8,128)(2,1)}, bf16[256,4608]{1,0:T(8,128)(2,1)}) custom-call(bf16[64,4608]{1,0:T(8,128)(2,1)} %tokens.1, f32[36,128]{1,0:T(8,128)} %bitcast.17, f32[36,128]{1,0:T(8,128)} %bitcast.18, bf16[18432,128]{1,0:T(8,128)(2,1)} %bitcast.13, ...), custom_call_target="tpu_custom_call" | custom-call | tf_op jit(solution)/shard_map/front/pallas_call | solution.py:483
  118.1 14.8 %finish.1 = (bf16[18432,128]{1,0:T(8,128)(2,1)}, f32[128,4608]{1,0:T(8,128)}, f32[128,4608]{1,0:T(8,128)}, bf16[64,4608]{1,0:T(8,128)(2,1)}, bf16[256,4608]{1,0:T(8,128)(2,1)}) custom-call(bf16[1024,4608]{1,0:T(8,128)(2,1)} %bitcast.12, bf16[512,1024]{1,0:T(8,128)(2,1)} %get-tuple-element.16.turned, bf16[128,4608]{1,0:T(8,128)(2,1)} %bitcast.15, ...), custom_call_target="tpu_custom_call" | custom-call | tf_op jit(solution)/shard_map/finish/pallas_call | solution.py:575
